TPU v7x, 32 devices: a whole 2x2x4 slice. The times are simulated.
32 devices in a mesh: clips: 8 (over y, x, core), slab: 4 (over z).
Axes of the slice: x: 2, y: 2, z: 4, core: 2. Of those that a mesh axis runs over, the one named last changes fastest.
Arguments:
- video: bfloat16 [16, 6, 4, 16, 256], P('clips', None, 'slab'), may hold values from -6 to 6
- clip_blocks: int32 [16], replicated, may hold values from 1 to 3, 32 in all
- deal_order: int32 [8], replicated, may hold values from 0 to 7, each once
- kernel: bfloat16 [256, 3456], P('clips', 'slab'), may hold values from -0.078125 to 0.078125
- gain: float32 [128], replicated, may hold values from 0.25 to 1.75
- bias: float32 [128], replicated, may hold values from -3 to 3
- cotangent: bfloat16 [32, 2, 4, 16, 128], P('clips', None, 'slab'), may hold values from -6 to 6
Outputs:
- activations: bfloat16 [32, 2, 4, 16, 128], P('clips', None, 'slab')
- video_grad: bfloat16 [16, 6, 4, 16, 256], P('clips', None, 'slab')
- kernel_grad: float32 [256, 3456], P('clips', 'slab')
- gain_grad: float32 [128], replicated
- bias_grad: float32 [128], replicated
Inputs may be any that keep to these rules, and one draw needn't show every extreme that they name: `clip_blocks`: the blocks of all clips add up to 4 times the number of devices along clips, so every device receives exactly 4 blocks; some clip has 3 blocks. `deal_order`: a permutation of the devices along clips.
All inputs are finite; a program needn't handle non-finite values.
Results may differ from a plain program's by a relative error of at most 0.0049.
Values may be sent and summed in bfloat16 or wider, within the bound.
No kernel may reach another device: no remote copies, remote signals or barrier semaphores. Data moves between devices by JAX's collectives and lax.ppermute only.
A program may use at most 64 MiB of HBM per device.

v0:
```python
import jax
import jax.numpy as jnp
from jax import lax
from jax.sharding import PartitionSpec as P

GROUPS = 16
TAPS = 27
FB = 2
BMAX = 3


def extended(array, sides, width):
    for axis, dim in sides:
        size, length = (lax.axis_size(axis), array.shape[dim])
        up = [(i, (i + 1) % size) for i in range(size - 1)]
        down = [(j, i) for i, j in up]
        last = lax.slice_in_dim(array, length - width, length, axis=dim)
        initial = lax.slice_in_dim(array, 0, width, axis=dim)
        before = lax.ppermute(last, axis, up)
        after = lax.ppermute(initial, axis, down)
        array = jnp.concatenate([before, array, after], axis=dim)
    return array


def body(video, clip_blocks, deal_order, kernel, gain, bias, cotangent):
    clip_devs = lax.axis_size("clips")
    slab_devs = lax.axis_size("slab")
    own_index = lax.axis_index("clips")
    held_clips, frame_count, row_count, column_count, in_channels = video.shape
    slot_count = cotangent.shape[0]
    out_channels = gain.shape[0]
    all_clips = clip_blocks.shape[0]
    per_group = out_channels // GROUPS
    capacity = -(-(held_clips * BMAX) // clip_devs)
    block_ends = jnp.cumsum(clip_blocks)
    block_starts = block_ends - clip_blocks
    device_ids = jnp.arange(clip_devs, dtype=jnp.int32)
    deal_slot = jnp.sum(
        jnp.where(deal_order[:, None] == device_ids[None, :], device_ids[:, None], 0), axis=0
    )
    first_clip = own_index * held_clips
    own_start = block_starts[first_clip]
    own_end = block_ends[first_clip + held_clips - 1]
    dest_rank = jnp.repeat(device_ids, capacity)
    turn_index = jnp.tile(jnp.arange(capacity, dtype=jnp.int32), clip_devs)
    slot_blocks = jnp.arange(slot_count, dtype=jnp.int32) * clip_devs + deal_slot[own_index]

    def clip_index(block_id):
        return jnp.sum((block_ends <= block_id[..., None]).astype(jnp.int32), axis=-1)

    full_kernel = lax.all_gather(kernel, "slab", axis=1, tiled=True)
    full_kernel = lax.all_gather(full_kernel, "clips", axis=0, tiled=True)
    kernel_taps = full_kernel.reshape(in_channels, out_channels, TAPS).transpose(2, 0, 1)

    def group_sums(values):
        return jnp.sum(values.reshape(values.shape[:4] + (GROUPS, per_group)), axis=(1, 2, 3, 5))

    def spread(stat):
        return stat[:, None, None, None, :, None]

    cells_clip = FB * row_count * slab_devs * column_count * per_group
    context_video = jnp.pad(video, ((0, 0), (2, 0), (0, 0), (0, 0), (0, 0)))
    highest = lax.Precision.HIGHEST
    first_block = own_start + jnp.mod(deal_slot[dest_rank] - own_start, clip_devs)
    block_id = first_block + turn_index * clip_devs
    is_live = block_id < own_end
    clip_global = jnp.minimum(clip_index(block_id), all_clips - 1)
    clip_local = jnp.clip(clip_global - first_clip, 0, held_clips - 1)
    block_local = jnp.clip(block_id - block_starts[clip_global], 0, BMAX - 1)
    window = FB + 2

    def window_of(clip_pick, block_pick):
        begin = (clip_pick, block_pick * FB, 0, 0, 0)
        sizes = (1, window, row_count, column_count, context_video.shape[-1])
        return lax.dynamic_slice(context_video, begin, sizes)[0]

    pieces = jax.vmap(window_of)(clip_local, block_local)
    pieces = jnp.where(
        is_live[:, None, None, None, None], pieces, jnp.zeros((), context_video.dtype)
    )
    sent = pieces.reshape((clip_devs, capacity) + pieces.shape[1:])
    received = lax.all_to_all(sent, "clips", split_axis=0, concat_axis=0, tiled=True)
    clip_global = clip_index(slot_blocks)
    source_rank = clip_global // held_clips
    turn_of = (slot_blocks - block_starts[source_rank * held_clips]) // clip_devs
    flat_rows = received.reshape((clip_devs * capacity,) + received.shape[2:])
    input_slots = flat_rows[source_rank * capacity + turn_of]
    rimmed = extended(input_slots, (("slab", 2),), 1)
    padded = jnp.pad(rimmed, ((0, 0), (0, 0), (0, 0), (1, 1), (0, 0)))
    forward_outputs = input_slots.shape[1] - 2
    totals = jnp.zeros(
        (input_slots.shape[0] * forward_outputs * row_count * column_count, out_channels),
        jnp.float32,
    )
    for forward_step_a in range(3):
        for forward_step_b in range(3):
            for forward_step_c in range(3):
                tap_rows = padded[
                    :,
                    forward_step_a : forward_step_a + forward_outputs,
                    forward_step_b : forward_step_b + row_count,
                    forward_step_c : forward_step_c + column_count,
                    :,
                ].reshape(-1, in_channels)
                totals = totals + jnp.dot(
                    tap_rows,
                    kernel_taps[(forward_step_a * 3 + forward_step_b) * 3 + forward_step_c],
                    preferred_element_type=jnp.float32,
                )
    conv_out = totals.reshape(
        input_slots.shape[0], forward_outputs, row_count, column_count, out_channels
    )
    slot_clip = clip_index(slot_blocks)
    chooser = (slot_clip[:, None] == jnp.arange(all_clips, dtype=jnp.int32)[None, :]).astype(
        jnp.float32
    )
    table_first = jnp.dot(chooser.T, group_sums(conv_out), precision=highest)
    table_second = jnp.dot(chooser.T, group_sums(conv_out * conv_out), precision=highest)
    table_first, table_second = lax.psum((table_first, table_second), ("clips", "slab"))
    counts = (clip_blocks * cells_clip).astype(jnp.float32)
    group_mean = table_first / counts[:, None]
    group_var = table_second / counts[:, None] - group_mean * group_mean
    clip_mean = group_mean
    clip_inv = lax.rsqrt(group_var + 1e-05)
    group_mean = jnp.dot(chooser, clip_mean, precision=highest)
    inv_std = jnp.dot(chooser, clip_inv, precision=highest)
    grouped = conv_out.reshape(conv_out.shape[:4] + (GROUPS, per_group))
    normed = ((grouped - spread(group_mean)) * spread(inv_std)).reshape(conv_out.shape)
    affine = normed * gain + bias
    activations = jax.nn.silu(affine).astype(jnp.bfloat16)
    sigmoid = jax.nn.sigmoid(affine)
    grad_affine = cotangent.astype(jnp.float32) * sigmoid * (1.0 + affine * (1.0 - sigmoid))
    gain_part = jnp.sum(grad_affine * normed, axis=(0, 1, 2, 3))
    bias_part = jnp.sum(grad_affine, axis=(0, 1, 2, 3))
    grad_normed, gain_part, bias_part = (grad_affine * gain, gain_part, bias_part)
    sum_grad = jnp.dot(chooser.T, group_sums(grad_normed), precision=highest)
    sum_cross = jnp.dot(chooser.T, group_sums(grad_normed * normed), precision=highest)
    sum_grad, sum_cross, gain_grad, bias_grad = lax.psum(
        (sum_grad, sum_cross, gain_part, bias_part), ("clips", "slab")
    )
    mean_grad = jnp.dot(chooser, sum_grad / counts[:, None], precision=highest)
    mean_cross = jnp.dot(chooser, sum_cross / counts[:, None], precision=highest)
    grouped = grad_normed.reshape(grad_normed.shape[:4] + (GROUPS, per_group))
    normed_groups = normed.reshape(grouped.shape)
    result = spread(inv_std) * (grouped - spread(mean_grad) - normed_groups * spread(mean_cross))
    grad_conv = result.reshape(grad_normed.shape).astype(jnp.bfloat16)
    range_start = block_starts[dest_rank * held_clips]
    range_end = block_ends[dest_rank * held_clips + held_clips - 1]
    first_block = range_start + jnp.mod(deal_slot[own_index] - range_start, clip_devs)
    block_id = first_block + turn_index * clip_devs
    is_live = block_id < range_end
    slot_index = jnp.clip(block_id // clip_devs, 0, slot_count - 1)
    pieces = jnp.where(
        is_live[:, None, None, None, None], grad_conv[slot_index], jnp.zeros((), grad_conv.dtype)
    )
    returned = lax.all_to_all(
        pieces.reshape((clip_devs, capacity) + pieces.shape[1:]),
        "clips",
        split_axis=0,
        concat_axis=0,
        tiled=True,
    )
    clip_global = first_clip + jnp.arange(held_clips, dtype=jnp.int32)[:, None]
    block_range = jnp.arange(BMAX, dtype=jnp.int32)[None, :]
    block_id = block_starts[clip_global] + block_range
    is_live = block_range < clip_blocks[clip_global]
    source_rank = deal_order[jnp.mod(block_id, clip_devs)]
    turn_of = (block_id - own_start) // clip_devs
    row_index = jnp.where(is_live, source_rank * capacity + turn_of, 0)
    flat_rows = returned.reshape((clip_devs * capacity,) + returned.shape[2:])
    pieces = jnp.where(
        is_live[:, :, None, None, None, None], flat_rows[row_index], jnp.zeros((), returned.dtype)
    )
    grad_clip = pieces.reshape((held_clips, frame_count) + pieces.shape[3:])
    rimmed_grad = extended(grad_clip, (("slab", 2),), 1)
    grad_padded = jnp.pad(rimmed_grad, ((0, 0), (0, 2), (0, 0), (1, 1), (0, 0)))
    totals = jnp.zeros(
        (held_clips * frame_count * row_count * column_count, in_channels), jnp.float32
    )
    for step_a in range(3):
        for step_b in range(3):
            for step_c in range(3):
                moved = grad_padded[
                    :,
                    2 - step_a : 2 - step_a + frame_count,
                    2 - step_b : 2 - step_b + row_count,
                    2 - step_c : 2 - step_c + column_count,
                    :,
                ].reshape(-1, out_channels)
                totals = totals + lax.dot_general(
                    moved,
                    kernel_taps[(step_a * 3 + step_b) * 3 + step_c],
                    (((1,), (1,)), ((), ())),
                    preferred_element_type=jnp.float32,
                )
    video_grad = totals.reshape(video.shape).astype(jnp.bfloat16)
    outputs = grad_conv.shape[1]
    grad_flat = grad_conv.reshape(-1, out_channels)
    take_count = in_channels // clip_devs * lax.axis_size("clips")
    tap_parts = []
    for step_a in range(3):
        for step_b in range(3):
            for step_c in range(3):
                tap_rows = padded[
                    :,
                    step_a : step_a + outputs,
                    step_b : step_b + row_count,
                    step_c : step_c + column_count,
                    :,
                ].reshape(-1, take_count)
                tap_parts.append(
                    lax.dot_general(
                        tap_rows,
                        grad_flat,
                        (((0,), (0,)), ((), ())),
                        preferred_element_type=jnp.float32,
                    )
                )
    partial_grad = lax.psum_scatter(
        jnp.stack(tap_parts, axis=2).reshape(take_count, out_channels * TAPS),
        "clips",
        scatter_dimension=0,
        tiled=True,
    )
    kernel_grad = lax.psum_scatter(partial_grad, "slab", scatter_dimension=1, tiled=True)
    return (activations, video_grad, kernel_grad, gain_grad, bias_grad)


def solution(mesh):
    return jax.shard_map(
        body,
        mesh=mesh,
        in_specs=(
            P("clips", None, "slab", None, None),
            P(),
            P(),
            P("clips", "slab"),
            P(),
            P(),
            P("clips", None, "slab", None, None),
        ),
        out_specs=(
            P("clips", None, "slab", None, None),
            P("clips", None, "slab", None, None),
            P("clips", "slab"),
            P(),
            P(),
        ),
        check_vma=False,
    )
```

profile of v0, /device:TPU:0, one launch (start us, length us, event | category | flops | bytes accessed | tf_op | source)
XLA Modules:
  0.0 350.8 jit_solution(8996184733195385492)
XLA Ops:
  11.8 1.3 broadcast_compare_fusion
  16.9 5.2 %all-to-all-start = ((bf16[8,1,4,1,16,256]{5,4,2,3,1,0:T(8,128)(2,1)}), bf16[8,1,4,1,16,256]{5,4,2,3,1,0:T(8,128)(2,1)S(1)}, u32[]{:S(2)}, u32[]{:S(2)}) async-start(bf16[8,1,4,1,16,256]{5,4,2,3,1,0:T(8,128)(2,1)} %fusion.51), calls=%async_computation | async-start | bytes 524288 | tf_op jit(solution)/shard_map/all_to_all | solution.py:82
  22.1 14.2 %all-gather = bf16[4,864,32]{1,2,0:T(8,128)(2,1)S(1)} all-gather(bf16[1,864,32]{1,2,0:T(8,128)(2,1)} %bitcast.751), channel_id=1, replica_groups=mesh['clips'=8,'slab'=4] {'slab'}, dimensions={0}, use_global_device_ids=true | all-gather | bytes 276480 | tf_op jit(solution)/shard_map/all_gather | solution.py:51
  47.2 1.3 collective-permute-start.1
  48.5 4.6 %collective-permute-start = (bf16[4,4,1,16,256]{4,3,1,0,2:T(8,128)(2,1)S(1)}, bf16[4,4,1,16,256]{4,3,1,0,2:T(8,128)(2,1)S(1)}, u32[]{:S(2)}, u32[]{:S(2)}) collective-permute-start(bf16[4,4,1,16,256]{4,3,1,0,2:T(8,128)(2,1)S(1)} %bitcast.686), channel_id=1, source_target_pairs={{0,1},{1,2},{2,3},{4,5},{5,6},{6,7},{8,9},{9,10},{10,11},{12,13},{... | collective-permute-start | bytes 393224 | tf_op jit(solution)/shard_map/ppermute | solution.py:19
  54.1 1.5 collective-permute-done
  58.3 7.7 %all-gather.3.cloned.1.call-done = bf16[256,3456]{1,0:T(8,128)(2,1)} async-done(((bf16[32,3456]{1,0:T(8,128)(2,1)}), bf16[256,3456]{1,0:T(8,128)(2,1)}) %all-gather.3.cloned.1.call-update) | async-done | bytes 1769488 | tf_op jit(solution)/shard_map/all_gather | solution.py:52
  66.0 3.9 %copy.95 = bf16[256,3456]{0,1:T(8,128)(2,1)} copy(bf16[256,3456]{1,0:T(8,128)(2,1)} %all-gather.3.cloned.1.call-done) | data formatting | bytes 3538944 | tf_op jit(solution)/shard_map/all_gather | solution.py:52
  69.9 2.6 reshape.1229
  72.4 1.7 fusion.228
  74.2 3.3 fusion.227
  127.4 39.5 %all-reduce.4 = (f32[16,16]{1,0:T(8,128)S(1)}, f32[16,16]{1,0:T(8,128)S(1)}) all-reduce(f32[16,16]{1,0:T(8,128)S(1)} %fusion.161, f32[16,16]{1,0:T(8,128)S(1)} %fusion.163), channel_id=1, replica_groups=mesh['clips'=8,'slab'=4] {'clips','slab'}, use_global_device_ids=true, to_apply=%region_7.8 | all-reduce | flops 512 | bytes 4096 | tf_op jit(solution)/shard_map/psum | solution.py:119
  169.2 41.6 %all-reduce.3 = (f32[16,16]{1,0:T(8,128)S(1)}, f32[16,16]{1,0:T(8,128)S(1)}, f32[128]{0:T(128)}, f32[128]{0:T(128)}) all-reduce(f32[16,16]{1,0:T(8,128)S(1)} %fusion.157, f32[16,16]{1,0:T(8,128)S(1)} %fusion.158, f32[128]{0:T(128)S(1)} %get-tuple-element.25, ...), channel_id=1, replica_groups=mesh['clips'=8,'slab'=4] {'clips','slab'}, use_global_device_ids=true, to_apply=%region_13.14 | all-reduce | flops 768 | bytes 6144 | tf_op jit(solution)/shard_map/psum | solution.py:138
  213.7 4.0 %all-to-all-start.1 = ((bf16[8,1,2,1,16,128]{5,4,2,3,1,0:T(8,128)(2,1)}), bf16[8,1,2,1,16,128]{5,4,2,3,1,0:T(8,128)(2,1)}, u32[]{:S(2)}, u32[]{:S(2)}) async-start(bf16[8,1,2,1,16,128]{5,4,2,3,1,0:T(8,128)(2,1)} %bitcast_select_fusion.1), calls=%async_computation.1 | async-start | bytes 131072 | tf_op jit(solution)/shard_map/all_to_all | solution.py:156
  240.3 6.0 %copy.126 = f32[256,128,27]{0,2,1:T(8,128)} copy(f32[256,128,27]{0,1,2:T(8,128)} %fusion.4) | data formatting | bytes 7077888 | tf_op jit(solution)/shard_map/stack | solution.py:220
  246.3 3.1 reshape.1311
  249.4 3.0 copy.156
  252.6 1.5 gather_fusion.11
  255.5 4.5 %collective-permute-start.2 = (bf16[2,6,1,16,128]{4,3,1,0,2:T(8,128)(2,1)S(1)}, bf16[2,6,1,16,128]{4,3,1,0,2:T(8,128)(2,1)S(1)}, u32[]{:S(2)}, u32[]{:S(2)}) collective-permute-start(bf16[2,6,1,16,128]{4,3,1,0,2:T(8,128)(2,1)S(1)} %broadcast_select_fusion.1), channel_id=1, source_target_pairs={{0,1},{1,2},{2,3},{4,5},{5,6},{6,7},{8,9},{9,10},{10,11},{12,13},{... | collective-permute-start | bytes 147464 | tf_op jit(solution)/shard_map/ppermute | solution.py:19
  260.2 1.6 collective-permute-done.2
  266.7 34.4 %reduce-scatter.7.cloned.1.call-done = f32[32,3456]{1,0:T(8,128)} async-done(((f32[256,3456]{1,0:T(8,128)}), f32[32,3456]{1,0:T(8,128)}) %reduce-scatter.7.cloned.1.call-update) | async-done | bytes 442384
  301.1 2.8 copy.157
  305.3 37.1 %reduce-scatter.5.cloned.1.call-done = f32[32,864]{0,1:T(8,128)} async-done(((f32[32,3456]{0,1:T(8,128)}), f32[32,864]{0,1:T(8,128)}) %reduce-scatter.5.cloned.1.call-update) | async-done | bytes 110608 | tf_op jit(solution)/shard_map/reduce_scatter | solution.py:225
  342.4 1.8 copy.128
  (349 shorter events, 107.0 us)
Async XLA Ops:
  7.2 32.3 %copy-start = (s32[8]{0:T(128)S(1)}, s32[8]{0:T(128)}, u32[]{:S(2)}) copy-start(s32[8]{0:T(128)} %param.9) | copy-start | bytes 100
  16.9 29.7 %all-to-all-start = ((bf16[8,1,4,1,16,256]{5,4,2,3,1,0:T(8,128)(2,1)}), bf16[8,1,4,1,16,256]{5,4,2,3,1,0:T(8,128)(2,1)S(1)}, u32[]{:S(2)}, u32[]{:S(2)}) async-start(bf16[8,1,4,1,16,256]{5,4,2,3,1,0:T(8,128)(2,1)} %fusion.51), calls=%async_computation | async-start | bytes 524288 | tf_op jit(solution)/shard_map/all_to_all | solution.py:82
  22.1 43.9 %all-gather.3.cloned.1.call-start = ((), (), s32[]{:S(2)}) async-start(), calls=%async_computation.4 | async-start | bytes 1990656 | tf_op jit(solution)/shard_map/all_gather | solution.py:52
  47.2 6.9 %collective-permute-start.1 = (bf16[4,4,1,16,256]{4,3,1,0,2:T(8,128)(2,1)S(1)}, bf16[4,4,1,16,256]{4,3,1,0,2:T(8,128)(2,1)S(1)}, u32[]{:S(2)}, u32[]{:S(2)}) collective-permute-start(bf16[4,4,1,16,256]{4,3,1,0,2:T(8,128)(2,1)S(1)} %bitcast.685), channel_id=1, source_target_pairs={{1,0},{2,1},{3,2},{5,4},{6,5},{7,6},{9,8},{10,9},{11,10},{13,12},{... | collective-permute-start | bytes 393224 | tf_op jit(solution)/shard_map/ppermute | solution.py:20
  48.5 7.1 %collective-permute-start = (bf16[4,4,1,16,256]{4,3,1,0,2:T(8,128)(2,1)S(1)}, bf16[4,4,1,16,256]{4,3,1,0,2:T(8,128)(2,1)S(1)}, u32[]{:S(2)}, u32[]{:S(2)}) collective-permute-start(bf16[4,4,1,16,256]{4,3,1,0,2:T(8,128)(2,1)S(1)} %bitcast.686), channel_id=1, source_target_pairs={{0,1},{1,2},{2,3},{4,5},{5,6},{6,7},{8,9},{9,10},{10,11},{12,13},{... | collective-permute-start | bytes 393224 | tf_op jit(solution)/shard_map/ppermute | solution.py:19
  78.6 32.5 %copy-start.14 = (bf16[1,256,128]{2,1,0:T(8,128)(2,1)}, bf16[1,256,128]{2,1,0:T(8,128)(2,1)S(1)}, u32[]{:S(2)}) copy-start(bf16[1,256,128]{2,1,0:T(8,128)(2,1)S(1)} %copy.103) | copy-start | bytes 196612
  79.6 30.4 %copy-start.34 = (bf16[1,256,128]{2,1,0:T(8,128)(2,1)}, bf16[1,256,128]{2,1,0:T(8,128)(2,1)S(1)}, u32[]{:S(2)}) copy-start(bf16[1,256,128]{2,1,0:T(8,128)(2,1)S(1)} %copy.102) | copy-start | bytes 196612
  87.1 37.3 %copy-start.8 = (bf16[1,256,128]{2,1,0:T(8,128)(2,1)}, bf16[1,256,128]{2,1,0:T(8,128)(2,1)S(1)}, u32[]{:S(2)}) copy-start(bf16[1,256,128]{2,1,0:T(8,128)(2,1)S(1)} %copy.121) | copy-start | bytes 196612
  89.2 35.0 %copy-start.24 = (bf16[1,256,128]{2,1,0:T(8,128)(2,1)}, bf16[1,256,128]{2,1,0:T(8,128)(2,1)S(1)}, u32[]{:S(2)}) copy-start(bf16[1,256,128]{2,1,0:T(8,128)(2,1)S(1)} %copy.120) | copy-start | bytes 196612
  90.3 32.9 %copy-start.26 = (bf16[1,256,128]{2,1,0:T(8,128)(2,1)}, bf16[1,256,128]{2,1,0:T(8,128)(2,1)S(1)}, u32[]{:S(2)}) copy-start(bf16[1,256,128]{2,1,0:T(8,128)(2,1)S(1)} %copy.119) | copy-start | bytes 196612
  91.3 30.8 %copy-start.28 = (bf16[1,256,128]{2,1,0:T(8,128)(2,1)}, bf16[1,256,128]{2,1,0:T(8,128)(2,1)S(1)}, u32[]{:S(2)}) copy-start(bf16[1,256,128]{2,1,0:T(8,128)(2,1)S(1)} %copy.118) | copy-start | bytes 196612
  111.0 55.8 %copy-start.66 = (f32[16]{0:T(128)S(1)}, f32[16]{0:T(128)}, u32[]{:S(2)}) copy-start(f32[16]{0:T(128)} %get-tuple-element.117) | copy-start | bytes 196
  112.1 55.5 %copy-start.62 = (bf16[4,2,1,16,128]{4,3,2,1,0:T(8,128)(2,1)S(1)}, bf16[4,2,1,16,128]{4,3,2,1,0:T(8,128)(2,1)}, u32[]{:S(2)}) copy-start(bf16[4,2,1,16,128]{4,3,2,1,0:T(8,128)(2,1)} %param.13) | copy-start | bytes 98308
  112.1 55.5 %copy-start.63 = (f32[128]{0:T(128)S(1)}, f32[128]{0:T(128)}, u32[]{:S(2)}) copy-start(f32[128]{0:T(128)} %param.11) | copy-start | bytes 1540
  112.1 55.5 %copy-start.64 = (f32[128]{0:T(128)S(1)}, f32[128]{0:T(128)}, u32[]{:S(2)}) copy-start(f32[128]{0:T(128)} %param.12) | copy-start | bytes 1540
  213.7 38.9 %all-to-all-start.1 = ((bf16[8,1,2,1,16,128]{5,4,2,3,1,0:T(8,128)(2,1)}), bf16[8,1,2,1,16,128]{5,4,2,3,1,0:T(8,128)(2,1)}, u32[]{:S(2)}, u32[]{:S(2)}) async-start(bf16[8,1,2,1,16,128]{5,4,2,3,1,0:T(8,128)(2,1)} %bitcast_select_fusion.1), calls=%async_computation.1 | async-start | bytes 131072 | tf_op jit(solution)/shard_map/all_to_all | solution.py:156
  217.7 83.4 %reduce-scatter.7.cloned.1.call-start = ((), (), s32[]{:S(2)}) async-start(), calls=%async_computation.6 | async-start | bytes 3981312
  252.5 89.9 %reduce-scatter.5.cloned.1.call-start = ((), (), s32[]{:S(2)}) async-start(), calls=%async_computation.5 | async-start | bytes 2211840 | tf_op jit(solution)/shard_map/reduce_scatter | solution.py:225
  254.2 6.0 %collective-permute-start.3 = (bf16[2,6,1,16,128]{4,3,1,0,2:T(8,128)(2,1)S(1)}, bf16[2,6,1,16,128]{4,3,1,0,2:T(8,128)(2,1)S(1)}, u32[]{:S(2)}, u32[]{:S(2)}) collective-permute-start(bf16[2,6,1,16,128]{4,3,1,0,2:T(8,128)(2,1)S(1)} %broadcast_select_fusion.1), channel_id=1, source_target_pairs={{1,0},{2,1},{3,2},{5,4},{6,5},{7,6},{9,8},{10,9},{11,10},{13,12},{... | collective-permute-start | bytes 147464 | tf_op jit(solution)/shard_map/ppermute | solution.py:20
  255.5 6.3 %collective-permute-start.2 = (bf16[2,6,1,16,128]{4,3,1,0,2:T(8,128)(2,1)S(1)}, bf16[2,6,1,16,128]{4,3,1,0,2:T(8,128)(2,1)S(1)}, u32[]{:S(2)}, u32[]{:S(2)}) collective-permute-start(bf16[2,6,1,16,128]{4,3,1,0,2:T(8,128)(2,1)S(1)} %broadcast_select_fusion.1), channel_id=1, source_target_pairs={{0,1},{1,2},{2,3},{4,5},{5,6},{6,7},{8,9},{9,10},{10,11},{12,13},{... | collective-permute-start | bytes 147464 | tf_op jit(solution)/shard_map/ppermute | solution.py:19
  265.5 38.4 %copy-start.3 = (bf16[1,256,128]{2,1,0:T(8,128)(2,1)S(1)}, bf16[1,256,128]{2,1,0:T(8,128)(2,1)}, u32[]{:S(2)}) copy-start(bf16[1,256,128]{2,1,0:T(8,128)(2,1)} %copy-done.2) | copy-start | bytes 196612
  265.7 38.4 %copy-start.27 = (bf16[1,256,128]{2,1,0:T(8,128)(2,1)S(1)}, bf16[1,256,128]{2,1,0:T(8,128)(2,1)}, u32[]{:S(2)}) copy-start(bf16[1,256,128]{2,1,0:T(8,128)(2,1)} %copy-done.26) | copy-start | bytes 196612
  265.9 38.4 %copy-start.25 = (bf16[1,256,128]{2,1,0:T(8,128)(2,1)S(1)}, bf16[1,256,128]{2,1,0:T(8,128)(2,1)}, u32[]{:S(2)}) copy-start(bf16[1,256,128]{2,1,0:T(8,128)(2,1)} %copy-done.24) | copy-start | bytes 196612
  266.1 38.4 %copy-start.9 = (bf16[1,256,128]{2,1,0:T(8,128)(2,1)S(1)}, bf16[1,256,128]{2,1,0:T(8,128)(2,1)}, u32[]{:S(2)}) copy-start(bf16[1,256,128]{2,1,0:T(8,128)(2,1)} %copy-done.8) | copy-start | bytes 196612
  (54 other events, 859.8 us)
Sparse Core Ops, SparseCore 0:
  37.5 28.4 all-gather.2
  252.6 48.3 reduce-scatter.6
  304.0 38.3 reduce-scatter.4
where the time goes:
time: 353 us; the launch traced here: 351 us
  blocking collectives  95.3 us (27%)
  waiting for transfers between devices  82.8 us (23%)
  local copies, waits for them, and re-layouts  69.8 us (20%)
  matrix products  54.7 us (15%)
  starting transfers between devices  21 us (6%)
  between operations  15.6 us (4%)
  other arithmetic  11.7 us (3%)
    psum x1, blocking collectives, body(): lax.psum((sum_grad, sum_cross, gain_part, bias_part), ('clips', 'slab'))  41.6 us
    psum x1, blocking collectives, body(): lax.psum((table_first, table_second), ('clips', 'slab'))  39.5 us
    reduce_scatter x1, waiting for transfers between devices, body(): lax.psum_scatter(partial_grad, 'slab', scatter_dimension=1, tiled=True)  37.1 us
    unnamed x4, waiting for transfers between devices  34.4 us
    slice x29, local copies, waits for them, and re-layouts, body(): kernel_taps[(forward_step_a * 3 + forward_step_b) * 3 + forward_step_c]  26.9 us
    dot_general x27, matrix products, body(): jnp.dot(tap_rows, kernel_taps[(forward_step_a * 3 + forward_step_b) * 3 +...  24.1 us
    dot_general x27, matrix products, body(): lax.dot_general(tap_rows, grad_flat, (((0,), (0,)), ((), ())), preferred_...  23.4 us
    all_gather x1, blocking collectives, body(): full_kernel = lax.all_gather(kernel, 'slab', axis=1, tiled=True)  14.2 us
  transfers between devices with their start and end apart: 9, of which 6 were waited for; matrix products, arithmetic and copies ran while one was open for 16% of the time, Pallas kernels for 0%

commit v1 on v0

v1 whole, which is shorter than its diff:
```python
import functools

import jax
import jax.numpy as jnp
import numpy as np
from jax import lax
from jax.experimental import pallas as pl
from jax.experimental.pallas import tpu as pltpu
from jax.sharding import PartitionSpec as P

GROUPS = 16
TAPS = 27
FB = 2
BMAX = 3
LANES = 128
F32 = jnp.float32
BF16 = jnp.bfloat16
SMEM = pl.BlockSpec(memory_space=pltpu.SMEM)
VMEM = pl.BlockSpec(memory_space=pltpu.VMEM)
PARAMS = pltpu.CompilerParams(vmem_limit_bytes=48 * 1024 * 1024)


def round_up(value, unit):
    return -(-value // unit) * unit


def column_table(och, width):
    table = np.zeros((width, 9 * LANES), np.float32)
    for o in range(och):
        for a in range(3):
            for b in range(3):
                for e in range(3):
                    table[27 * o + 9 * a + 3 * b + e, (3 * b + e) * LANES + (2 - a) * och + o] = 1
    return table.astype(BF16)


def fold(values, slice_index, och):
    groups = LANES // och
    rows = round_up(-(-values.shape[0] // groups), 16)
    short = rows * groups - values.shape[0]
    if short:
        values = jnp.concatenate([values, jnp.zeros((short, LANES), values.dtype)], axis=0)
    lane_group = lax.broadcasted_iota(jnp.int32, (rows, LANES), 1) // och
    total = jnp.zeros((rows, LANES), F32)
    for g in range(groups):
        shift = jnp.mod((g - slice_index) * och + LANES, LANES)
        moved = pltpu.roll(values[g * rows : (g + 1) * rows], shift, 1)
        total = total + jnp.where(lane_group == g, moved, 0.0)
    return total


def first_block_of(blocks_ref, first_clip, clips):
    start = jnp.int32(0)
    for k in range(clips):
        start = start + jnp.where(k < first_clip, blocks_ref[k], 0)
    return start


def slot_holders(blocks_ref, order_ref, me, slots, clips, held, devs):
    residue = jnp.int32(0)
    for r in range(devs):
        residue = jnp.where(order_ref[r] == me, r, residue)
    clip_of = [jnp.int32(0)] * slots
    end = jnp.int32(0)
    for k in range(clips):
        end = end + blocks_ref[k]
        for q in range(slots):
            clip_of[q] = clip_of[q] + jnp.where(end <= q * devs + residue, 1, 0)
    return [jnp.minimum(c, clips - 1) // held for c in clip_of]


def pack_kernel(dims, blocks_ref, order_ref, kernel_ref, cot_ref, out_ref):
    devs, slots, clips, held, rows_in, cols, lane0 = dims
    me = lax.axis_index("clips")
    holders = slot_holders(blocks_ref, order_ref, me, slots, clips, held, devs)
    rows = out_ref.shape[1]
    weights = kernel_ref[...].astype(F32)
    weights = jnp.concatenate([weights, jnp.zeros((rows_in, lane0 - cols), F32)], axis=1)
    if rows > rows_in:
        weights = jnp.concatenate([weights, jnp.zeros((rows - rows_in, lane0), F32)], axis=0)
    weights = weights.astype(BF16)
    for d in range(devs):
        out_ref[d, :, 0:lane0] = weights
    for q in range(slots):
        out_ref[holders[q], :, lane0 : lane0 + LANES] = cot_ref[q]


def spread_kernel(dims, blocks_ref, order_ref, table_ref, received_ref, *outs):
    devs, slab, clips, held, rows_in, lane0, och = dims
    weights_ref, payload_refs = outs[0], outs[1:]
    me, own = lax.axis_index("clips"), lax.axis_index("slab")
    start = first_block_of(blocks_ref, me * held, clips)
    pieces = []
    for k in range(held):
        count = blocks_ref[me * held + k]
        for b in range(BMAX):
            source = order_ref[jnp.mod(start + b, devs)]
            piece = received_ref[source, :, lane0 : lane0 + LANES].astype(F32)
            pieces.append(jnp.where(b < count, piece, 0.0))
        start = start + count
    cot = jnp.concatenate(pieces, axis=0)
    for i, ref in enumerate(payload_refs):
        ref[...] = fold(cot, jnp.mod(own + i, slab), och).astype(BF16)
    weights = received_ref[:, :, 0:lane0]
    if weights.shape[1] > rows_in:
        weights = weights.astype(F32)[:, :rows_in].reshape(devs * rows_in, lane0).astype(BF16)
    else:
        weights = weights.reshape(devs * rows_in, lane0)
    weights_ref[...] = jnp.dot(weights, table_ref[...], preferred_element_type=F32).astype(BF16)


def split3(values):
    high = values.astype(BF16).astype(F32)
    rest = values - high
    middle = rest.astype(BF16).astype(F32)
    return [high, middle, rest - middle]


def main_kernel(dims, blocks_ref, order_ref, gain_ref, bias_ref, table_ref, weights_ref, *refs):
    devs, slab, clips, held, frames, columns, rows_in, cols, lane0, och, per_group = dims
    video_refs, cot_refs = refs[:slab], refs[slab : 2 * slab]
    out_ref, grad_ref, video_pad, cot_rows = refs[2 * slab :]
    me, own = lax.axis_index("clips"), lax.axis_index("slab")
    places = held * frames * columns
    per_clip = frames * columns
    c_in = video_pad.shape[2]
    groups = LANES // och
    video_pad[0] = jnp.zeros((places, c_in), BF16)
    video_pad[slab + 1] = jnp.zeros((places, c_in), BF16)
    for i in range(slab):
        row = jnp.mod(own - i + slab, slab)
        video_pad[row + 1] = video_refs[i][...]
        folded = cot_refs[i][...].astype(F32)
        parts = [folded[:, g * och : (g + 1) * och] for g in range(groups)]
        cot_rows[row] = jnp.concatenate(parts, axis=0)[:places]

    total = None
    for b in range(3):
        rows = video_pad[b : b + slab].reshape(slab * places, c_in)
        term = jnp.dot(rows, weights_ref[:, 384 * b : 384 * (b + 1)], preferred_element_type=F32)
        total = term if total is None else total + term
    column = lax.broadcasted_iota(jnp.int32, (slab * places, LANES), 0) % columns
    many = slab * places

    def from_left(values):
        return jnp.where(column > 0, pltpu.roll(values, 1, 0), 0.0)

    def from_right(values):
        return jnp.where(column < columns - 1, pltpu.roll(values, many - 1, 0), 0.0)

    mixed = (
        from_left(total[:, 0:LANES])
        + total[:, LANES : 2 * LANES]
        + from_right(total[:, 2 * LANES :])
    ).reshape(slab, places, LANES)
    frame_shifts = [mixed[:, :, a * och : (a + 1) * och] for a in range(3)]

    shift = jnp.mod(LANES - own * och, LANES)
    gain = pltpu.roll(jnp.broadcast_to(gain_ref[...], (8, LANES)), shift, 1)[0:1, :och]
    bias = pltpu.roll(jnp.broadcast_to(bias_ref[...], (8, LANES)), shift, 1)[0:1, :och]
    same = lax.broadcasted_iota(jnp.int32, (och, och), 0) // per_group
    same = (same == lax.broadcasted_iota(jnp.int32, (och, och), 1) // per_group).astype(F32)

    def group_mean_of(values, count):
        sums = jnp.sum(jnp.sum(values, axis=0), axis=0, keepdims=True)
        sums = jnp.broadcast_to(sums, (8, och))
        sums = jnp.dot(sums, same, precision=lax.Precision.HIGHEST, preferred_element_type=F32)
        return (sums[0:1] / count)[None]

    frame_of = lax.broadcasted_iota(jnp.int32, (slab, per_clip, och), 1) // columns
    gain_part = jnp.zeros((1, och), F32)
    bias_part = jnp.zeros((1, och), F32)
    start = first_block_of(blocks_ref, me * held, clips)
    conv_grads = []
    act_blocks = []
    for k in range(held):
        blocks = blocks_ref[me * held + k]
        conv = frame_shifts[0][:, k * per_clip : (k + 1) * per_clip]
        for a in (1, 2):
            part = frame_shifts[a][:, k * per_clip : (k + 1) * per_clip - a * columns]
            conv = conv + jnp.concatenate([jnp.zeros((slab, a * columns, och), F32), part], axis=1)
        alive = frame_of < blocks * FB
        count = (blocks * (FB * slab * columns * per_group)).astype(F32)
        kept = jnp.where(alive, conv, 0.0)
        mean = group_mean_of(kept, count)
        var = group_mean_of(kept * conv, count) - mean * mean
        inv_std = lax.rsqrt(var + 1e-05)
        normed = (conv - mean) * inv_std
        affine = normed * gain[None] + bias[None]
        sigmoid = jax.nn.sigmoid(affine)
        act = affine * sigmoid
        cot = cot_rows[:, k * per_clip : (k + 1) * per_clip, :]
        grad_affine = jnp.where(alive, cot * sigmoid * (1.0 + affine * (1.0 - sigmoid)), 0.0)
        gain_part += jnp.sum(jnp.sum(grad_affine * normed, axis=0), axis=0, keepdims=True)
        bias_part += jnp.sum(jnp.sum(grad_affine, axis=0), axis=0, keepdims=True)
        grad_normed = grad_affine * gain[None]
        mean_grad = group_mean_of(grad_normed, count)
        mean_cross = group_mean_of(grad_normed * normed, count)
        grad_conv = inv_std * (grad_normed - mean_grad - normed * mean_cross)
        grad_conv = jnp.where(alive, grad_conv, 0.0).astype(BF16).astype(F32)
        lanes = [grad_conv]
        for a in (1, 2):
            zeros = jnp.zeros((slab, a * columns, och), F32)
            lanes.append(jnp.concatenate([grad_conv[:, a * columns :], zeros], axis=1))
        if LANES > 3 * och:
            lanes.append(jnp.zeros((slab, per_clip, LANES - 3 * och), F32))
        conv_grads.append(jnp.concatenate(lanes, axis=2))
        rows = FB * columns
        for b in range(BMAX):
            block = [act[h, b * rows : (b + 1) * rows] for h in range(slab)]
            dest = order_ref[jnp.mod(start + b, devs)]
            act_blocks.append((b < blocks, dest, jnp.concatenate(block, axis=1).astype(BF16)))
        start = start + blocks

    grads = jnp.concatenate(conv_grads, axis=1).reshape(many, LANES)
    grad_ref[0] = jnp.zeros((places, 3 * LANES), BF16)
    grad_ref[slab + 1] = jnp.zeros((places, 3 * LANES), BF16)
    for e, shifted in enumerate((from_right(grads), grads, from_left(grads))):
        shifted = shifted.astype(BF16).reshape(slab, places, LANES)
        grad_ref[1 : slab + 1, :, e * LANES : (e + 1) * LANES] = shifted

    video_t = jnp.transpose(video_pad[1 : slab + 1].reshape(many, c_in))
    parts = []
    for b in range(3):
        moved = grad_ref[2 - b : 2 - b + slab].reshape(many, 3 * LANES)
        parts.append(jnp.dot(video_t, moved, preferred_element_type=F32).astype(BF16))
    native = lax.dot_general(
        jnp.concatenate(parts, axis=1),
        table_ref[...],
        (((1,), (1,)), ((), ())),
        preferred_element_type=F32,
    ).reshape(devs, rows_in, lane0)
    out_rows = out_ref.shape[1]
    if out_rows > rows_in:
        zeros = jnp.zeros((devs, out_rows - rows_in, lane0), F32)
        native = jnp.concatenate([native, zeros], axis=1)
    sums = split3(gain_part) + split3(bias_part)
    sums = jnp.concatenate(sums + [jnp.zeros((out_rows - 6, och), F32)], axis=0)
    fill = jnp.zeros((out_rows, LANES - och), F32)
    sums = jnp.concatenate([fill, sums], axis=1)
    out_ref[:, :, 0 : lane0 - LANES] = native[:, :, 0 : lane0 - LANES].astype(BF16)
    last = native[:, :, lane0 - LANES : lane0] + sums[None]
    out_ref[:, :, lane0 - LANES : lane0] = last.astype(BF16)
    for alive, dest, block in act_blocks:

        @pl.when(alive)
        def _(dest=dest, block=block):
            out_ref[dest, :, lane0 : lane0 + LANES] = block


def video_grad_kernel(slab, grad_ref, weights_ref, *outs):
    own = lax.axis_index("slab")
    for i, ref in enumerate(outs):
        row = jnp.mod(own + i, slab)
        total = None
        for b in range(3):
            term = lax.dot_general(
                grad_ref[row + 2 - b],
                weights_ref[:, 384 * b : 384 * (b + 1)],
                (((1,), (1,)), ((), ())),
                preferred_element_type=F32,
            )
            total = term if total is None else total + term
        ref[...] = total.astype(ref.dtype)


def settle_kernel(dims, blocks_ref, order_ref, received_ref, kernel_grad_ref, *payload_refs):
    devs, slab, slots, clips, held, rows_in, cols, lane0, och = dims
    me, own = lax.axis_index("clips"), lax.axis_index("slab")
    total = received_ref[0, :, 0:lane0].astype(F32)
    for d in range(1, devs):
        total = total + received_ref[d, :, 0:lane0].astype(F32)
    kernel_grad_ref[...] = total[:rows_in, :cols]
    sums = total[:, lane0 - och : lane0]
    pair = [sums[0:1] + (sums[1:2] + sums[2:3]), sums[3:4] + (sums[4:5] + sums[5:6])]
    sums = jnp.concatenate(split3(pair[0]) + split3(pair[1]) + [jnp.zeros((10, och), F32)], axis=0)
    sums = jnp.concatenate([sums, jnp.zeros((16, LANES - och), F32)], axis=1)
    holders = slot_holders(blocks_ref, order_ref, me, slots, clips, held, devs)
    acts = [received_ref[h, :, lane0 : lane0 + LANES].astype(F32) for h in holders]
    acts = jnp.concatenate(acts, axis=0)
    for i, ref in enumerate(payload_refs):
        folded = fold(acts, jnp.mod(own + i, slab), och)
        ref[...] = jnp.concatenate([folded, sums], axis=0).astype(BF16)


def finish_kernel(slab, och, *refs):
    grad_refs, payload_refs = refs[:slab], refs[slab : 2 * slab]
    video_grad_ref, act_ref, gain_ref, bias_ref = refs[2 * slab :]
    own = lax.axis_index("slab")
    total = grad_refs[0][...]
    for ref in grad_refs[1:]:
        total = total + ref[...].astype(F32)
    video_grad_ref[...] = total.astype(BF16)
    groups = LANES // och
    rows = payload_refs[0].shape[0] - 16
    lane_group = lax.broadcasted_iota(jnp.int32, (rows, LANES), 1) // och
    acts = [jnp.zeros((rows, LANES), F32)] * groups
    sums = jnp.zeros((16, LANES), F32)
    for i, ref in enumerate(payload_refs):
        source = jnp.mod(own - i + slab, slab)
        payload = ref[...].astype(F32)
        for g in range(groups):
            shift = jnp.mod((source - g) * och + LANES, LANES)
            moved = pltpu.roll(payload[:rows], shift, 1)
            acts[g] = acts[g] + jnp.where(lane_group == source, moved, 0.0)
        moved = pltpu.roll(payload[rows:], source * och, 1)
        sums = sums + jnp.where(lane_group[:16] == source, moved, 0.0)
    act_ref[...] = jnp.concatenate(acts, axis=0)[: act_ref.shape[0]].astype(BF16)
    gain_ref[...] = sums[0:1] + (sums[1:2] + sums[2:3])
    bias_ref[...] = sums[3:4] + (sums[4:5] + sums[5:6])


def call(kernel, outs, specs, scratch=()):
    return pl.pallas_call(
        kernel,
        out_shape=outs,
        in_specs=specs,
        out_specs=[VMEM] * len(outs),
        scratch_shapes=list(scratch),
        compiler_params=PARAMS,
    )


def shifts(arrays, axis):
    size = lax.axis_size(axis)
    moved = [arrays[0]]
    for i in range(1, size):
        moved.append(lax.ppermute(arrays[i], axis, [(j, (j + i) % size) for j in range(size)]))
    return moved


def body(video, clip_blocks, deal_order, kernel, gain, bias, cotangent):
    devs, slab = lax.axis_size("clips"), lax.axis_size("slab")
    held, frames, _, columns, c_in = video.shape
    slots, clips = cotangent.shape[0], clip_blocks.shape[0]
    c_out = gain.shape[0]
    rows_in, cols = kernel.shape
    och = c_out // slab
    per_group = c_out // GROUPS
    lane0 = round_up(cols, LANES)
    places = held * frames * columns
    block_rows = FB * columns
    out_rows = max(rows_in, block_rows)
    shape = jax.ShapeDtypeStruct
    table = jnp.asarray(column_table(och, lane0))
    gain, bias = gain.reshape(1, c_out), bias.reshape(1, c_out)

    packed = call(
        functools.partial(pack_kernel, (devs, slots, clips, held, rows_in, cols, lane0)),
        [shape((devs, out_rows, lane0 + LANES), BF16)],
        [SMEM, SMEM, VMEM, VMEM],
    )(clip_blocks, deal_order, kernel, cotangent.reshape(slots, block_rows, c_out))[0]
    received = lax.all_to_all(packed, "clips", split_axis=0, concat_axis=0, tiled=True)
    videos = shifts([video.reshape(places, c_in)] * slab, "slab")

    fold_rows = round_up(-(-places // (LANES // och)), 16)
    weights, *cots = call(
        functools.partial(spread_kernel, (devs, slab, clips, held, rows_in, lane0, och)),
        [shape((c_in, 9 * LANES), BF16)] + [shape((fold_rows, LANES), BF16)] * slab,
        [SMEM, SMEM, VMEM, VMEM],
    )(clip_blocks, deal_order, table, received)
    cots = shifts(cots, "slab")

    dims = (devs, slab, clips, held, frames, columns, rows_in, cols, lane0, och, per_group)
    packed, grads = call(
        functools.partial(main_kernel, dims),
        [
            shape((devs, out_rows, lane0 + LANES), BF16),
            shape((slab + 2, places, 3 * LANES), BF16),
        ],
        [SMEM, SMEM] + [VMEM] * (4 + 2 * slab),
        [
            pltpu.VMEM((slab + 2, places, c_in), BF16),
            pltpu.VMEM((slab, places, och), F32),
        ],
    )(clip_blocks, deal_order, gain, bias, table, weights, *videos, *cots)
    received = lax.all_to_all(packed, "clips", split_axis=0, concat_axis=0, tiled=True)

    video_grads = call(
        functools.partial(video_grad_kernel, slab),
        [shape((places, c_in), F32 if i == 0 else BF16) for i in range(slab)],
        [VMEM, VMEM],
    )(grads, weights)
    video_grads = shifts(video_grads, "slab")

    fold_rows = round_up(-(-slots * block_rows // (LANES // och)), 16)
    kernel_grad, *payloads = call(
        functools.partial(
            settle_kernel, (devs, slab, slots, clips, held, rows_in, cols, lane0, och)
        ),
        [shape((rows_in, cols), F32)] + [shape((fold_rows + 16, LANES), BF16)] * slab,
        [SMEM, SMEM, VMEM],
    )(clip_blocks, deal_order, received)
    payloads = shifts(payloads, "slab")

    video_grad, act, gain_grad, bias_grad = call(
        functools.partial(finish_kernel, slab, och),
        [
            shape((places, c_in), BF16),
            shape((slots * block_rows, c_out), BF16),
            shape((1, c_out), F32),
            shape((1, c_out), F32),
        ],
        [VMEM] * (2 * slab),
    )(*video_grads, *payloads)
    return (
        act.reshape(cotangent.shape),
        video_grad.reshape(video.shape),
        kernel_grad,
        gain_grad.reshape(c_out),
        bias_grad.reshape(c_out),
    )


def solution(mesh):
    return jax.shard_map(
        body,
        mesh=mesh,
        in_specs=(
            P("clips", None, "slab", None, None),
            P(),
            P(),
            P("clips", "slab"),
            P(),
            P(),
            P("clips", None, "slab", None, None),
        ),
        out_specs=(
            P("clips", None, "slab", None, None),
            P("clips", None, "slab", None, None),
            P("clips", "slab"),
            P(),
            P(),
        ),
        check_vma=False,
    )
```

time: 353 us -> 60.4 us (0.17)
  blocking collectives: 95.3 us -> 0 us
  waiting for transfers between devices: 82.8 us -> 15.8 us
  local copies, waits for them, and re-layouts: 69.8 us -> 5.79 us
  matrix products: 54.7 us -> 0 us
  between operations: 15.6 us -> 0.71 us
  other arithmetic: 11.7 us -> 0 us
  Pallas kernels: 0 us -> 11 us
  starting transfers between devices: 21 us -> 26.6 us
    psum x2 -> x0, blocking collectives: 81 us -> none  [the longest x1 41.6 us: body(): lax.psum((sum_grad, sum_cross, gain_part, bias_part), ('clips', 'slab'))]
    dot_general x89 -> x0, matrix products: 54.7 us -> none  [the longest x27 24.1 us: body(): jnp.dot(tap_rows, kernel_taps[(forward_step_a * 3 + forward_step_b) * 3 +...]
    reduce_scatter x1 -> x0, waiting for transfers between devices: 37.1 us -> none  [body(): lax.psum_scatter(partial_grad, 'slab', scatter_dimension=1, tiled=True)]
    unnamed x4 -> x0, waiting for transfers between devices: 34.4 us -> none
    slice x35 -> x0, local copies, waits for them, and re-layouts: 30.2 us -> none  [the longest x29 26.9 us: body(): kernel_taps[(forward_step_a * 3 + forward_step_b) * 3 + forward_step_c]]
    all_gather x1 -> x0, blocking collectives: 14.2 us -> none  [body(): full_kernel = lax.all_gather(kernel, 'slab', axis=1, tiled=True)]
    pallas_call x0 -> x6, Pallas kernels: none -> 11 us  [the longest x1 4.97 us: body(): call(functools.partial(main_kernel, dims), [shape((devs, out_rows, lane0...]
    all_to_all x2, waiting for transfers between devices: 0.01 us -> 9.92 us  [body(): lax.all_to_all(packed, 'clips', split_axis=0, concat_axis=0, tiled=True)]
  transfers between devices with their start and end apart: 9 -> 14, of which waited for: 6 -> 6; matrix products, arithmetic and copies ran while one was open for 16% -> 0% of each run, Pallas kernels for 0% -> 6%
where the time goes in v1:
time: 60.4 us; the launch traced here: 59.9 us
  starting transfers between devices  26.6 us (44%)
  waiting for transfers between devices  15.8 us (26%)
  Pallas kernels  11 us (18%)
  local copies, waits for them, and re-layouts  5.79 us (10%)
  between operations  0.71 us (1%)
    ppermute x12, starting transfers between devices, shifts(): lax.ppermute(arrays[i], axis, [(j, (j + i) % size) for j in range(size)])  17.9 us
    all_to_all x2, waiting for transfers between devices, body(): lax.all_to_all(packed, 'clips', split_axis=0, concat_axis=0, tiled=True)  9.92 us
    all_to_all x2, starting transfers between devices, body(): lax.all_to_all(packed, 'clips', split_axis=0, concat_axis=0, tiled=True)  8.66 us
    ppermute x12, waiting for transfers between devices, shifts(): lax.ppermute(arrays[i], axis, [(j, (j + i) % size) for j in range(size)])  5.92 us
    unnamed x24, local copies, waits for them, and re-layouts  5.79 us
    pallas_call x1, Pallas kernels, body(): call(functools.partial(main_kernel, dims), [shape((devs, out_rows, lane0...  4.97 us
    pallas_call x1, Pallas kernels, body(): call(functools.partial(pack_kernel, (devs, slots, clips, held, rows_in, c...  1.46 us
    pallas_call x1, Pallas kernels, body(): call(functools.partial(settle_kernel, (devs, slab, slots, clips, held, ro...  1.43 us
  transfers between devices with their start and end apart: 14, of which 6 were waited for; matrix products, arithmetic and copies ran while one was open for 0% of the time, Pallas kernels for 6%

profile of v1, /device:TPU:0, one launch (start us, length us, event | category | flops | bytes accessed | tf_op | source)
XLA Modules:
  0.0 59.9 jit_solution(6196585146732045563)
XLA Ops:
  0.6 0.8 %copy-done.2 = bf16[32,864]{1,0:T(8,128)(2,1)S(1)} copy-done((bf16[32,864]{1,0:T(8,128)(2,1)S(1)}, bf16[32,864]{1,0:T(8,128)(2,1)}, u32[]{:S(2)}) %copy-start.2) | copy-done | bytes 55320
  1.5 0.8 %copy-done.3 = bf16[4,2,1,16,128]{4,3,2,1,0:T(8,128)(2,1)S(1)} copy-done((bf16[4,2,1,16,128]{4,3,2,1,0:T(8,128)(2,1)S(1)}, bf16[4,2,1,16,128]{4,3,2,1,0:T(8,128)(2,1)}, u32[]{:S(2)}) %copy-start.3) | copy-done | bytes 32792
  2.2 0.7 %copy-done.4 = s32[16]{0:T(128)S(1)} copy-done((s32[16]{0:T(128)S(1)}, s32[16]{0:T(128)}, u32[]{:S(2)}) %copy-start.4) | copy-done | bytes 88
  3.5 1.5 %shard_map.119 = bf16[8,32,1024]{2,1,0:T(8,128)(2,1)} custom-call(s32[16]{0:T(128)S(1)} %copy-done.4, s32[8]{0:T(128)S(1)} %copy-done.7, bf16[32,864]{1,0:T(8,128)(2,1)S(1)} %copy-done.2, bf16[4,32,128]{2,1,0:T(8,128)(2,1)S(1)} %bitcast.16), custom_call_target="tpu_custom_call" | custom-call | tf_op jit(solution)/shard_map/pallas_call | solution.py:348
  5.0 5.2 %all-to-all-start = ((bf16[8,32,1024]{2,1,0:T(8,128)(2,1)}), bf16[8,32,1024]{2,1,0:T(8,128)(2,1)S(1)}, u32[]{:S(2)}, u32[]{:S(2)}) async-start(bf16[8,32,1024]{2,1,0:T(8,128)(2,1)} %shard_map.119), calls=%async_computation | async-start | bytes 1048576 | tf_op jit(solution)/shard_map/all_to_all | solution.py:353
  10.2 3.6 %collective-permute-start.2 = (bf16[192,256]{1,0:T(8,128)(2,1)}, bf16[192,256]{1,0:T(8,128)(2,1)S(1)}, u32[]{:S(2)}, u32[]{:S(2)}) collective-permute-start(bf16[192,256]{1,0:T(8,128)(2,1)} %bitcast.12), channel_id=1, source_target_pairs={{0,3},{1,0},{2,1},{3,2},{4,7},{5,4},{6,5},{7,6},{8,11},{9,8},{10,9... | collective-permute-start | bytes 294920 | tf_op jit(solution)/shard_map/ppermute | solution.py:328
  13.8 1.0 %collective-permute-start = (bf16[192,256]{1,0:T(8,128)(2,1)}, bf16[192,256]{1,0:T(8,128)(2,1)S(1)}, u32[]{:S(2)}, u32[]{:S(2)}) collective-permute-start(bf16[192,256]{1,0:T(8,128)(2,1)} %bitcast.14), channel_id=1, source_target_pairs={{0,1},{1,2},{2,3},{3,0},{4,5},{5,6},{6,7},{7,4},{8,9},{9,10},{10,1... | collective-permute-start | bytes 294920 | tf_op jit(solution)/shard_map/ppermute | solution.py:328
  14.8 5.1 %all-to-all-done.received_ref = bf16[8,32,1024]{2,1,0:T(8,128)(2,1)S(1)} async-done(((bf16[8,32,1024]{2,1,0:T(8,128)(2,1)}), bf16[8,32,1024]{2,1,0:T(8,128)(2,1)S(1)}, u32[]{:S(2)}, u32[]{:S(2)}) %all-to-all-start) | async-done | bytes 524320 | tf_op jit(solution)/shard_map/all_to_all | solution.py:353
  19.9 1.6 %copy-done = bf16[896,1152]{1,0:T(8,128)(2,1)S(1)} copy-done((bf16[896,1152]{1,0:T(8,128)(2,1)S(1)}, bf16[896,1152]{1,0:T(8,128)(2,1)}, u32[]{:S(2)}) %copy-start) | copy-done | bytes 2064408
  22.8 1.4 %shard_map.120 = (bf16[256,1152]{1,0:T(8,128)(2,1)S(1)}, bf16[48,128]{1,0:T(8,128)(2,1)S(1)}, bf16[48,128]{1,0:T(8,128)(2,1)S(1)}, bf16[48,128]{1,0:T(8,128)(2,1)S(1)}, bf16[48,128]{1,0:T(8,128)(2,1)S(1)}) custom-call(s32[16]{0:T(128)S(1)} %copy-done.5, s32[8]{0:T(128)S(1)} %copy-done.8, bf16[896,1152]{1,0:T(8,128)(2,1)S(1)} %copy-done, ...), custom_call_target="tpu_custom_call" | custom-call | tf_op jit(solution)/shard_map/pallas_call | solution.py:357
  24.2 1.6 %collective-permute-start.3 = (bf16[48,128]{1,0:T(8,128)(2,1)S(1)}, bf16[48,128]{1,0:T(8,128)(2,1)S(1)}, u32[]{:S(2)}, u32[]{:S(2)}) collective-permute-start(bf16[48,128]{1,0:T(8,128)(2,1)S(1)} %get-tuple-element.27), channel_id=1, source_target_pairs={{0,1},{1,2},{2,3},{3,0},{4,5},{5,6},{6,7},{7,4},{8,9},{9,10},{10,1... | collective-permute-start | bytes 36872 | tf_op jit(solution)/shard_map/ppermute | solution.py:328
  25.8 2.6 %collective-permute-start.4 = (bf16[48,128]{1,0:T(8,128)(2,1)S(1)}, bf16[48,128]{1,0:T(8,128)(2,1)S(1)}, u32[]{:S(2)}, u32[]{:S(2)}) collective-permute-start(bf16[48,128]{1,0:T(8,128)(2,1)S(1)} %get-tuple-element.28), channel_id=1, source_target_pairs={{0,2},{1,3},{2,0},{3,1},{4,6},{5,7},{6,4},{7,5},{8,10},{9,11},{10,... | collective-permute-start | bytes 36872 | tf_op jit(solution)/shard_map/ppermute | solution.py:328
  28.4 1.3 %collective-permute-start.5 = (bf16[48,128]{1,0:T(8,128)(2,1)S(1)}, bf16[48,128]{1,0:T(8,128)(2,1)S(1)}, u32[]{:S(2)}, u32[]{:S(2)}) collective-permute-start(bf16[48,128]{1,0:T(8,128)(2,1)S(1)} %get-tuple-element.29), channel_id=1, source_target_pairs={{0,3},{1,0},{2,1},{3,2},{4,7},{5,4},{6,5},{7,6},{8,11},{9,8},{10,9... | collective-permute-start | bytes 36872 | tf_op jit(solution)/shard_map/ppermute | solution.py:328
  30.4 1.7 %collective-permute-done.5.refs_7_ = bf16[48,128]{1,0:T(8,128)(2,1)S(1)} collective-permute-done((bf16[48,128]{1,0:T(8,128)(2,1)S(1)}, bf16[48,128]{1,0:T(8,128)(2,1)S(1)}, u32[]{:S(2)}, u32[]{:S(2)}) %collective-permute-start.5) | collective-permute-done | bytes 12320 | tf_op jit(solution)/shard_map/ppermute | solution.py:328
  32.1 5.0 %shard_map.121 = (bf16[8,32,1024]{2,1,0:T(8,128)(2,1)}, bf16[6,192,384]{2,1,0:T(8,128)(2,1)S(1)}) custom-call(s32[16]{0:T(128)S(1)} %copy-done.5, s32[8]{0:T(128)S(1)} %copy-done.8, f32[1,128]{1,0:T(1,128)S(1)} %bitcast.17, f32[1,128]{1,0:T(1,128)S(1)} %bitcast.18, bf16[896,1152]{1,0:T(8,128)(2,1)S(1)} %copy-done, ...), custom_call_target="tpu_custom_call" | custom-call | tf_op jit(solution)/shard_map/pallas_call | solution.py:365
  37.1 3.5 %all-to-all-start.1 = ((bf16[8,32,1024]{2,1,0:T(8,128)(2,1)}), bf16[8,32,1024]{2,1,0:T(8,128)(2,1)S(1)}, u32[]{:S(2)}, u32[]{:S(2)}) async-start(bf16[8,32,1024]{2,1,0:T(8,128)(2,1)} %get-tuple-element.35), calls=%async_computation.1 | async-start | bytes 1048576 | tf_op jit(solution)/shard_map/all_to_all | solution.py:377
  40.6 1.0 %shard_map.122 = (f32[192,256]{1,0:T(8,128)S(1)}, bf16[192,256]{1,0:T(8,128)(2,1)S(1)}, bf16[192,256]{1,0:T(8,128)(2,1)S(1)}, bf16[192,256]{1,0:T(8,128)(2,1)S(1)}) custom-call(bf16[6,192,384]{2,1,0:T(8,128)(2,1)S(1)} %get-tuple-element.30.grad_ref, bf16[256,1152]{1,0:T(8,128)(2,1)S(1)} %get-tuple-element.25.weights_ref), custom_call_target="tpu_custom_call" | custom-call | tf_op jit(solution)/shard_map/pallas_call | solution.py:379
  41.8 3.5 %collective-permute-start.7 = (bf16[192,256]{1,0:T(8,128)(2,1)S(1)}, bf16[192,256]{1,0:T(8,128)(2,1)S(1)}, u32[]{:S(2)}, u32[]{:S(2)}) collective-permute-start(bf16[192,256]{1,0:T(8,128)(2,1)S(1)} %get-tuple-element.33), channel_id=1, source_target_pairs={{0,2},{1,3},{2,0},{3,1},{4,6},{5,7},{6,4},{7,5},{8,10},{9,11},{10,... | collective-permute-start | bytes 294920 | tf_op jit(solution)/shard_map/ppermute | solution.py:328
  45.5 4.8 %all-to-all-done.1.received_ref = bf16[8,32,1024]{2,1,0:T(8,128)(2,1)S(1)} async-done(((bf16[8,32,1024]{2,1,0:T(8,128)(2,1)}), bf16[8,32,1024]{2,1,0:T(8,128)(2,1)S(1)}, u32[]{:S(2)}, u32[]{:S(2)}) %all-to-all-start.1) | async-done | bytes 524320 | tf_op jit(solution)/shard_map/all_to_all | solution.py:377
  50.3 1.4 %shard_map.123 = (f32[32,864]{1,0:T(8,128)}, bf16[48,128]{1,0:T(8,128)(2,1)S(1)}, bf16[48,128]{1,0:T(8,128)(2,1)S(1)}, bf16[48,128]{1,0:T(8,128)(2,1)S(1)}, bf16[48,128]{1,0:T(8,128)(2,1)S(1)}) custom-call(s32[16]{0:T(128)S(1)} %copy-done.6, s32[8]{0:T(128)S(1)} %copy-done.9, bf16[8,32,1024]{2,1,0:T(8,128)(2,1)S(1)} %all-to-all-done.1.received_ref), custom_call_target="tpu_custom_call" | custom-call | tf_op jit(solution)/shard_map/pallas_call | solution.py:387
  51.9 3.5 %collective-permute-start.10 = (bf16[48,128]{1,0:T(8,128)(2,1)S(1)}, bf16[48,128]{1,0:T(8,128)(2,1)S(1)}, u32[]{:S(2)}, u32[]{:S(2)}) collective-permute-start(bf16[48,128]{1,0:T(8,128)(2,1)S(1)} %get-tuple-element.38), channel_id=1, source_target_pairs={{0,2},{1,3},{2,0},{3,1},{4,6},{5,7},{6,4},{7,5},{8,10},{9,11},{10,... | collective-permute-start | bytes 36872 | tf_op jit(solution)/shard_map/ppermute | solution.py:328
  55.5 1.7 %collective-permute-done.9.refs_5_ = bf16[48,128]{1,0:T(8,128)(2,1)S(1)} collective-permute-done((bf16[48,128]{1,0:T(8,128)(2,1)S(1)}, bf16[48,128]{1,0:T(8,128)(2,1)S(1)}, u32[]{:S(2)}, u32[]{:S(2)}) %collective-permute-start.9) | collective-permute-done | bytes 12320 | tf_op jit(solution)/shard_map/ppermute | solution.py:328
  57.2 1.9 %collective-permute-done.11.refs_7_ = bf16[48,128]{1,0:T(8,128)(2,1)S(1)} collective-permute-done((bf16[48,128]{1,0:T(8,128)(2,1)S(1)}, bf16[48,128]{1,0:T(8,128)(2,1)S(1)}, u32[]{:S(2)}, u32[]{:S(2)}) %collective-permute-start.11) | collective-permute-done | bytes 12320 | tf_op jit(solution)/shard_map/ppermute | solution.py:328
  59.1 0.8 %shard_map.124 = (bf16[192,256]{1,0:T(8,128)(2,1)}, bf16[128,128]{1,0:T(8,128)(2,1)}, f32[1,128]{1,0:T(1,128)}, f32[1,128]{1,0:T(1,128)}) custom-call(f32[192,256]{1,0:T(8,128)S(1)} %get-tuple-element.31.refs_0_, bf16[192,256]{1,0:T(8,128)(2,1)S(1)} %collective-permute-done.6.refs_1_, bf16[192,256]{1,0:T(8,128)(2,1)S(1)} %collective-permute-done.7.refs_2_, ...), custom_call_target="tpu_custom_call" | custom-call | tf_op jit(solution)/shard_map/pallas_call | solution.py:396
  (34 shorter events, 3.4 us)
Async XLA Ops:
  0.6 0.8 %copy-start.2 = (bf16[32,864]{1,0:T(8,128)(2,1)S(1)}, bf16[32,864]{1,0:T(8,128)(2,1)}, u32[]{:S(2)}) copy-start(bf16[32,864]{1,0:T(8,128)(2,1)} %kernel_ref.1) | copy-start | bytes 165892
  1.5 0.8 %copy-start.3 = (bf16[4,2,1,16,128]{4,3,2,1,0:T(8,128)(2,1)S(1)}, bf16[4,2,1,16,128]{4,3,2,1,0:T(8,128)(2,1)}, u32[]{:S(2)}) copy-start(bf16[4,2,1,16,128]{4,3,2,1,0:T(8,128)(2,1)} %param.14) | copy-start | bytes 98308
  2.2 0.7 %copy-start.4 = (s32[16]{0:T(128)S(1)}, s32[16]{0:T(128)}, u32[]{:S(2)}) copy-start(s32[16]{0:T(128)} %blocks_ref.7) | copy-start | bytes 196
  3.5 28.6 %copy-start.1 = (bf16[2,6,1,16,256]{4,3,2,1,0:T(8,128)(2,1)S(1)}, bf16[2,6,1,16,256]{4,3,2,1,0:T(8,128)(2,1)}, u32[]{:S(2)}) copy-start(bf16[2,6,1,16,256]{4,3,2,1,0:T(8,128)(2,1)} %param.8) | copy-start | bytes 294916
  3.5 28.6 %copy-start.10 = (f32[128]{0:T(128)S(1)}, f32[128]{0:T(128)}, u32[]{:S(2)}) copy-start(f32[128]{0:T(128)} %param.12) | copy-start | bytes 1540
  3.5 28.6 %copy-start.11 = (f32[128]{0:T(128)S(1)}, f32[128]{0:T(128)}, u32[]{:S(2)}) copy-start(f32[128]{0:T(128)} %param.13) | copy-start | bytes 1540
  5.0 14.9 %all-to-all-start = ((bf16[8,32,1024]{2,1,0:T(8,128)(2,1)}), bf16[8,32,1024]{2,1,0:T(8,128)(2,1)S(1)}, u32[]{:S(2)}, u32[]{:S(2)}) async-start(bf16[8,32,1024]{2,1,0:T(8,128)(2,1)} %shard_map.119), calls=%async_computation | async-start | bytes 1048576 | tf_op jit(solution)/shard_map/all_to_all | solution.py:353
  10.2 18.2 %collective-permute-start.2 = (bf16[192,256]{1,0:T(8,128)(2,1)}, bf16[192,256]{1,0:T(8,128)(2,1)S(1)}, u32[]{:S(2)}, u32[]{:S(2)}) collective-permute-start(bf16[192,256]{1,0:T(8,128)(2,1)} %bitcast.12), channel_id=1, source_target_pairs={{0,3},{1,0},{2,1},{3,2},{4,7},{5,4},{6,5},{7,6},{8,11},{9,8},{10,9... | collective-permute-start | bytes 294920 | tf_op jit(solution)/shard_map/ppermute | solution.py:328
  13.8 16.0 %collective-permute-start.1 = (bf16[192,256]{1,0:T(8,128)(2,1)}, bf16[192,256]{1,0:T(8,128)(2,1)S(1)}, u32[]{:S(2)}, u32[]{:S(2)}) collective-permute-start(bf16[192,256]{1,0:T(8,128)(2,1)} %bitcast.13), channel_id=1, source_target_pairs={{0,2},{1,3},{2,0},{3,1},{4,6},{5,7},{6,4},{7,5},{8,10},{9,11},{10,... | collective-permute-start | bytes 294920 | tf_op jit(solution)/shard_map/ppermute | solution.py:328
  13.8 16.0 %collective-permute-start = (bf16[192,256]{1,0:T(8,128)(2,1)}, bf16[192,256]{1,0:T(8,128)(2,1)S(1)}, u32[]{:S(2)}, u32[]{:S(2)}) collective-permute-start(bf16[192,256]{1,0:T(8,128)(2,1)} %bitcast.14), channel_id=1, source_target_pairs={{0,1},{1,2},{2,3},{3,0},{4,5},{5,6},{6,7},{7,4},{8,9},{9,10},{10,1... | collective-permute-start | bytes 294920 | tf_op jit(solution)/shard_map/ppermute | solution.py:328
  19.9 1.6 %copy-start = (bf16[896,1152]{1,0:T(8,128)(2,1)S(1)}, bf16[896,1152]{1,0:T(8,128)(2,1)}, u32[]{:S(2)}) copy-start(bf16[896,1152]{1,0:T(8,128)(2,1)} %constant.2.clone.table_ref) | copy-start | bytes 6193156
  22.1 0.7 %copy-start.8 = (s32[8]{0:T(128)S(1)}, s32[8]{0:T(128)}, u32[]{:S(2)}) copy-start(s32[8]{0:T(128)} %order_ref.7) | copy-start | bytes 100
  24.2 5.6 %collective-permute-start.3 = (bf16[48,128]{1,0:T(8,128)(2,1)S(1)}, bf16[48,128]{1,0:T(8,128)(2,1)S(1)}, u32[]{:S(2)}, u32[]{:S(2)}) collective-permute-start(bf16[48,128]{1,0:T(8,128)(2,1)S(1)} %get-tuple-element.27), channel_id=1, source_target_pairs={{0,1},{1,2},{2,3},{3,0},{4,5},{5,6},{6,7},{7,4},{8,9},{9,10},{10,1... | collective-permute-start | bytes 36872 | tf_op jit(solution)/shard_map/ppermute | solution.py:328
  25.8 4.6 %collective-permute-start.4 = (bf16[48,128]{1,0:T(8,128)(2,1)S(1)}, bf16[48,128]{1,0:T(8,128)(2,1)S(1)}, u32[]{:S(2)}, u32[]{:S(2)}) collective-permute-start(bf16[48,128]{1,0:T(8,128)(2,1)S(1)} %get-tuple-element.28), channel_id=1, source_target_pairs={{0,2},{1,3},{2,0},{3,1},{4,6},{5,7},{6,4},{7,5},{8,10},{9,11},{10,... | collective-permute-start | bytes 36872 | tf_op jit(solution)/shard_map/ppermute | solution.py:328
  28.4 3.7 %collective-permute-start.5 = (bf16[48,128]{1,0:T(8,128)(2,1)S(1)}, bf16[48,128]{1,0:T(8,128)(2,1)S(1)}, u32[]{:S(2)}, u32[]{:S(2)}) collective-permute-start(bf16[48,128]{1,0:T(8,128)(2,1)S(1)} %get-tuple-element.29), channel_id=1, source_target_pairs={{0,3},{1,0},{2,1},{3,2},{4,7},{5,4},{6,5},{7,6},{8,11},{9,8},{10,9... | collective-permute-start | bytes 36872 | tf_op jit(solution)/shard_map/ppermute | solution.py:328
  32.1 18.2 %copy-start.6 = (s32[16]{0:T(128)S(1)}, s32[16]{0:T(128)}, u32[]{:S(2)}) copy-start(s32[16]{0:T(128)} %blocks_ref.7) | copy-start | bytes 196
  32.1 18.2 %copy-start.9 = (s32[8]{0:T(128)S(1)}, s32[8]{0:T(128)}, u32[]{:S(2)}) copy-start(s32[8]{0:T(128)} %order_ref.7) | copy-start | bytes 100
  37.1 13.2 %all-to-all-start.1 = ((bf16[8,32,1024]{2,1,0:T(8,128)(2,1)}), bf16[8,32,1024]{2,1,0:T(8,128)(2,1)S(1)}, u32[]{:S(2)}, u32[]{:S(2)}) async-start(bf16[8,32,1024]{2,1,0:T(8,128)(2,1)} %get-tuple-element.35), calls=%async_computation.1 | async-start | bytes 1048576 | tf_op jit(solution)/shard_map/all_to_all | solution.py:377
  41.6 13.8 %collective-permute-start.6 = (bf16[192,256]{1,0:T(8,128)(2,1)S(1)}, bf16[192,256]{1,0:T(8,128)(2,1)S(1)}, u32[]{:S(2)}, u32[]{:S(2)}) collective-permute-start(bf16[192,256]{1,0:T(8,128)(2,1)S(1)} %get-tuple-element.32), channel_id=1, source_target_pairs={{0,1},{1,2},{2,3},{3,0},{4,5},{5,6},{6,7},{7,4},{8,9},{9,10},{10,1... | collective-permute-start | bytes 294920 | tf_op jit(solution)/shard_map/ppermute | solution.py:328
  41.8 13.7 %collective-permute-start.7 = (bf16[192,256]{1,0:T(8,128)(2,1)S(1)}, bf16[192,256]{1,0:T(8,128)(2,1)S(1)}, u32[]{:S(2)}, u32[]{:S(2)}) collective-permute-start(bf16[192,256]{1,0:T(8,128)(2,1)S(1)} %get-tuple-element.33), channel_id=1, source_target_pairs={{0,2},{1,3},{2,0},{3,1},{4,6},{5,7},{6,4},{7,5},{8,10},{9,11},{10,... | collective-permute-start | bytes 294920 | tf_op jit(solution)/shard_map/ppermute | solution.py:328
  45.3 10.2 %collective-permute-start.8 = (bf16[192,256]{1,0:T(8,128)(2,1)S(1)}, bf16[192,256]{1,0:T(8,128)(2,1)S(1)}, u32[]{:S(2)}, u32[]{:S(2)}) collective-permute-start(bf16[192,256]{1,0:T(8,128)(2,1)S(1)} %get-tuple-element.34), channel_id=1, source_target_pairs={{0,3},{1,0},{2,1},{3,2},{4,7},{5,4},{6,5},{7,6},{8,11},{9,8},{10,9... | collective-permute-start | bytes 294920 | tf_op jit(solution)/shard_map/ppermute | solution.py:328
  51.7 5.5 %collective-permute-start.9 = (bf16[48,128]{1,0:T(8,128)(2,1)S(1)}, bf16[48,128]{1,0:T(8,128)(2,1)S(1)}, u32[]{:S(2)}, u32[]{:S(2)}) collective-permute-start(bf16[48,128]{1,0:T(8,128)(2,1)S(1)} %get-tuple-element.37), channel_id=1, source_target_pairs={{0,1},{1,2},{2,3},{3,0},{4,5},{5,6},{6,7},{7,4},{8,9},{9,10},{10,1... | collective-permute-start | bytes 36872 | tf_op jit(solution)/shard_map/ppermute | solution.py:328
  51.9 5.3 %collective-permute-start.10 = (bf16[48,128]{1,0:T(8,128)(2,1)S(1)}, bf16[48,128]{1,0:T(8,128)(2,1)S(1)}, u32[]{:S(2)}, u32[]{:S(2)}) collective-permute-start(bf16[48,128]{1,0:T(8,128)(2,1)S(1)} %get-tuple-element.38), channel_id=1, source_target_pairs={{0,2},{1,3},{2,0},{3,1},{4,6},{5,7},{6,4},{7,5},{8,10},{9,11},{10,... | collective-permute-start | bytes 36872 | tf_op jit(solution)/shard_map/ppermute | solution.py:328
  55.4 3.7 %collective-permute-start.11 = (bf16[48,128]{1,0:T(8,128)(2,1)S(1)}, bf16[48,128]{1,0:T(8,128)(2,1)S(1)}, u32[]{:S(2)}, u32[]{:S(2)}) collective-permute-start(bf16[48,128]{1,0:T(8,128)(2,1)S(1)} %get-tuple-element.39), channel_id=1, source_target_pairs={{0,3},{1,0},{2,1},{3,2},{4,7},{5,4},{6,5},{7,6},{8,11},{9,8},{10,9... | collective-permute-start | bytes 36872 | tf_op jit(solution)/shard_map/ppermute | solution.py:328
  (2 other events, 1.3 us)

commit v2 on v1

v2 whole, which is shorter than its diff:
```python
import functools

import jax
import jax.numpy as jnp
from jax import lax
from jax.experimental import pallas as pl
from jax.experimental.pallas import tpu as pltpu
from jax.sharding import PartitionSpec as P

GROUPS = 16
TAPS = 27
FB = 2
BMAX = 3
LANES = 128
F32 = jnp.float32
BF16 = jnp.bfloat16
HBM = pl.BlockSpec(memory_space=pltpu.HBM)
VMEM = pl.BlockSpec(memory_space=pltpu.VMEM)
MIB = 1024 * 1024
FIRST = 10**6
STAGE = 10**10


def round_up(value, unit):
    return -(-value // unit) * unit


def fold(values, slice_index, och, unit):
    groups = LANES // och
    rows = round_up(-(-values.shape[0] // groups), unit)
    short = rows * groups - values.shape[0]
    if short:
        values = jnp.concatenate([values, jnp.zeros((short, LANES), values.dtype)], axis=0)
    lane_group = lax.broadcasted_iota(jnp.int32, (rows, LANES), 1) // och
    total = jnp.zeros((rows, LANES), F32)
    for g in range(groups):
        shift = (g - slice_index) * och % LANES
        moved = pltpu.roll(values[g * rows : (g + 1) * rows], shift, 1) if shift else values[g * rows : (g + 1) * rows]
        total = total + jnp.where(lane_group == g, moved, 0.0)
    return total


def first_block_of(blocks_ref, first_clip, clips):
    start = jnp.int32(0)
    for k in range(clips):
        start = start + jnp.where(k < first_clip, blocks_ref[k], 0)
    return start


def slot_holders(blocks_ref, order_ref, me, slots, clips, held, devs):
    residue = jnp.int32(0)
    for r in range(devs):
        residue = jnp.where(order_ref[r] == me, r, residue)
    clip_of = [jnp.int32(0)] * slots
    end = jnp.int32(0)
    for k in range(clips):
        end = end + blocks_ref[k]
        for q in range(slots):
            clip_of[q] = clip_of[q] + jnp.where(end <= q * devs + residue, 1, 0)
    return [jnp.minimum(c, clips - 1) // held for c in clip_of]


def split3(values):
    high = values.astype(BF16).astype(F32)
    rest = values - high
    middle = rest.astype(BF16).astype(F32)
    return [high, middle, rest - middle]


def fetch(pairs, sems):
    copies = [pltpu.make_async_copy(a, b, sems.at[i]) for i, (a, b) in enumerate(pairs)]
    for copy in copies:
        copy.start()
    return copies


def send_kernel(
    dims, blocks_hbm, order_hbm, cot_hbm, kernel_hbm, out_ref, shard_ref, blocks_ref, order_ref, cot_ref, sems
):
    devs, slab, slots, clips, held, och = dims
    pairs = [(blocks_hbm, blocks_ref), (order_hbm, order_ref), (cot_hbm, cot_ref), (kernel_hbm, shard_ref)]
    for copy in fetch(pairs, sems):
        copy.wait()
    me = lax.axis_index("clips")
    holders = slot_holders(blocks_ref, order_ref, me, slots, clips, held, devs)
    for q in range(slots):
        block = cot_ref[q].astype(F32)
        for s in range(slab):
            out_ref[holders[q] * slab + s] = fold(block, s, och, 8).astype(BF16)


def make_table(och, out_ref):
    rows = out_ref.shape[0]
    lane = lax.broadcasted_iota(jnp.int32, (8, LANES), 1)
    source = jnp.where(lane < 3 * och, 27 * (lane % och) + 9 * (2 - lane // och), -rows)
    ahead = source - lax.broadcasted_iota(jnp.int32, (8, LANES), 0)
    for group in range(9):
        for i in range(0, rows, 16):
            top = jnp.where(ahead == i - group, 1.0, 0.0)
            bottom = jnp.where(ahead == i + 8 - group, 1.0, 0.0)
            both = jnp.concatenate([top, bottom], axis=0).astype(BF16)
            out_ref[i : i + 16, group * LANES : (group + 1) * LANES] = both


def stage_kernel(slab, *refs):
    video_refs, video_pad = refs[:slab], refs[slab]
    own = lax.axis_index("slab")
    zeros = jnp.zeros(video_pad.shape[1:], BF16)
    video_pad[0] = zeros
    video_pad[slab + 1] = zeros
    for i in range(slab):
        video_pad[jnp.mod(own - i + slab, slab) + 1] = video_refs[i][...]


def forward_kernel(dims, blocks_hbm, *refs):
    devs, slab, clips, held, frames, columns, rows_in, cols, och, per_group = dims
    shard_refs, video_pad = refs[:devs], refs[devs]
    weights_ref, normed_ref, inv_ref, table_ref, shards, blocks_ref, sems = refs[devs + 1 :]
    make_table(och, table_ref)
    copy = fetch([(blocks_hbm, blocks_ref)], sems)[0]
    me = lax.axis_index("clips")
    places = held * frames * columns
    per_clip = frames * columns
    c_in = video_pad.shape[2]
    many = slab * places
    width = table_ref.shape[0]
    chips = devs // 2
    for t in range(chips):
        for e in range(2):
            source = 2 * partner(me // 2, t, chips) + (me % 2 + e) % 2
            shard = shard_refs[t + e * chips][...].astype(F32)
            shards[source] = jnp.concatenate([shard, jnp.zeros((rows_in, width - cols), F32)], axis=1)
    weights = shards[...].reshape(c_in, width).astype(BF16)
    weights_ref[...] = jnp.dot(weights, table_ref[...], preferred_element_type=F32).astype(BF16)

    total = None
    for b in range(3):
        rows = video_pad[b : b + slab].reshape(many, c_in)
        term = jnp.dot(rows, weights_ref[:, 384 * b : 384 * (b + 1)], preferred_element_type=F32)
        total = term if total is None else total + term
    mixed = (
        from_left(total[:, 0:LANES], columns)
        + total[:, LANES : 2 * LANES]
        + from_right(total[:, 2 * LANES :], columns)
    ).reshape(slab, places, LANES)
    frame_shifts = [mixed[:, :, a * och : (a + 1) * och] for a in range(3)]
    frame_of = lax.broadcasted_iota(jnp.int32, (slab, per_clip, och), 1) // columns
    copy.wait()
    for k in range(held):
        blocks = blocks_ref[me * held + k]
        conv = frame_shifts[0][:, k * per_clip : (k + 1) * per_clip]
        for a in (1, 2):
            part = frame_shifts[a][:, k * per_clip : (k + 1) * per_clip - a * columns]
            conv = conv + jnp.concatenate([jnp.zeros((slab, a * columns, och), F32), part], axis=1)
        alive = frame_of < blocks * FB
        count = (blocks * (FB * slab * columns * per_group)).astype(F32)
        kept = jnp.where(alive, conv, 0.0)
        mean = group_mean_of(kept, count, per_group)
        var = group_mean_of(kept * conv, count, per_group) - mean * mean
        inv_std = lax.rsqrt(var + 1e-05)
        normed_ref[:, k * per_clip : (k + 1) * per_clip, :] = (conv - mean) * inv_std
        inv_ref[k] = jnp.broadcast_to(inv_std[0], (8, och))


def from_left(values, columns):
    column = lax.broadcasted_iota(jnp.int32, values.shape, 0) % columns
    return jnp.where(column > 0, pltpu.roll(values, 1, 0), 0.0)


def from_right(values, columns):
    column = lax.broadcasted_iota(jnp.int32, values.shape, 0) % columns
    return jnp.where(column < columns - 1, pltpu.roll(values, values.shape[0] - 1, 0), 0.0)


def group_mean_of(values, count, per_group):
    och = values.shape[-1]
    same = lax.broadcasted_iota(jnp.int32, (och, och), 0) // per_group
    same = (same == lax.broadcasted_iota(jnp.int32, (och, och), 1) // per_group).astype(F32)
    sums = jnp.sum(jnp.sum(values, axis=0), axis=0, keepdims=True)
    sums = jnp.broadcast_to(sums, (8, och))
    sums = jnp.dot(sums, same, precision=lax.Precision.HIGHEST, preferred_element_type=F32)
    return (sums[0:1] / count)[None]


def backward_kernel(dims, blocks_hbm, order_hbm, gain_ref, bias_ref, weights_ref, *refs):
    devs, slab, clips, held, frames, columns, rows_in, cols, och, per_group = dims
    video_pad, normed_ref, inv_ref, cot_ref = refs[:4]
    act_hbm, keep_ref, send_ref = refs[4:7]
    video_grad_refs = refs[7 : 7 + slab]
    table_ref, act_ref, grad_ref, blocks_ref, order_ref, sems = refs[7 + slab :]
    copies = fetch([(blocks_hbm, blocks_ref), (order_hbm, order_ref)], sems)
    make_table(och, table_ref)
    me, own = lax.axis_index("clips"), lax.axis_index("slab")
    places = held * frames * columns
    per_clip = frames * columns
    block_rows = FB * columns
    c_in = video_pad.shape[2]
    groups = LANES // och
    many = slab * places
    shift = jnp.mod(LANES - own * och, LANES)
    gain = pltpu.roll(jnp.broadcast_to(gain_ref[...], (8, LANES)), shift, 1)[0:1, :och]
    bias = pltpu.roll(jnp.broadcast_to(bias_ref[...], (8, LANES)), shift, 1)[0:1, :och]
    frame_of = lax.broadcasted_iota(jnp.int32, (slab, per_clip, och), 1) // columns
    gain_part = jnp.zeros((1, och), F32)
    bias_part = jnp.zeros((1, och), F32)
    for copy in copies:
        copy.wait()
    start = first_block_of(blocks_ref, me * held, clips)
    conv_grads = []
    act_blocks = []
    for k in range(held):
        blocks = blocks_ref[me * held + k]
        cot = []
        for b in range(BMAX):
            device = order_ref[jnp.mod(start + b, devs)]
            rows = []
            for s in range(slab):
                folded = cot_ref[device * slab + s].astype(F32)
                parts = [folded[:, g * och : (g + 1) * och] for g in range(groups)]
                rows.append(jnp.concatenate(parts, axis=0)[:block_rows])
            cot.append(jnp.stack(rows, axis=0))
        cot = jnp.concatenate(cot, axis=1)
        alive = frame_of < blocks * FB
        count = (blocks * (FB * slab * columns * per_group)).astype(F32)
        inv_std = inv_ref[k][None, 0:1]
        normed = normed_ref[:, k * per_clip : (k + 1) * per_clip, :]
        affine = normed * gain[None] + bias[None]
        sigmoid = jax.nn.sigmoid(affine)
        act = affine * sigmoid
        grad_affine = jnp.where(alive, cot * sigmoid * (1.0 + affine * (1.0 - sigmoid)), 0.0)
        gain_part += jnp.sum(jnp.sum(grad_affine * normed, axis=0), axis=0, keepdims=True)
        bias_part += jnp.sum(jnp.sum(grad_affine, axis=0), axis=0, keepdims=True)
        grad_normed = grad_affine * gain[None]
        mean_grad = group_mean_of(grad_normed, count, per_group)
        mean_cross = group_mean_of(grad_normed * normed, count, per_group)
        grad_conv = inv_std * (grad_normed - mean_grad - normed * mean_cross)
        grad_conv = jnp.where(alive, grad_conv, 0.0).astype(BF16).astype(F32)
        lanes = [grad_conv]
        for a in (1, 2):
            zeros = jnp.zeros((slab, a * columns, och), F32)
            lanes.append(jnp.concatenate([grad_conv[:, a * columns :], zeros], axis=1))
        if LANES > 3 * och:
            lanes.append(jnp.zeros((slab, per_clip, LANES - 3 * och), F32))
        conv_grads.append(jnp.concatenate(lanes, axis=2))
        for b in range(BMAX):
            device = order_ref[jnp.mod(start + b, devs)]
            for h in range(slab):
                block = unfolded_to_lanes(act[h, b * block_rows : (b + 1) * block_rows], 8)
                act_blocks.append((b < blocks, device * slab + h, block))
        start = start + blocks

    sums = split3(gain_part) + split3(bias_part) + [jnp.zeros((2, och), F32)]
    sums = jnp.concatenate(sums, axis=0)
    sums = jnp.concatenate([sums, jnp.zeros((8, LANES - och), F32)], axis=1)
    nothing = jnp.concatenate([jnp.zeros_like(act_blocks[0][2]), sums], axis=0).astype(BF16)
    for d in range(devs * slab):
        act_ref[d] = nothing
    for alive, dest, block in act_blocks:

        @pl.when(alive)
        def _(dest=dest, block=block):
            act_ref[dest] = jnp.concatenate([block, sums], axis=0).astype(BF16)

    act_copy = pltpu.make_async_copy(act_ref, act_hbm, sems.at[2])
    act_copy.start()

    grads = jnp.concatenate(conv_grads, axis=1).reshape(many, LANES)
    grad_ref[0] = jnp.zeros((places, 3 * LANES), BF16)
    grad_ref[slab + 1] = jnp.zeros((places, 3 * LANES), BF16)
    for e, shifted in enumerate((from_right(grads, columns), grads, from_left(grads, columns))):
        shifted = shifted.astype(BF16).reshape(slab, places, LANES)
        grad_ref[1 : slab + 1, :, e * LANES : (e + 1) * LANES] = shifted

    for i, ref in enumerate(video_grad_refs):
        row = jnp.mod(own + i, slab)
        total = None
        for b in range(3):
            term = lax.dot_general(
                grad_ref[row + 2 - b],
                weights_ref[:, 384 * b : 384 * (b + 1)],
                (((1,), (1,)), ((), ())),
                preferred_element_type=F32,
            )
            total = term if total is None else total + term
        ref[...] = total.astype(ref.dtype)

    video_t = jnp.transpose(video_pad[1 : slab + 1].reshape(many, c_in))
    parts = []
    for b in range(3):
        moved = grad_ref[2 - b : 2 - b + slab].reshape(many, 3 * LANES)
        parts.append(jnp.dot(video_t, moved, preferred_element_type=F32).astype(BF16))
    native = lax.dot_general(
        jnp.concatenate(parts, axis=1),
        table_ref[...],
        (((1,), (1,)), ((), ())),
        preferred_element_type=F32,
    ).reshape(devs // 2, 2 * rows_in, table_ref.shape[0])
    low, high = native[:, :rows_in, :cols], native[:, rows_in:, :cols]
    odd = me % 2 == 1
    keep_ref[...] = jnp.where(odd, high, low)
    send_ref[...] = jnp.where(odd, low, high).astype(BF16)
    act_copy.wait()


def unfolded_to_lanes(values, unit):
    groups = LANES // values.shape[1]
    rows = round_up(-(-values.shape[0] // groups), unit)
    short = rows * groups - values.shape[0]
    if short:
        values = jnp.concatenate([values, jnp.zeros((short, values.shape[1]), F32)], axis=0)
    return jnp.concatenate([values[g * rows : (g + 1) * rows] for g in range(groups)], axis=1)


def pair_kernel(chips, keep_ref, other_ref, *outs):
    me = lax.axis_index("clips") // 2
    for t, ref in enumerate(outs):
        chip = partner(me, t, chips)
        ref[...] = (keep_ref[chip] + other_ref[chip].astype(F32)).astype(ref.dtype)


def finish_kernel(dims, blocks_hbm, order_hbm, act_in, *refs):
    devs, slab, slots, clips, held, och = dims
    chips = devs // 2
    kernel_refs, grad_refs = refs[:chips], refs[chips : chips + slab]
    kernel_grad_ref, video_grad_ref, act_ref, gain_ref, bias_ref = refs[chips + slab : -3]
    blocks_ref, order_ref, sems = refs[-3:]
    copies = fetch([(blocks_hbm, blocks_ref), (order_hbm, order_ref)], sems)
    total = kernel_refs[0][...]
    for ref in kernel_refs[1:]:
        total = total + ref[...].astype(F32)
    kernel_grad_ref[...] = total
    total = grad_refs[0][...]
    for ref in grad_refs[1:]:
        total = total + ref[...].astype(F32)
    video_grad_ref[...] = total.astype(BF16)
    groups = LANES // och
    rows = act_in.shape[1] - 8
    sums = []
    for s in range(slab):
        part = act_in[s].astype(F32)[rows:]
        for d in range(1, devs):
            part = part + act_in[d * slab + s].astype(F32)[rows:]
        sums.append(part[:, :och])
    sums = jnp.concatenate(sums, axis=1)
    gain_ref[...] = sums[0:1] + (sums[1:2] + sums[2:3])
    bias_ref[...] = sums[3:4] + (sums[4:5] + sums[5:6])
    for copy in copies:
        copy.wait()
    me = lax.axis_index("clips")
    holders = slot_holders(blocks_ref, order_ref, me, slots, clips, held, devs)
    for q in range(slots):
        parts = [act_in[holders[q] * slab + s].astype(F32)[:rows] for s in range(slab)]
        block = []
        for g in range(groups):
            block.append(jnp.concatenate([p[:, g * och : (g + 1) * och] for p in parts], axis=1))
        act_ref[q] = jnp.concatenate(block, axis=0)[: act_ref.shape[1]].astype(BF16)


def call(kernel, outs, specs, scratch=(), limit=4 * MIB, out_specs=None, cost=None):
    return pl.pallas_call(
        kernel,
        out_shape=outs,
        in_specs=specs,
        out_specs=out_specs or [VMEM] * len(outs),
        cost_estimate=cost,
        scratch_shapes=list(scratch),
        compiler_params=pltpu.CompilerParams(vmem_limit_bytes=limit),
    )


def partner(index, step, size):
    return index ^ step if size & (size - 1) == 0 else (index + step) % size


def shifts(arrays, axis):
    size = lax.axis_size(axis)
    moved = [arrays[0]]
    for i in range(1, size):
        moved.append(lax.ppermute(arrays[i], axis, [(j, (j + i) % size) for j in range(size)]))
    return moved


def chip_swaps(arrays, axis):
    size = lax.axis_size(axis)
    moved = [arrays[0]]
    for t in range(1, size // 2):
        pairs = [(j, 2 * partner(j // 2, t, size // 2) + j % 2) for j in range(size)]
        moved.append(lax.ppermute(arrays[t], axis, pairs))
    return moved


def core_swap(array, axis):
    return lax.ppermute(array, axis, [(j, j ^ 1) for j in range(lax.axis_size(axis))])


def body(video, clip_blocks, deal_order, kernel, gain, bias, cotangent):
    devs, slab = lax.axis_size("clips"), lax.axis_size("slab")
    held, frames, _, columns, c_in = video.shape
    slots, clips = cotangent.shape[0], clip_blocks.shape[0]
    c_out = gain.shape[0]
    rows_in, cols = kernel.shape
    och = c_out // slab
    per_group = c_out // GROUPS
    width = round_up(cols, LANES)
    places = held * frames * columns
    block_rows = FB * columns
    fold_rows = round_up(-(-block_rows // (LANES // och)), 8)
    chips = devs // 2
    everyone = ("clips", "slab")
    shape = jax.ShapeDtypeStruct
    smem = [pltpu.SMEM((clips,), jnp.int32), pltpu.SMEM((devs,), jnp.int32)]
    large = (6 + 3 * slab) * MIB
    gain, bias = gain.reshape(1, c_out), bias.reshape(1, c_out)
    clip_blocks = pltpu.with_memory_space_constraint(clip_blocks, pltpu.HBM)
    deal_order = pltpu.with_memory_space_constraint(deal_order, pltpu.HBM)
    kernel = pltpu.with_memory_space_constraint(kernel, pltpu.HBM)
    cotangent_blocks = pltpu.with_memory_space_constraint(
        cotangent.reshape(slots, block_rows, c_out), pltpu.HBM
    )

    videos = shifts([video.reshape(places, c_in)] * slab, "slab")
    cots, shard = call(
        functools.partial(send_kernel, (devs, slab, slots, clips, held, och)),
        [shape((devs * slab, fold_rows, LANES), BF16), shape((rows_in, cols), BF16)],
        [HBM, HBM, HBM, HBM],
        smem + [pltpu.VMEM((slots, block_rows, c_out), BF16), pltpu.SemaphoreType.DMA((4,))],
        cost=pl.CostEstimate(flops=FIRST, bytes_accessed=0, transcendentals=0),
    )(clip_blocks, deal_order, cotangent_blocks, kernel)
    cots = lax.all_to_all(cots, everyone, split_axis=0, concat_axis=0, tiled=True)
    shards = chip_swaps([shard] * chips, "clips")
    shards = shards + [core_swap(shard, "clips") for shard in shards]

    dims = (devs, slab, clips, held, frames, columns, rows_in, cols, och, per_group)
    video_pad = call(
        functools.partial(stage_kernel, slab),
        [shape((slab + 2, places, c_in), BF16)],
        [VMEM] * slab,
        cost=pl.CostEstimate(flops=STAGE, bytes_accessed=0, transcendentals=0),
    )(*videos)[0]
    weights, normed, inv_std = call(
        functools.partial(forward_kernel, dims),
        [
            shape((c_in, 9 * LANES), BF16),
            shape((slab, places, och), F32),
            shape((held, 8, och), F32),
        ],
        [HBM] + [VMEM] * (devs + 1),
        [
            pltpu.VMEM((width, 9 * LANES), BF16),
            pltpu.VMEM((devs, rows_in, width), F32),
            smem[0],
            pltpu.SemaphoreType.DMA((1,)),
        ],
        large,
    )(clip_blocks, *shards, video_pad)
    acts, keep, send, *video_grads = call(
        functools.partial(backward_kernel, dims),
        [
            pltpu.HBM((devs * slab, fold_rows + 8, LANES), BF16),
            shape((chips, rows_in, cols), F32),
            shape((chips, rows_in, cols), BF16),
        ]
        + [shape((places, c_in), F32 if i == 0 else BF16) for i in range(slab)],
        [HBM, HBM] + [VMEM] * 7,
        [
            pltpu.VMEM((width, 9 * LANES), BF16),
            pltpu.VMEM((devs * slab, fold_rows + 8, LANES), BF16),
            pltpu.VMEM((slab + 2, places, 3 * LANES), BF16),
        ]
        + smem
        + [pltpu.SemaphoreType.DMA((3,))],
        large,
        [HBM] + [VMEM] * (2 + slab),
    )(clip_blocks, deal_order, gain, bias, weights, video_pad, normed, inv_std, cots)
    video_grads = shifts(video_grads, "slab")
    send = core_swap(send, "clips")
    acts = lax.all_to_all(acts, everyone, split_axis=0, concat_axis=0, tiled=True)
    kernel_grads = call(
        functools.partial(pair_kernel, chips),
        [shape((rows_in, cols), F32 if t == 0 else BF16) for t in range(chips)],
        [VMEM, VMEM],
    )(keep, send)
    kernel_grads = chip_swaps(kernel_grads, "clips")

    kernel_grad, video_grad, act, gain_grad, bias_grad = call(
        functools.partial(finish_kernel, (devs, slab, slots, clips, held, och)),
        [
            shape((rows_in, cols), F32),
            shape((places, c_in), BF16),
            shape((slots, block_rows, c_out), BF16),
            shape((1, c_out), F32),
            shape((1, c_out), F32),
        ],
        [HBM, HBM] + [VMEM] * (1 + chips + slab),
        smem + [pltpu.SemaphoreType.DMA((2,))],
    )(clip_blocks, deal_order, acts, *kernel_grads, *video_grads)
    return (
        act.reshape(cotangent.shape),
        video_grad.reshape(video.shape),
        kernel_grad,
        gain_grad.reshape(c_out),
        bias_grad.reshape(c_out),
    )


def solution(mesh):
    return jax.shard_map(
        body,
        mesh=mesh,
        in_specs=(
            P("clips", None, "slab", None, None),
            P(),
            P(),
            P("clips", "slab"),
            P(),
            P(),
            P("clips", None, "slab", None, None),
        ),
        out_specs=(
            P("clips", None, "slab", None, None),
            P("clips", None, "slab", None, None),
            P("clips", "slab"),
            P(),
            P(),
        ),
        check_vma=False,
    )
```

time: 60.4 us -> 49.1 us (0.81)
  waiting for transfers between devices: 15.8 us -> 7.29 us
  local copies, waits for them, and re-layouts: 5.79 us -> 0.68 us
  starting transfers between devices: 26.6 us -> 30 us
  Pallas kernels: 11 us -> 9.95 us
    ppermute x0 -> x11, starting transfers between devices: none -> 11.3 us  [the longest x6 10.4 us: chip_swaps(): moved.append(lax.ppermute(arrays[t], axis, pairs))]
    all_to_all x2, waiting for transfers between devices: 9.92 us -> 2.2 us  [the longest x1 2.2 us: body(): lax.all_to_all(cots, everyone, split_axis=0, concat_axis=0, tiled=True)]
    ppermute x12 -> x6, starting transfers between devices: 17.9 us -> 10.3 us  [shifts(): lax.ppermute(arrays[i], axis, [(j, (j + i) % size) for j in range(size)])]
    unnamed x24 -> x6, local copies, waits for them, and re-layouts: 5.79 us -> 0.68 us
    ppermute x12 -> x6, waiting for transfers between devices: 5.92 us -> 2.68 us  [shifts(): lax.ppermute(arrays[i], axis, [(j, (j + i) % size) for j in range(size)])]
    ppermute x0 -> x11, waiting for transfers between devices: none -> 2.4 us  [the longest x6 1.23 us: chip_swaps(): moved.append(lax.ppermute(arrays[t], axis, pairs))]
    pallas_call x6, Pallas kernels: 11 us -> 9.95 us  [the longest x1 4.1 us: body(): call(functools.partial(backward_kernel, dims), [pltpu.HBM((devs * slab, f...]
  transfers between devices with their start and end apart: 14 -> 19, of which waited for: 6 -> 8; matrix products, arithmetic and copies ran while one was open for 0% -> 0% of each run, Pallas kernels for 6% -> 6%
where the time goes in v2:
time: 49.1 us; the launch traced here: 48.6 us
  starting transfers between devices  30 us (61%)
  Pallas kernels  9.95 us (20%)
  waiting for transfers between devices  7.29 us (15%)
  between operations  0.75 us (2%)
  local copies, waits for them, and re-layouts  0.68 us (1%)
    ppermute x6, starting transfers between devices, chip_swaps(): moved.append(lax.ppermute(arrays[t], axis, pairs))  10.4 us
    ppermute x6, starting transfers between devices, shifts(): lax.ppermute(arrays[i], axis, [(j, (j + i) % size) for j in range(size)])  10.3 us
    all_to_all x1, starting transfers between devices, body(): lax.all_to_all(cots, everyone, split_axis=0, concat_axis=0, tiled=True)  5.06 us
    pallas_call x1, Pallas kernels, body(): call(functools.partial(backward_kernel, dims), [pltpu.HBM((devs * slab, f...  4.1 us
    all_to_all x1, starting transfers between devices, body(): lax.all_to_all(acts, everyone, split_axis=0, concat_axis=0, tiled=True)  3.31 us
    ppermute x6, waiting for transfers between devices, shifts(): lax.ppermute(arrays[i], axis, [(j, (j + i) % size) for j in range(size)])  2.68 us
    pallas_call x1, Pallas kernels, body(): call(functools.partial(forward_kernel, dims), [shape((c_in, 9 * LANES), B...  2.62 us
    all_to_all x1, waiting for transfers between devices, body(): lax.all_to_all(cots, everyone, split_axis=0, concat_axis=0, tiled=True)  2.2 us
  transfers between devices with their start and end apart: 19, of which 8 were waited for; matrix products, arithmetic and copies ran while one was open for 0% of the time, Pallas kernels for 6%

profile of v2, /device:TPU:0, one launch (start us, length us, event | category | flops | bytes accessed | tf_op | source)
XLA Modules:
  0.0 48.6 jit_solution(11638718451666873209)
XLA Ops:
  0.6 1.6 %shard_map.110 = (bf16[32,8,128]{2,1,0:T(8,128)(2,1)}, bf16[32,864]{1,0:T(8,128)(2,1)S(1)}) custom-call(s32[16]{0:T(128)} %blocks_hbm.7, s32[8]{0:T(128)} %order_hbm.5, bf16[4,32,128]{2,1,0:T(8,128)(2,1)} %bitcast.18, bf16[32,864]{1,0:T(8,128)(2,1)} %kernel_hbm.1), custom_call_target="tpu_custom_call" | custom-call | flops 1000000 | tf_op jit(solution)/shard_map/pallas_call | solution.py:422
  2.3 4.0 %collective-permute-start.2 = (bf16[32,864]{1,0:T(8,128)(2,1)S(1)}, bf16[32,864]{1,0:T(8,128)(2,1)S(1)}, u32[]{:S(2)}, u32[]{:S(2)}) collective-permute-start(bf16[32,864]{1,0:T(8,128)(2,1)S(1)} %get-tuple-element.26.refs_0_), channel_id=1, source_target_pairs={{0,24},{4,28},{8,16},{12,20},{16,8},{20,12},{24,0},{28,4},{1,25},{... | collective-permute-start | bytes 165896 | tf_op jit(solution)/shard_map/ppermute | solution.py:388
  6.3 3.6 %collective-permute-start.9 = (bf16[192,256]{1,0:T(8,128)(2,1)}, bf16[192,256]{1,0:T(8,128)(2,1)S(1)}, u32[]{:S(2)}, u32[]{:S(2)}) collective-permute-start(bf16[192,256]{1,0:T(8,128)(2,1)} %bitcast.14), channel_id=1, source_target_pairs={{0,3},{1,0},{2,1},{3,2},{4,7},{5,4},{6,5},{7,6},{8,11},{9,8},{10,9... | collective-permute-start | bytes 294920 | tf_op jit(solution)/shard_map/ppermute | solution.py:379
  9.9 1.0 %collective-permute-start.7 = (bf16[192,256]{1,0:T(8,128)(2,1)}, bf16[192,256]{1,0:T(8,128)(2,1)S(1)}, u32[]{:S(2)}, u32[]{:S(2)}) collective-permute-start(bf16[192,256]{1,0:T(8,128)(2,1)} %bitcast.16), channel_id=1, source_target_pairs={{0,1},{1,2},{2,3},{3,0},{4,5},{5,6},{6,7},{7,4},{8,9},{9,10},{10,1... | collective-permute-start | bytes 294920 | tf_op jit(solution)/shard_map/ppermute | solution.py:379
  10.9 0.5 %collective-permute-start.1 = (bf16[32,864]{1,0:T(8,128)(2,1)S(1)}, bf16[32,864]{1,0:T(8,128)(2,1)S(1)}, u32[]{:S(2)}, u32[]{:S(2)}) collective-permute-start(bf16[32,864]{1,0:T(8,128)(2,1)S(1)} %get-tuple-element.26.refs_0_), channel_id=1, source_target_pairs={{0,16},{4,20},{8,24},{12,28},{16,0},{20,4},{24,8},{28,12},{1,17},{... | collective-permute-start | bytes 165896 | tf_op jit(solution)/shard_map/ppermute | solution.py:388
  11.4 0.5 %collective-permute-start = (bf16[32,864]{1,0:T(8,128)(2,1)S(1)}, bf16[32,864]{1,0:T(8,128)(2,1)S(1)}, u32[]{:S(2)}, u32[]{:S(2)}) collective-permute-start(bf16[32,864]{1,0:T(8,128)(2,1)S(1)} %get-tuple-element.26.refs_0_), channel_id=1, source_target_pairs={{0,8},{4,12},{8,0},{12,4},{16,24},{20,28},{24,16},{28,20},{1,9},{5... | collective-permute-start | bytes 165896 | tf_op jit(solution)/shard_map/ppermute | solution.py:388
  11.9 5.1 %all-to-all-start = ((bf16[32,8,128]{2,1,0:T(8,128)(2,1)}), bf16[32,8,128]{2,1,0:T(8,128)(2,1)S(1)}, u32[]{:S(2)}, u32[]{:S(2)}) async-start(bf16[32,8,128]{2,1,0:T(8,128)(2,1)} %get-tuple-element.30), calls=%async_computation | async-start | bytes 131072 | tf_op jit(solution)/shard_map/all_to_all | solution.py:429
  17.8 0.6 %collective-permute-done.8.refs_2_ = bf16[192,256]{1,0:T(8,128)(2,1)S(1)} collective-permute-done((bf16[192,256]{1,0:T(8,128)(2,1)}, bf16[192,256]{1,0:T(8,128)(2,1)S(1)}, u32[]{:S(2)}, u32[]{:S(2)}) %collective-permute-start.8) | collective-permute-done | bytes 98336 | tf_op jit(solution)/shard_map/ppermute | solution.py:379
  18.8 0.8 %collective-permute-done.4.refs_5_ = bf16[32,864]{1,0:T(8,128)(2,1)S(1)} collective-permute-done((bf16[32,864]{1,0:T(8,128)(2,1)S(1)}, bf16[32,864]{1,0:T(8,128)(2,1)S(1)}, u32[]{:S(2)}, u32[]{:S(2)}) %collective-permute-start.4) | collective-permute-done | bytes 55328 | tf_op jit(solution)/shard_map/ppermute | solution.py:393
  19.7 2.6 %shard_map.112 = (bf16[256,1152]{1,0:T(8,128)(2,1)S(1)}, f32[4,192,32]{2,1,0:T(8,128)S(1)}, f32[2,8,32]{2,1,0:T(8,128)S(1)}) custom-call(s32[16]{0:T(128)} %blocks_hbm.7, bf16[32,864]{1,0:T(8,128)(2,1)S(1)} %get-tuple-element.26.refs_0_, bf16[32,864]{1,0:T(8,128)(2,1)S(1)} %collective-permute-done.refs_1_, ...), custom_call_target="tpu_custom_call" | custom-call | tf_op jit(solution)/shard_map/pallas_call | solution.py:440
  22.3 2.2 %all-to-all-done.refs_3_ = bf16[32,8,128]{2,1,0:T(8,128)(2,1)S(1)} async-done(((bf16[32,8,128]{2,1,0:T(8,128)(2,1)}), bf16[32,8,128]{2,1,0:T(8,128)(2,1)S(1)}, u32[]{:S(2)}, u32[]{:S(2)}) %all-to-all-start) | async-done | bytes 65568 | tf_op jit(solution)/shard_map/all_to_all | solution.py:429
  24.5 0.7 %copy-done = f32[128]{0:T(128)S(1)} copy-done((f32[128]{0:T(128)S(1)}, f32[128]{0:T(128)}, u32[]{:S(2)}) %copy-start) | copy-done | bytes 536
  25.2 4.1 %shard_map.113 = (bf16[32,16,128]{2,1,0:T(8,128)(2,1)}, f32[4,32,864]{2,1,0:T(8,128)S(1)}, bf16[4,32,864]{2,1,0:T(8,128)(2,1)S(1)}, f32[192,256]{1,0:T(8,128)S(1...) custom-call(s32[16]{0:T(128)} %blocks_hbm.7, s32[8]{0:T(128)} %order_hbm.5, ...), custom_call_target="tpu_custom_call" | custom-call | tf_op jit(solution)/shard_map/pallas_call | solution.py:456
  29.3 3.3 %all-to-all-start.1 = ((bf16[32,16,128]{2,1,0:T(8,128)(2,1)}), bf16[32,16,128]{2,1,0:T(8,128)(2,1)S(1)}, u32[]{:S(2)}, u32[]{:S(2)}) async-start(bf16[32,16,128]{2,1,0:T(8,128)(2,1)} %get-tuple-element.31), calls=%async_computation.1 | async-start | bytes 262144 | tf_op jit(solution)/shard_map/all_to_all | solution.py:477
  32.7 1.8 %collective-permute-start.14 = (bf16[192,256]{1,0:T(8,128)(2,1)S(1)}, bf16[192,256]{1,0:T(8,128)(2,1)S(1)}, u32[]{:S(2)}, u32[]{:S(2)}) collective-permute-start(bf16[192,256]{1,0:T(8,128)(2,1)S(1)} %get-tuple-element.39), channel_id=1, source_target_pairs={{0,1},{1,2},{2,3},{3,0},{4,5},{5,6},{6,7},{7,4},{8,9},{9,10},{10,1... | collective-permute-start | bytes 294920 | tf_op jit(solution)/shard_map/ppermute | solution.py:379
  34.5 2.4 %collective-permute-start.15 = (bf16[192,256]{1,0:T(8,128)(2,1)S(1)}, bf16[192,256]{1,0:T(8,128)(2,1)S(1)}, u32[]{:S(2)}, u32[]{:S(2)}) collective-permute-start(bf16[192,256]{1,0:T(8,128)(2,1)S(1)} %get-tuple-element.40), channel_id=1, source_target_pairs={{0,2},{1,3},{2,0},{3,1},{4,6},{5,7},{6,4},{7,5},{8,10},{9,11},{10,... | collective-permute-start | bytes 294920 | tf_op jit(solution)/shard_map/ppermute | solution.py:379
  36.9 1.4 %collective-permute-start.16 = (bf16[192,256]{1,0:T(8,128)(2,1)S(1)}, bf16[192,256]{1,0:T(8,128)(2,1)S(1)}, u32[]{:S(2)}, u32[]{:S(2)}) collective-permute-start(bf16[192,256]{1,0:T(8,128)(2,1)S(1)} %get-tuple-element.41), channel_id=1, source_target_pairs={{0,3},{1,0},{2,1},{3,2},{4,7},{5,4},{6,5},{7,6},{8,11},{9,8},{10,9... | collective-permute-start | bytes 294920 | tf_op jit(solution)/shard_map/ppermute | solution.py:379
  38.4 1.5 %collective-permute-start.11 = (bf16[32,864]{1,0:T(8,128)(2,1)S(1)}, bf16[32,864]{1,0:T(8,128)(2,1)S(1)}, u32[]{:S(2)}, u32[]{:S(2)}) collective-permute-start(bf16[32,864]{1,0:T(8,128)(2,1)S(1)} %get-tuple-element.35), channel_id=1, source_target_pairs={{0,8},{4,12},{8,0},{12,4},{16,24},{20,28},{24,16},{28,20},{1,9},{5... | collective-permute-start | bytes 165896 | tf_op jit(solution)/shard_map/ppermute | solution.py:388
  39.9 1.5 %collective-permute-start.12 = (bf16[32,864]{1,0:T(8,128)(2,1)S(1)}, bf16[32,864]{1,0:T(8,128)(2,1)S(1)}, u32[]{:S(2)}, u32[]{:S(2)}) collective-permute-start(bf16[32,864]{1,0:T(8,128)(2,1)S(1)} %get-tuple-element.36), channel_id=1, source_target_pairs={{0,16},{4,20},{8,24},{12,28},{16,0},{20,4},{24,8},{28,12},{1,17},{... | collective-permute-start | bytes 165896 | tf_op jit(solution)/shard_map/ppermute | solution.py:388
  41.4 0.7 %collective-permute-done.14.refs_5_ = bf16[192,256]{1,0:T(8,128)(2,1)S(1)} collective-permute-done((bf16[192,256]{1,0:T(8,128)(2,1)S(1)}, bf16[192,256]{1,0:T(8,128)(2,1)S(1)}, u32[]{:S(2)}, u32[]{:S(2)}) %collective-permute-start.14) | collective-permute-done | bytes 98336 | tf_op jit(solution)/shard_map/ppermute | solution.py:379
  42.1 2.4 %collective-permute-start.13 = (bf16[32,864]{1,0:T(8,128)(2,1)S(1)}, bf16[32,864]{1,0:T(8,128)(2,1)S(1)}, u32[]{:S(2)}, u32[]{:S(2)}) collective-permute-start(bf16[32,864]{1,0:T(8,128)(2,1)S(1)} %get-tuple-element.37), channel_id=1, source_target_pairs={{0,24},{4,28},{8,16},{12,20},{16,8},{20,12},{24,0},{28,4},{1,25},{... | collective-permute-start | bytes 165896 | tf_op jit(solution)/shard_map/ppermute | solution.py:388
  44.5 1.4 %collective-permute-done.15.refs_6_ = bf16[192,256]{1,0:T(8,128)(2,1)S(1)} collective-permute-done((bf16[192,256]{1,0:T(8,128)(2,1)S(1)}, bf16[192,256]{1,0:T(8,128)(2,1)S(1)}, u32[]{:S(2)}, u32[]{:S(2)}) %collective-permute-start.15) | collective-permute-done | bytes 98336 | tf_op jit(solution)/shard_map/ppermute | solution.py:379
  45.9 1.2 %collective-permute-done.13.refs_3_ = bf16[32,864]{1,0:T(8,128)(2,1)S(1)} collective-permute-done((bf16[32,864]{1,0:T(8,128)(2,1)S(1)}, bf16[32,864]{1,0:T(8,128)(2,1)S(1)}, u32[]{:S(2)}, u32[]{:S(2)}) %collective-permute-start.13) | collective-permute-done | bytes 55328 | tf_op jit(solution)/shard_map/ppermute | solution.py:388
  47.1 1.5 %shard_map.115 = (f32[32,864]{1,0:T(8,128)}, bf16[192,256]{1,0:T(8,128)(2,1)}, bf16[4,32,128]{2,1,0:T(8,128)(2,1)}, f32[1,128]{1,0:T(1,128)}, f32[1,128]{1,0:T(1,128)}) custom-call(s32[16]{0:T(128)} %blocks_hbm.7, s32[8]{0:T(128)} %order_hbm.5, bf16[32,16,128]{2,1,0:T(8,128)(2,1)S(1)} %all-to-all-done.1.act_in, f32[32,864]{1,0:T(8,128)S(1)} %get-tuple-element.34.refs_0_, ...), custom_call_target="tpu_custom_call" | custom-call | tf_op jit(solution)/shard_map/pallas_call | solution.py:485
  (26 shorter events, 1.4 us)
Async XLA Ops:
  0.6 17.8 %copy-start.2 = (bf16[2,6,1,16,256]{4,3,2,1,0:T(8,128)(2,1)S(1)}, bf16[2,6,1,16,256]{4,3,2,1,0:T(8,128)(2,1)}, u32[]{:S(2)}) copy-start(bf16[2,6,1,16,256]{4,3,2,1,0:T(8,128)(2,1)} %param.7) | copy-start | bytes 294916
  2.3 9.1 %collective-permute-start.2 = (bf16[32,864]{1,0:T(8,128)(2,1)S(1)}, bf16[32,864]{1,0:T(8,128)(2,1)S(1)}, u32[]{:S(2)}, u32[]{:S(2)}) collective-permute-start(bf16[32,864]{1,0:T(8,128)(2,1)S(1)} %get-tuple-element.26.refs_0_), channel_id=1, source_target_pairs={{0,24},{4,28},{8,16},{12,20},{16,8},{20,12},{24,0},{28,4},{1,25},{... | collective-permute-start | bytes 165896 | tf_op jit(solution)/shard_map/ppermute | solution.py:388
  6.3 11.3 %collective-permute-start.9 = (bf16[192,256]{1,0:T(8,128)(2,1)}, bf16[192,256]{1,0:T(8,128)(2,1)S(1)}, u32[]{:S(2)}, u32[]{:S(2)}) collective-permute-start(bf16[192,256]{1,0:T(8,128)(2,1)} %bitcast.14), channel_id=1, source_target_pairs={{0,3},{1,0},{2,1},{3,2},{4,7},{5,4},{6,5},{7,6},{8,11},{9,8},{10,9... | collective-permute-start | bytes 294920 | tf_op jit(solution)/shard_map/ppermute | solution.py:379
  9.9 8.6 %collective-permute-start.8 = (bf16[192,256]{1,0:T(8,128)(2,1)}, bf16[192,256]{1,0:T(8,128)(2,1)S(1)}, u32[]{:S(2)}, u32[]{:S(2)}) collective-permute-start(bf16[192,256]{1,0:T(8,128)(2,1)} %bitcast.15), channel_id=1, source_target_pairs={{0,2},{1,3},{2,0},{3,1},{4,6},{5,7},{6,4},{7,5},{8,10},{9,11},{10,... | collective-permute-start | bytes 294920 | tf_op jit(solution)/shard_map/ppermute | solution.py:379
  9.9 8.6 %collective-permute-start.7 = (bf16[192,256]{1,0:T(8,128)(2,1)}, bf16[192,256]{1,0:T(8,128)(2,1)S(1)}, u32[]{:S(2)}, u32[]{:S(2)}) collective-permute-start(bf16[192,256]{1,0:T(8,128)(2,1)} %bitcast.16), channel_id=1, source_target_pairs={{0,1},{1,2},{2,3},{3,0},{4,5},{5,6},{6,7},{7,4},{8,9},{9,10},{10,1... | collective-permute-start | bytes 294920 | tf_op jit(solution)/shard_map/ppermute | solution.py:379
  10.9 6.1 %collective-permute-start.1 = (bf16[32,864]{1,0:T(8,128)(2,1)S(1)}, bf16[32,864]{1,0:T(8,128)(2,1)S(1)}, u32[]{:S(2)}, u32[]{:S(2)}) collective-permute-start(bf16[32,864]{1,0:T(8,128)(2,1)S(1)} %get-tuple-element.26.refs_0_), channel_id=1, source_target_pairs={{0,16},{4,20},{8,24},{12,28},{16,0},{20,4},{24,8},{28,12},{1,17},{... | collective-permute-start | bytes 165896 | tf_op jit(solution)/shard_map/ppermute | solution.py:388
  11.4 5.9 %collective-permute-start = (bf16[32,864]{1,0:T(8,128)(2,1)S(1)}, bf16[32,864]{1,0:T(8,128)(2,1)S(1)}, u32[]{:S(2)}, u32[]{:S(2)}) collective-permute-start(bf16[32,864]{1,0:T(8,128)(2,1)S(1)} %get-tuple-element.26.refs_0_), channel_id=1, source_target_pairs={{0,8},{4,12},{8,0},{12,4},{16,24},{20,28},{24,16},{28,20},{1,9},{5... | collective-permute-start | bytes 165896 | tf_op jit(solution)/shard_map/ppermute | solution.py:388
  11.9 12.6 %all-to-all-start = ((bf16[32,8,128]{2,1,0:T(8,128)(2,1)}), bf16[32,8,128]{2,1,0:T(8,128)(2,1)S(1)}, u32[]{:S(2)}, u32[]{:S(2)}) async-start(bf16[32,8,128]{2,1,0:T(8,128)(2,1)} %get-tuple-element.30), calls=%async_computation | async-start | bytes 131072 | tf_op jit(solution)/shard_map/all_to_all | solution.py:429
  17.0 1.5 %collective-permute-start.3 = (bf16[32,864]{1,0:T(8,128)(2,1)S(1)}, bf16[32,864]{1,0:T(8,128)(2,1)S(1)}, u32[]{:S(2)}, u32[]{:S(2)}) collective-permute-start(bf16[32,864]{1,0:T(8,128)(2,1)S(1)} %get-tuple-element.26.refs_0_), channel_id=1, source_target_pairs={{0,4},{4,0},{8,12},{12,8},{16,20},{20,16},{24,28},{28,24},{1,5},{5... | collective-permute-start | bytes 165896 | tf_op jit(solution)/shard_map/ppermute | solution.py:393
  17.3 1.2 %collective-permute-start.6 = (bf16[32,864]{1,0:T(8,128)(2,1)S(1)}, bf16[32,864]{1,0:T(8,128)(2,1)S(1)}, u32[]{:S(2)}, u32[]{:S(2)}) collective-permute-start(bf16[32,864]{1,0:T(8,128)(2,1)S(1)} %collective-permute-done.2.refs_3_), channel_id=1, source_target_pairs={{0,4},{4,0},{8,12},{12,8},{16,20},{20,16},{24,28},{28,24},{1,5},{5... | collective-permute-start | bytes 165896 | tf_op jit(solution)/shard_map/ppermute | solution.py:393
  17.6 1.2 %collective-permute-start.5 = (bf16[32,864]{1,0:T(8,128)(2,1)S(1)}, bf16[32,864]{1,0:T(8,128)(2,1)S(1)}, u32[]{:S(2)}, u32[]{:S(2)}) collective-permute-start(bf16[32,864]{1,0:T(8,128)(2,1)S(1)} %collective-permute-done.1.refs_2_), channel_id=1, source_target_pairs={{0,4},{4,0},{8,12},{12,8},{16,20},{20,16},{24,28},{28,24},{1,5},{5... | collective-permute-start | bytes 165896 | tf_op jit(solution)/shard_map/ppermute | solution.py:393
  18.4 1.2 %collective-permute-start.4 = (bf16[32,864]{1,0:T(8,128)(2,1)S(1)}, bf16[32,864]{1,0:T(8,128)(2,1)S(1)}, u32[]{:S(2)}, u32[]{:S(2)}) collective-permute-start(bf16[32,864]{1,0:T(8,128)(2,1)S(1)} %collective-permute-done.refs_1_), channel_id=1, source_target_pairs={{0,4},{4,0},{8,12},{12,8},{16,20},{20,16},{24,28},{28,24},{1,5},{5... | collective-permute-start | bytes 165896 | tf_op jit(solution)/shard_map/ppermute | solution.py:393
  24.5 0.7 %copy-start = (f32[128]{0:T(128)S(1)}, f32[128]{0:T(128)}, u32[]{:S(2)}) copy-start(f32[128]{0:T(128)} %param.11) | copy-start | bytes 1540
  24.5 0.7 %copy-start.1 = (f32[128]{0:T(128)S(1)}, f32[128]{0:T(128)}, u32[]{:S(2)}) copy-start(f32[128]{0:T(128)} %param.12) | copy-start | bytes 1540
  29.3 9.1 %collective-permute-start.10 = (bf16[4,32,864]{2,1,0:T(8,128)(2,1)S(1)}, bf16[4,32,864]{2,1,0:T(8,128)(2,1)S(1)}, u32[]{:S(2)}, u32[]{:S(2)}) collective-permute-start(bf16[4,32,864]{2,1,0:T(8,128)(2,1)S(1)} %get-tuple-element.33), channel_id=1, source_target_pairs={{0,4},{4,0},{8,12},{12,8},{16,20},{20,16},{24,28},{28,24},{1,5},{5... | collective-permute-start | bytes 663560 | tf_op jit(solution)/shard_map/ppermute | solution.py:393
  29.3 16.6 %all-to-all-start.1 = ((bf16[32,16,128]{2,1,0:T(8,128)(2,1)}), bf16[32,16,128]{2,1,0:T(8,128)(2,1)S(1)}, u32[]{:S(2)}, u32[]{:S(2)}) async-start(bf16[32,16,128]{2,1,0:T(8,128)(2,1)} %get-tuple-element.31), calls=%async_computation.1 | async-start | bytes 262144 | tf_op jit(solution)/shard_map/all_to_all | solution.py:477
  32.7 9.4 %collective-permute-start.14 = (bf16[192,256]{1,0:T(8,128)(2,1)S(1)}, bf16[192,256]{1,0:T(8,128)(2,1)S(1)}, u32[]{:S(2)}, u32[]{:S(2)}) collective-permute-start(bf16[192,256]{1,0:T(8,128)(2,1)S(1)} %get-tuple-element.39), channel_id=1, source_target_pairs={{0,1},{1,2},{2,3},{3,0},{4,5},{5,6},{6,7},{7,4},{8,9},{9,10},{10,1... | collective-permute-start | bytes 294920 | tf_op jit(solution)/shard_map/ppermute | solution.py:379
  34.5 11.4 %collective-permute-start.15 = (bf16[192,256]{1,0:T(8,128)(2,1)S(1)}, bf16[192,256]{1,0:T(8,128)(2,1)S(1)}, u32[]{:S(2)}, u32[]{:S(2)}) collective-permute-start(bf16[192,256]{1,0:T(8,128)(2,1)S(1)} %get-tuple-element.40), channel_id=1, source_target_pairs={{0,2},{1,3},{2,0},{3,1},{4,6},{5,7},{6,4},{7,5},{8,10},{9,11},{10,... | collective-permute-start | bytes 294920 | tf_op jit(solution)/shard_map/ppermute | solution.py:379
  36.9 9.0 %collective-permute-start.16 = (bf16[192,256]{1,0:T(8,128)(2,1)S(1)}, bf16[192,256]{1,0:T(8,128)(2,1)S(1)}, u32[]{:S(2)}, u32[]{:S(2)}) collective-permute-start(bf16[192,256]{1,0:T(8,128)(2,1)S(1)} %get-tuple-element.41), channel_id=1, source_target_pairs={{0,3},{1,0},{2,1},{3,2},{4,7},{5,4},{6,5},{7,6},{8,11},{9,8},{10,9... | collective-permute-start | bytes 294920 | tf_op jit(solution)/shard_map/ppermute | solution.py:379
  38.4 7.5 %collective-permute-start.11 = (bf16[32,864]{1,0:T(8,128)(2,1)S(1)}, bf16[32,864]{1,0:T(8,128)(2,1)S(1)}, u32[]{:S(2)}, u32[]{:S(2)}) collective-permute-start(bf16[32,864]{1,0:T(8,128)(2,1)S(1)} %get-tuple-element.35), channel_id=1, source_target_pairs={{0,8},{4,12},{8,0},{12,4},{16,24},{20,28},{24,16},{28,20},{1,9},{5... | collective-permute-start | bytes 165896 | tf_op jit(solution)/shard_map/ppermute | solution.py:388
  39.9 6.0 %collective-permute-start.12 = (bf16[32,864]{1,0:T(8,128)(2,1)S(1)}, bf16[32,864]{1,0:T(8,128)(2,1)S(1)}, u32[]{:S(2)}, u32[]{:S(2)}) collective-permute-start(bf16[32,864]{1,0:T(8,128)(2,1)S(1)} %get-tuple-element.36), channel_id=1, source_target_pairs={{0,16},{4,20},{8,24},{12,28},{16,0},{20,4},{24,8},{28,12},{1,17},{... | collective-permute-start | bytes 165896 | tf_op jit(solution)/shard_map/ppermute | solution.py:388
  42.1 5.1 %collective-permute-start.13 = (bf16[32,864]{1,0:T(8,128)(2,1)S(1)}, bf16[32,864]{1,0:T(8,128)(2,1)S(1)}, u32[]{:S(2)}, u32[]{:S(2)}) collective-permute-start(bf16[32,864]{1,0:T(8,128)(2,1)S(1)} %get-tuple-element.37), channel_id=1, source_target_pairs={{0,24},{4,28},{8,16},{12,20},{16,8},{20,12},{24,0},{28,4},{1,25},{... | collective-permute-start | bytes 165896 | tf_op jit(solution)/shard_map/ppermute | solution.py:388

commit v3 on v2

--- a/solution.py
+++ b/solution.py
@@ -15,6 +15,7 @@
 F32 = jnp.float32
 BF16 = jnp.bfloat16
 HBM = pl.BlockSpec(memory_space=pltpu.HBM)
+ANY = pl.BlockSpec(memory_space=pl.ANY)
 VMEM = pl.BlockSpec(memory_space=pltpu.VMEM)
 MIB = 1024 * 1024
 FIRST = 10**6
@@ -75,10 +76,10 @@
 
 
 def send_kernel(
-    dims, blocks_hbm, order_hbm, cot_hbm, kernel_hbm, out_ref, shard_ref, blocks_ref, order_ref, cot_ref, sems
+    dims, blocks_hbm, order_hbm, cot_hbm, out_ref, holds_ref, blocks_ref, order_ref, cot_ref, sems
 ):
     devs, slab, slots, clips, held, och = dims
-    pairs = [(blocks_hbm, blocks_ref), (order_hbm, order_ref), (cot_hbm, cot_ref), (kernel_hbm, shard_ref)]
+    pairs = [(blocks_hbm, blocks_ref), (order_hbm, order_ref), (cot_hbm, cot_ref)]
     for copy in fetch(pairs, sems):
         copy.wait()
     me = lax.axis_index("clips")
@@ -87,6 +88,8 @@
         block = cot_ref[q].astype(F32)
         for s in range(slab):
             out_ref[holders[q] * slab + s] = fold(block, s, och, 8).astype(BF16)
+        for d in range(devs):
+            holds_ref[q * devs + d] = jnp.full((1, LANES), jnp.where(holders[q] == d, 1.0, 0.0), F32)
 
 
 def make_table(och, out_ref):
@@ -102,23 +105,26 @@
             out_ref[i : i + 16, group * LANES : (group + 1) * LANES] = both
 
 
-def stage_kernel(slab, *refs):
-    video_refs, video_pad = refs[:slab], refs[slab]
+def stage_kernel(slab, och, *refs):
+    video_refs, video_pad, table_ref, sems = refs[1:slab], refs[slab], refs[slab + 1], refs[slab + 2]
     own = lax.axis_index("slab")
+    copy = fetch([(refs[0], video_pad.at[own + 1])], sems)[0]
+    make_table(och, table_ref)
     zeros = jnp.zeros(video_pad.shape[1:], BF16)
     video_pad[0] = zeros
     video_pad[slab + 1] = zeros
-    for i in range(slab):
-        video_pad[jnp.mod(own - i + slab, slab) + 1] = video_refs[i][...]
-
-
-def forward_kernel(dims, blocks_hbm, *refs):
+    for i in range(1, slab):
+        video_pad[jnp.mod(own - i + slab, slab) + 1] = video_refs[i - 1][...]
+    copy.wait()
+
+
+def forward_kernel(dims, blocks_hbm, gain_ref, bias_ref, *refs):
     devs, slab, clips, held, frames, columns, rows_in, cols, och, per_group = dims
-    shard_refs, video_pad = refs[:devs], refs[devs]
-    weights_ref, normed_ref, inv_ref, table_ref, shards, blocks_ref, sems = refs[devs + 1 :]
-    make_table(och, table_ref)
+    shard_refs, video_pad, table_ref = refs[:devs], refs[devs], refs[devs + 1]
+    weights_ref, video_t_ref, normed_ref, inv_ref, slope_ref, act_ref = refs[devs + 2 : devs + 8]
+    shards, blocks_ref, sems = refs[devs + 8 :]
     copy = fetch([(blocks_hbm, blocks_ref)], sems)[0]
-    me = lax.axis_index("clips")
+    me, own = lax.axis_index("clips"), lax.axis_index("slab")
     places = held * frames * columns
     per_clip = frames * columns
     c_in = video_pad.shape[2]
@@ -127,16 +133,17 @@
     chips = devs // 2
     for t in range(chips):
         for e in range(2):
-            source = 2 * partner(me // 2, t, chips) + (me % 2 + e) % 2
+            source = 2 * ((me // 2) ^ t) + (me % 2 + e) % 2
             shard = shard_refs[t + e * chips][...].astype(F32)
-            shards[source] = jnp.concatenate([shard, jnp.zeros((rows_in, width - cols), F32)], axis=1)
+            shard = jnp.concatenate([shard, jnp.zeros((rows_in, width - cols), F32)], axis=1)
+            shards[source] = shard.astype(shards.dtype)
     weights = shards[...].reshape(c_in, width).astype(BF16)
-    weights_ref[...] = jnp.dot(weights, table_ref[...], preferred_element_type=F32).astype(BF16)
+    weights = jnp.dot(weights, table_ref[...], preferred_element_type=F32).astype(BF16)
 
     total = None
     for b in range(3):
         rows = video_pad[b : b + slab].reshape(many, c_in)
-        term = jnp.dot(rows, weights_ref[:, 384 * b : 384 * (b + 1)], preferred_element_type=F32)
+        term = jnp.dot(rows, weights[:, 384 * b : 384 * (b + 1)], preferred_element_type=F32)
         total = term if total is None else total + term
     mixed = (
         from_left(total[:, 0:LANES], columns)
@@ -145,6 +152,10 @@
     ).reshape(slab, places, LANES)
     frame_shifts = [mixed[:, :, a * och : (a + 1) * och] for a in range(3)]
     frame_of = lax.broadcasted_iota(jnp.int32, (slab, per_clip, och), 1) // columns
+    shift = jnp.mod(LANES - own * och, LANES)
+    gain = pltpu.roll(jnp.broadcast_to(gain_ref[...], (8, LANES)), shift, 1)[0:1, :och]
+    bias = pltpu.roll(jnp.broadcast_to(bias_ref[...], (8, LANES)), shift, 1)[0:1, :och]
+    block_rows = FB * columns
     copy.wait()
     for k in range(held):
         blocks = blocks_ref[me * held + k]
@@ -158,8 +169,20 @@
         mean = group_mean_of(kept, count, per_group)
         var = group_mean_of(kept * conv, count, per_group) - mean * mean
         inv_std = lax.rsqrt(var + 1e-05)
-        normed_ref[:, k * per_clip : (k + 1) * per_clip, :] = (conv - mean) * inv_std
+        normed = (conv - mean) * inv_std
+        normed_ref[:, k * per_clip : (k + 1) * per_clip, :] = normed
         inv_ref[k] = jnp.broadcast_to(inv_std[0], (8, och))
+        affine = normed * gain[None] + bias[None]
+        sigmoid = jax.nn.sigmoid(affine)
+        act = affine * sigmoid
+        slope = sigmoid * (1.0 + affine * (1.0 - sigmoid))
+        slope_ref[:, k * per_clip : (k + 1) * per_clip, :] = slope
+        for b in range(BMAX):
+            for h in range(slab):
+                block = act[h, b * block_rows : (b + 1) * block_rows]
+                act_ref[k * BMAX + b, h] = unfolded_to_lanes(block, 8)
+    weights_ref[...] = jnp.transpose(weights)
+    video_t_ref[...] = jnp.transpose(video_pad[1 : slab + 1].reshape(many, c_in))
 
 
 def from_left(values, columns):
@@ -182,24 +205,22 @@
     return (sums[0:1] / count)[None]
 
 
-def backward_kernel(dims, blocks_hbm, order_hbm, gain_ref, bias_ref, weights_ref, *refs):
+def backward_kernel(dims, blocks_hbm, order_hbm, gain_ref, weights_ref, *refs):
     devs, slab, clips, held, frames, columns, rows_in, cols, och, per_group = dims
-    video_pad, normed_ref, inv_ref, cot_ref = refs[:4]
-    act_hbm, keep_ref, send_ref = refs[4:7]
-    video_grad_refs = refs[7 : 7 + slab]
-    table_ref, act_ref, grad_ref, blocks_ref, order_ref, sems = refs[7 + slab :]
+    video_t_ref, normed_ref, inv_ref, slope_ref, act_in, cot_ref = refs[:6]
+    act_hbm, keep_ref, send_ref = refs[6:9]
+    video_grad_refs = refs[9 : 9 + slab]
+    act_ref, grad_ref, rows_ref, blocks_ref, order_ref, sems = refs[9 + slab :]
     copies = fetch([(blocks_hbm, blocks_ref), (order_hbm, order_ref)], sems)
-    make_table(och, table_ref)
     me, own = lax.axis_index("clips"), lax.axis_index("slab")
     places = held * frames * columns
     per_clip = frames * columns
     block_rows = FB * columns
-    c_in = video_pad.shape[2]
+    c_in = video_t_ref.shape[0]
     groups = LANES // och
     many = slab * places
     shift = jnp.mod(LANES - own * och, LANES)
     gain = pltpu.roll(jnp.broadcast_to(gain_ref[...], (8, LANES)), shift, 1)[0:1, :och]
-    bias = pltpu.roll(jnp.broadcast_to(bias_ref[...], (8, LANES)), shift, 1)[0:1, :och]
     frame_of = lax.broadcasted_iota(jnp.int32, (slab, per_clip, och), 1) // columns
     gain_part = jnp.zeros((1, och), F32)
     bias_part = jnp.zeros((1, och), F32)
@@ -224,10 +245,8 @@
         count = (blocks * (FB * slab * columns * per_group)).astype(F32)
         inv_std = inv_ref[k][None, 0:1]
         normed = normed_ref[:, k * per_clip : (k + 1) * per_clip, :]
-        affine = normed * gain[None] + bias[None]
-        sigmoid = jax.nn.sigmoid(affine)
-        act = affine * sigmoid
-        grad_affine = jnp.where(alive, cot * sigmoid * (1.0 + affine * (1.0 - sigmoid)), 0.0)
+        slope = slope_ref[:, k * per_clip : (k + 1) * per_clip, :]
+        grad_affine = jnp.where(alive, cot * slope, 0.0)
         gain_part += jnp.sum(jnp.sum(grad_affine * normed, axis=0), axis=0, keepdims=True)
         bias_part += jnp.sum(jnp.sum(grad_affine, axis=0), axis=0, keepdims=True)
         grad_normed = grad_affine * gain[None]
@@ -245,8 +264,7 @@
         for b in range(BMAX):
             device = order_ref[jnp.mod(start + b, devs)]
             for h in range(slab):
-                block = unfolded_to_lanes(act[h, b * block_rows : (b + 1) * block_rows], 8)
-                act_blocks.append((b < blocks, device * slab + h, block))
+                act_blocks.append((b < blocks, device * slab + h, act_in[k * BMAX + b, h]))
         start = start + blocks
 
     sums = split3(gain_part) + split3(bias_part) + [jnp.zeros((2, och), F32)]
@@ -271,31 +289,24 @@
         shifted = shifted.astype(BF16).reshape(slab, places, LANES)
         grad_ref[1 : slab + 1, :, e * LANES : (e + 1) * LANES] = shifted
 
+    total = None
+    for b in range(3):
+        term = jnp.dot(
+            grad_ref[2 - b : 2 - b + slab].reshape(many, 3 * LANES),
+            weights_ref[384 * b : 384 * (b + 1)],
+            preferred_element_type=F32,
+        )
+        total = term if total is None else total + term
+    rows_ref[...] = total.reshape(slab, places, c_in)
     for i, ref in enumerate(video_grad_refs):
-        row = jnp.mod(own + i, slab)
-        total = None
-        for b in range(3):
-            term = lax.dot_general(
-                grad_ref[row + 2 - b],
-                weights_ref[:, 384 * b : 384 * (b + 1)],
-                (((1,), (1,)), ((), ())),
-                preferred_element_type=F32,
-            )
-            total = term if total is None else total + term
-        ref[...] = total.astype(ref.dtype)
-
-    video_t = jnp.transpose(video_pad[1 : slab + 1].reshape(many, c_in))
+        ref[...] = rows_ref[jnp.mod(own + i, slab)].astype(ref.dtype)
+
     parts = []
     for b in range(3):
         moved = grad_ref[2 - b : 2 - b + slab].reshape(many, 3 * LANES)
-        parts.append(jnp.dot(video_t, moved, preferred_element_type=F32).astype(BF16))
-    native = lax.dot_general(
-        jnp.concatenate(parts, axis=1),
-        table_ref[...],
-        (((1,), (1,)), ((), ())),
-        preferred_element_type=F32,
-    ).reshape(devs // 2, 2 * rows_in, table_ref.shape[0])
-    low, high = native[:, :rows_in, :cols], native[:, rows_in:, :cols]
+        parts.append(jnp.dot(video_t_ref[...], moved, preferred_element_type=F32))
+    terms = jnp.concatenate(parts, axis=1).reshape(devs // 2, 2 * rows_in, 9 * LANES)
+    low, high = terms[:, :rows_in], terms[:, rows_in:]
     odd = me % 2 == 1
     keep_ref[...] = jnp.where(odd, high, low)
     send_ref[...] = jnp.where(odd, low, high).astype(BF16)
@@ -318,45 +329,73 @@
         ref[...] = (keep_ref[chip] + other_ref[chip].astype(F32)).astype(ref.dtype)
 
 
-def finish_kernel(dims, blocks_hbm, order_hbm, act_in, *refs):
-    devs, slab, slots, clips, held, och = dims
-    chips = devs // 2
-    kernel_refs, grad_refs = refs[:chips], refs[chips : chips + slab]
-    kernel_grad_ref, video_grad_ref, act_ref, gain_ref, bias_ref = refs[chips + slab : -3]
-    blocks_ref, order_ref, sems = refs[-3:]
-    copies = fetch([(blocks_hbm, blocks_ref), (order_hbm, order_ref)], sems)
+def sum_kernel(*refs):
+    total = refs[0][...]
+    for ref in refs[1:-1]:
+        total = total + ref[...].astype(F32)
+    refs[-1][...] = total.astype(refs[-1].dtype)
+
+
+def table_kernel(och, after_ref, table_ref):
+    rows, cols = table_ref.shape
+    lane = lax.broadcasted_iota(jnp.int32, (LANES, LANES), 0)
+    source = jnp.where(lane < 3 * och, 27 * (lane % och) + 9 * (2 - lane // och), -cols)
+    ahead = source - lax.broadcasted_iota(jnp.int32, (LANES, LANES), 1)
+    for group in range(rows // LANES):
+        for j in range(0, cols, LANES):
+            hit = jnp.where(ahead == j - group, 1.0, 0.0).astype(BF16)
+            table_ref[group * LANES : (group + 1) * LANES, j : j + LANES] = hit
+
+
+def weights_kernel(*refs):
+    kernel_refs, table_ref, kernel_grad_ref = refs[:-2], refs[-2], refs[-1]
     total = kernel_refs[0][...]
     for ref in kernel_refs[1:]:
         total = total + ref[...].astype(F32)
-    kernel_grad_ref[...] = total
-    total = grad_refs[0][...]
-    for ref in grad_refs[1:]:
-        total = total + ref[...].astype(F32)
-    video_grad_ref[...] = total.astype(BF16)
+    rows, cols = kernel_grad_ref.shape
+    native = jnp.dot(
+        jnp.concatenate(split3(total), axis=0).astype(BF16),
+        table_ref[...],
+        preferred_element_type=F32,
+    )
+    native = native[:rows] + (native[rows : 2 * rows] + native[2 * rows :])
+    kernel_grad_ref[...] = native[:, :cols]
+
+
+def finish_kernel(dims, holds_ref, act_in, after_ref, *refs):
+    devs, slab, slots, och = dims
+    hbm_refs, (act_ref, gain_ref, bias_ref), sems = refs[:3], refs[3:6], refs[6]
     groups = LANES // och
     rows = act_in.shape[1] - 8
     sums = []
+    blocks = [[jnp.zeros((rows, LANES), F32)] * slab for _ in range(slots)]
     for s in range(slab):
-        part = act_in[s].astype(F32)[rows:]
-        for d in range(1, devs):
-            part = part + act_in[d * slab + s].astype(F32)[rows:]
+        part = jnp.zeros((8, LANES), F32)
+        for d in range(devs):
+            both = act_in[d * slab + s].astype(F32)
+            part = part + both[rows:]
+            for q in range(slots):
+                blocks[q][s] = blocks[q][s] + both[:rows] * holds_ref[q * devs + d]
         sums.append(part[:, :och])
     sums = jnp.concatenate(sums, axis=1)
     gain_ref[...] = sums[0:1] + (sums[1:2] + sums[2:3])
     bias_ref[...] = sums[3:4] + (sums[4:5] + sums[5:6])
+    copies = [pltpu.make_async_copy(a, b, sems.at[i]) for i, (a, b) in enumerate(zip(refs[3:6], hbm_refs))]
+    copies[1].start()
+    copies[2].start()
+    for q in range(slots):
+        block = []
+        for g in range(groups):
+            parts = [p[:, g * och : (g + 1) * och] for p in blocks[q]]
+            block.append(jnp.concatenate(parts, axis=1))
+        act_ref[q] = jnp.concatenate(block, axis=0)[: act_ref.shape[1]].astype(BF16)
+    copies[0].start()
     for copy in copies:
         copy.wait()
-    me = lax.axis_index("clips")
-    holders = slot_holders(blocks_ref, order_ref, me, slots, clips, held, devs)
-    for q in range(slots):
-        parts = [act_in[holders[q] * slab + s].astype(F32)[:rows] for s in range(slab)]
-        block = []
-        for g in range(groups):
-            block.append(jnp.concatenate([p[:, g * och : (g + 1) * och] for p in parts], axis=1))
-        act_ref[q] = jnp.concatenate(block, axis=0)[: act_ref.shape[1]].astype(BF16)
-
-
-def call(kernel, outs, specs, scratch=(), limit=4 * MIB, out_specs=None, cost=None):
+
+
+def call(kernel, outs, specs, scratch=(), limit=None, out_specs=None, cost=None):
+    limit = limit or lax.axis_size("slab") * MIB
     return pl.pallas_call(
         kernel,
         out_shape=outs,
@@ -413,87 +452,112 @@
     gain, bias = gain.reshape(1, c_out), bias.reshape(1, c_out)
     clip_blocks = pltpu.with_memory_space_constraint(clip_blocks, pltpu.HBM)
     deal_order = pltpu.with_memory_space_constraint(deal_order, pltpu.HBM)
-    kernel = pltpu.with_memory_space_constraint(kernel, pltpu.HBM)
     cotangent_blocks = pltpu.with_memory_space_constraint(
         cotangent.reshape(slots, block_rows, c_out), pltpu.HBM
     )
 
     videos = shifts([video.reshape(places, c_in)] * slab, "slab")
-    cots, shard = call(
+    cots, holds = call(
         functools.partial(send_kernel, (devs, slab, slots, clips, held, och)),
-        [shape((devs * slab, fold_rows, LANES), BF16), shape((rows_in, cols), BF16)],
-        [HBM, HBM, HBM, HBM],
-        smem + [pltpu.VMEM((slots, block_rows, c_out), BF16), pltpu.SemaphoreType.DMA((4,))],
+        [shape((devs * slab, fold_rows, LANES), BF16), shape((slots * devs, 1, LANES), F32)],
+        [HBM, HBM, HBM],
+        smem + [pltpu.VMEM((slots, block_rows, c_out), BF16), pltpu.SemaphoreType.DMA((3,))],
         cost=pl.CostEstimate(flops=FIRST, bytes_accessed=0, transcendentals=0),
-    )(clip_blocks, deal_order, cotangent_blocks, kernel)
+    )(clip_blocks, deal_order, cotangent_blocks)
     cots = lax.all_to_all(cots, everyone, split_axis=0, concat_axis=0, tiled=True)
-    shards = chip_swaps([shard] * chips, "clips")
+    shards = [kernel]
+    while len(shards) < chips:
+        pairs = [(j, j ^ (2 * len(shards))) for j in range(devs)]
+        shards = shards + [lax.ppermute(shard, "clips", pairs) for shard in shards]
     shards = shards + [core_swap(shard, "clips") for shard in shards]
 
     dims = (devs, slab, clips, held, frames, columns, rows_in, cols, och, per_group)
-    video_pad = call(
-        functools.partial(stage_kernel, slab),
-        [shape((slab + 2, places, c_in), BF16)],
-        [VMEM] * slab,
+    video_pad, table = call(
+        functools.partial(stage_kernel, slab, och),
+        [shape((slab + 2, places, c_in), BF16), shape((width, 9 * LANES), BF16)],
+        [HBM] + [VMEM] * (slab - 1),
+        [pltpu.SemaphoreType.DMA((1,))],
         cost=pl.CostEstimate(flops=STAGE, bytes_accessed=0, transcendentals=0),
-    )(*videos)[0]
-    weights, normed, inv_std = call(
+    )(pltpu.with_memory_space_constraint(videos[0], pltpu.HBM), *videos[1:])
+    weights, video_t, normed, inv_std, slope, act = call(
         functools.partial(forward_kernel, dims),
         [
-            shape((c_in, 9 * LANES), BF16),
+            shape((9 * LANES, c_in), BF16),
+            shape((c_in, slab * places), BF16),
             shape((slab, places, och), F32),
             shape((held, 8, och), F32),
+            shape((slab, places, och), F32),
+            shape((held * BMAX, slab, fold_rows, LANES), F32),
         ],
-        [HBM] + [VMEM] * (devs + 1),
+        [HBM] + [VMEM] * (devs + 4),
         [
-            pltpu.VMEM((width, 9 * LANES), BF16),
-            pltpu.VMEM((devs, rows_in, width), F32),
+            pltpu.VMEM((devs, rows_in, width), F32 if rows_in % 16 else BF16),
             smem[0],
             pltpu.SemaphoreType.DMA((1,)),
         ],
         large,
-    )(clip_blocks, *shards, video_pad)
+    )(clip_blocks, gain, bias, *shards, video_pad, table)
     acts, keep, send, *video_grads = call(
         functools.partial(backward_kernel, dims),
         [
             pltpu.HBM((devs * slab, fold_rows + 8, LANES), BF16),
-            shape((chips, rows_in, cols), F32),
-            shape((chips, rows_in, cols), BF16),
+            shape((chips, rows_in, 9 * LANES), F32),
+            shape((chips, rows_in, 9 * LANES), BF16),
         ]
         + [shape((places, c_in), F32 if i == 0 else BF16) for i in range(slab)],
-        [HBM, HBM] + [VMEM] * 7,
+        [HBM, HBM] + [VMEM] * 8,
         [
-            pltpu.VMEM((width, 9 * LANES), BF16),
             pltpu.VMEM((devs * slab, fold_rows + 8, LANES), BF16),
             pltpu.VMEM((slab + 2, places, 3 * LANES), BF16),
+            pltpu.VMEM((slab, places, c_in), F32),
         ]
         + smem
         + [pltpu.SemaphoreType.DMA((3,))],
         large,
         [HBM] + [VMEM] * (2 + slab),
-    )(clip_blocks, deal_order, gain, bias, weights, video_pad, normed, inv_std, cots)
+    )(clip_blocks, deal_order, gain, weights, video_t, normed, inv_std, slope, act, cots)
     video_grads = shifts(video_grads, "slab")
     send = core_swap(send, "clips")
     acts = lax.all_to_all(acts, everyone, split_axis=0, concat_axis=0, tiled=True)
     kernel_grads = call(
         functools.partial(pair_kernel, chips),
-        [shape((rows_in, cols), F32 if t == 0 else BF16) for t in range(chips)],
+        [shape((rows_in, 9 * LANES), F32 if t == 0 else BF16) for t in range(chips)],
         [VMEM, VMEM],
     )(keep, send)
+    table = call(
+        functools.partial(table_kernel, och), [shape((9 * LANES, width), BF16)], [ANY]
+    )(kernel_grads[1])[0]
     kernel_grads = chip_swaps(kernel_grads, "clips")
 
-    kernel_grad, video_grad, act, gain_grad, bias_grad = call(
-        functools.partial(finish_kernel, (devs, slab, slots, clips, held, och)),
+    video_grad = call(
+        sum_kernel,
+        [shape((places, c_in), BF16)],
+        [VMEM] * slab,
+        cost=pl.CostEstimate(flops=STAGE, bytes_accessed=0, transcendentals=0),
+    )(*video_grads)[0]
+    kernel_grad = call(
+        weights_kernel,
+        [shape((rows_in, cols), F32)],
+        [VMEM] * (chips + 1),
+        limit=2 * slab * MIB,
+        cost=pl.CostEstimate(flops=STAGE, bytes_accessed=0, transcendentals=0),
+    )(*kernel_grads, table)[0]
+    act, gain_grad, bias_grad = call(
+        functools.partial(finish_kernel, (devs, slab, slots, och)),
         [
-            shape((rows_in, cols), F32),
-            shape((places, c_in), BF16),
-            shape((slots, block_rows, c_out), BF16),
-            shape((1, c_out), F32),
-            shape((1, c_out), F32),
+            pltpu.HBM((slots, block_rows, c_out), BF16),
+            pltpu.HBM((1, c_out), F32),
+            pltpu.HBM((1, c_out), F32),
         ],
-        [HBM, HBM] + [VMEM] * (1 + chips + slab),
-        smem + [pltpu.SemaphoreType.DMA((2,))],
-    )(clip_blocks, deal_order, acts, *kernel_grads, *video_grads)
+        [VMEM, VMEM, HBM],
+        [
+            pltpu.VMEM((slots, block_rows, c_out), BF16),
+            pltpu.VMEM((1, c_out), F32),
+            pltpu.VMEM((1, c_out), F32),
+            pltpu.SemaphoreType.DMA((3,)),
+        ],
+        out_specs=[HBM] * 3,
+    )(holds, acts, pltpu.with_memory_space_constraint(kernel_grad, pltpu.HBM))
     return (
         act.reshape(cotangent.shape),
         video_grad.reshape(video.shape),

time: 49.1 us -> 43.3 us (0.88)
  starting transfers between devices: 30 us -> 24.3 us
  Pallas kernels: 9.95 us -> 11.1 us
  local copies, waits for them, and re-layouts: 0.68 us -> 0.02 us
  waiting for transfers between devices: 7.29 us -> 6.68 us
    ppermute x6 -> x3, starting transfers between devices: 10.4 us -> 3.55 us  [chip_swaps(): moved.append(lax.ppermute(arrays[t], axis, pairs))]
    ppermute x0 -> x3, starting transfers between devices: none -> 5.03 us  [body(): shards = shards + [lax.ppermute(shard, 'clips', pairs) for shard in shards]]
    pallas_call x4 -> x7, Pallas kernels: 4.21 us -> 6.79 us  [the longest x1 2.84 us: body(): call(functools.partial(forward_kernel, dims), [shape((9 * LANES, c_in), B...]
    all_to_all x1, starting transfers between devices: 5.06 us -> 2.59 us  [body(): lax.all_to_all(cots, everyone, split_axis=0, concat_axis=0, tiled=True)]
    ppermute x6 -> x3, waiting for transfers between devices: 1.23 us -> 3.15 us  [chip_swaps(): moved.append(lax.ppermute(arrays[t], axis, pairs))]
    ppermute x6, waiting for transfers between devices: 2.68 us -> 0.99 us  [shifts(): lax.ppermute(arrays[i], axis, [(j, (j + i) % size) for j in range(size)])]
    pallas_call x1, Pallas kernels: 4.1 us -> 2.81 us  [body(): call(functools.partial(backward_kernel, dims), [pltpu.HBM((devs * slab, f...]
    ppermute x5, waiting for transfers between devices: 1.18 us -> 0.01 us  [core_swap(): lax.ppermute(array, axis, [(j, j ^ 1) for j in range(lax.axis_size(axis))])]
  transfers between devices with their start and end apart: 19 -> 19, of which waited for: 8 -> 4; matrix products, arithmetic and copies ran while one was open for 0% -> 0% of each run, Pallas kernels for 6% -> 18%
where the time goes in v3:
time: 43.3 us; the launch traced here: 42.9 us
  starting transfers between devices  24.3 us (56%)
  Pallas kernels  11.1 us (26%)
  waiting for transfers between devices  6.68 us (15%)
  between operations  0.81 us (2%)
    ppermute x6, starting transfers between devices, shifts(): lax.ppermute(arrays[i], axis, [(j, (j + i) % size) for j in range(size)])  9.39 us
    ppermute x3, starting transfers between devices, body(): shards = shards + [lax.ppermute(shard, 'clips', pairs) for shard in shards]  5.03 us
    ppermute x3, starting transfers between devices, chip_swaps(): moved.append(lax.ppermute(arrays[t], axis, pairs))  3.55 us
    ppermute x3, waiting for transfers between devices, chip_swaps(): moved.append(lax.ppermute(arrays[t], axis, pairs))  3.15 us
    pallas_call x1, Pallas kernels, body(): call(functools.partial(forward_kernel, dims), [shape((9 * LANES, c_in), B...  2.84 us
    pallas_call x1, Pallas kernels, body(): call(functools.partial(backward_kernel, dims), [pltpu.HBM((devs * slab, f...  2.81 us
    all_to_all x1, starting transfers between devices, body(): lax.all_to_all(cots, everyone, split_axis=0, concat_axis=0, tiled=True)  2.59 us
    all_to_all x1, starting transfers between devices, body(): lax.all_to_all(acts, everyone, split_axis=0, concat_axis=0, tiled=True)  2.57 us
  transfers between devices with their start and end apart: 19, of which 4 were waited for; matrix products, arithmetic and copies ran while one was open for 0% of the time, Pallas kernels for 18%

profile of v3, /device:TPU:0, one launch (start us, length us, event | category | flops | bytes accessed | tf_op | source)
XLA Modules:
  0.0 42.9 jit_solution(16485807827386219708)
XLA Ops:
  0.6 3.0 %collective-permute-start = (bf16[32,864]{1,0:T(8,128)(2,1)}, bf16[32,864]{1,0:T(8,128)(2,1)S(1)}, u32[]{:S(2)}, u32[]{:S(2)}) collective-permute-start(bf16[32,864]{1,0:T(8,128)(2,1)} %refs_0_.1), channel_id=1, source_target_pairs={{0,8},{4,12},{8,0},{12,4},{16,24},{20,28},{24,16},{28,20},{1,9},{5... | collective-permute-start | bytes 165896 | tf_op jit(solution)/shard_map/ppermute | solution.py:471
  3.6 1.6 %collective-permute-start.7 = (bf16[192,256]{1,0:T(8,128)(2,1)}, bf16[192,256]{1,0:T(8,128)(2,1)S(1)}, u32[]{:S(2)}, u32[]{:S(2)}) collective-permute-start(bf16[192,256]{1,0:T(8,128)(2,1)} %bitcast.16), channel_id=1, source_target_pairs={{0,1},{1,2},{2,3},{3,0},{4,5},{5,6},{6,7},{7,4},{8,9},{9,10},{10,1... | collective-permute-start | bytes 294920 | tf_op jit(solution)/shard_map/ppermute | solution.py:418
  5.2 2.6 %collective-permute-start.8 = (bf16[192,256]{1,0:T(8,128)(2,1)}, bf16[192,256]{1,0:T(8,128)(2,1)S(1)}, u32[]{:S(2)}, u32[]{:S(2)}) collective-permute-start(bf16[192,256]{1,0:T(8,128)(2,1)} %bitcast.17), channel_id=1, source_target_pairs={{0,2},{1,3},{2,0},{3,1},{4,6},{5,7},{6,4},{7,5},{8,10},{9,11},{10,... | collective-permute-start | bytes 294920 | tf_op jit(solution)/shard_map/ppermute | solution.py:418
  7.8 1.3 %collective-permute-start.9 = (bf16[192,256]{1,0:T(8,128)(2,1)}, bf16[192,256]{1,0:T(8,128)(2,1)S(1)}, u32[]{:S(2)}, u32[]{:S(2)}) collective-permute-start(bf16[192,256]{1,0:T(8,128)(2,1)} %bitcast.18), channel_id=1, source_target_pairs={{0,3},{1,0},{2,1},{3,2},{4,7},{5,4},{6,5},{7,6},{8,11},{9,8},{10,9... | collective-permute-start | bytes 294920 | tf_op jit(solution)/shard_map/ppermute | solution.py:418
  9.2 1.5 %collective-permute-start.1 = (bf16[32,864]{1,0:T(8,128)(2,1)}, bf16[32,864]{1,0:T(8,128)(2,1)S(1)}, u32[]{:S(2)}, u32[]{:S(2)}) collective-permute-start(bf16[32,864]{1,0:T(8,128)(2,1)} %refs_0_.1), channel_id=1, source_target_pairs={{0,16},{4,20},{8,24},{12,28},{16,0},{20,4},{24,8},{28,12},{1,17},{... | collective-permute-start | bytes 165896 | tf_op jit(solution)/shard_map/ppermute | solution.py:471
  10.7 0.5 %collective-permute-start.2 = (bf16[32,864]{1,0:T(8,128)(2,1)S(1)}, bf16[32,864]{1,0:T(8,128)(2,1)S(1)}, u32[]{:S(2)}, u32[]{:S(2)}) collective-permute-start(bf16[32,864]{1,0:T(8,128)(2,1)S(1)} %collective-permute-done.refs_1_), channel_id=1, source_target_pairs={{0,16},{4,20},{8,24},{12,28},{16,0},{20,4},{24,8},{28,12},{1,17},{... | collective-permute-start | bytes 165896 | tf_op jit(solution)/shard_map/ppermute | solution.py:471
  11.2 1.5 %shard_map.110 = (bf16[32,8,128]{2,1,0:T(8,128)(2,1)}, f32[32,1,128]{2,1,0:T(1,128)S(1)}) custom-call(s32[16]{0:T(128)} %blocks_hbm.5, s32[8]{0:T(128)} %order_hbm.3, bf16[4,32,128]{2,1,0:T(8,128)(2,1)} %bitcast.15), custom_call_target="tpu_custom_call" | custom-call | flops 1000000 | tf_op jit(solution)/shard_map/pallas_call | solution.py:460
  12.7 2.6 %all-to-all-start = ((bf16[32,8,128]{2,1,0:T(8,128)(2,1)}), bf16[32,8,128]{2,1,0:T(8,128)(2,1)S(1)}, u32[]{:S(2)}, u32[]{:S(2)}) async-start(bf16[32,8,128]{2,1,0:T(8,128)(2,1)} %get-tuple-element.38), calls=%async_computation | async-start | bytes 131072 | tf_op jit(solution)/shard_map/all_to_all | solution.py:467
  15.6 0.4 collective-permute-start.4
  16.5 0.9 %shard_map.111 = (bf16[6,192,256]{2,1,0:T(8,128)(2,1)S(1)}, bf16[896,1152]{1,0:T(8,128)(2,1)S(1)}) custom-call(bf16[192,256]{1,0:T(8,128)(2,1)} %bitcast.19, bf16[192,256]{1,0:T(8,128)(2,1)S(1)} %collective-permute-done.7.refs_1_, bf16[192,256]{1,0:T(8,128)(2,1)S(1)} %collective-permute-done.8.refs_2_, bf16[192,256]{1,0:T(8,128)(2,1)S(1)} %collective-permute-done.9.refs_3_), custom_call_target="tpu_custom_call" | custom-call | flops 10000000000 | tf_op jit(solution)/shard_map/pallas_call | solution.py:475
  17.5 2.8 %shard_map.112 = (bf16[1152,256]{1,0:T(8,128)(2,1)S(1)}, bf16[256,768]{1,0:T(8,128)(2,1)S(1)}, f32[4,192,32]{2,1,0:T(8,128)S(1)}, f32[2,8,32]{2,1,0:T(8,128)S(1)...) custom-call(s32[16]{0:T(128)} %blocks_hbm.5, f32[1,128]{1,0:T(1,128)S(1)} %bitcast.12, f32[1,128]{1,0:T(1,128)S(1)} %bitcast.14, ...), custom_call_target="tpu_custom_call" | custom-call | tf_op jit(solution)/shard_map/pallas_call | solution.py:482
  20.3 2.5 %all-to-all-done.refs_5_ = bf16[32,8,128]{2,1,0:T(8,128)(2,1)S(1)} async-done(((bf16[32,8,128]{2,1,0:T(8,128)(2,1)}), bf16[32,8,128]{2,1,0:T(8,128)(2,1)S(1)}, u32[]{:S(2)}, u32[]{:S(2)}) %all-to-all-start) | async-done | bytes 65568 | tf_op jit(solution)/shard_map/all_to_all | solution.py:467
  22.8 2.8 %shard_map.113 = (bf16[32,16,128]{2,1,0:T(8,128)(2,1)}, f32[4,32,1152]{2,1,0:T(8,128)S(1)}, bf16[4,32,1152]{2,1,0:T(8,128)(2,1)S(1)}, f32[192,256]{1,0:T(8,128)S...) custom-call(s32[16]{0:T(128)} %blocks_hbm.5, s32[8]{0:T(128)} %order_hbm.3, ...), custom_call_target="tpu_custom_call" | custom-call | tf_op jit(solution)/shard_map/pallas_call | solution.py:500
  26.1 1.6 %collective-permute-start.15 = (bf16[192,256]{1,0:T(8,128)(2,1)S(1)}, bf16[192,256]{1,0:T(8,128)(2,1)S(1)}, u32[]{:S(2)}, u32[]{:S(2)}) collective-permute-start(bf16[192,256]{1,0:T(8,128)(2,1)S(1)} %get-tuple-element.49), channel_id=1, source_target_pairs={{0,2},{1,3},{2,0},{3,1},{4,6},{5,7},{6,4},{7,5},{8,10},{9,11},{10,... | collective-permute-start | bytes 294920 | tf_op jit(solution)/shard_map/ppermute | solution.py:418
  27.6 1.9 %collective-permute-start.16 = (bf16[192,256]{1,0:T(8,128)(2,1)S(1)}, bf16[192,256]{1,0:T(8,128)(2,1)S(1)}, u32[]{:S(2)}, u32[]{:S(2)}) collective-permute-start(bf16[192,256]{1,0:T(8,128)(2,1)S(1)} %get-tuple-element.50), channel_id=1, source_target_pairs={{0,3},{1,0},{2,1},{3,2},{4,7},{5,4},{6,5},{7,6},{8,11},{9,8},{10,9... | collective-permute-start | bytes 294920 | tf_op jit(solution)/shard_map/ppermute | solution.py:418
  29.6 2.6 %all-to-all-start.1 = ((bf16[32,16,128]{2,1,0:T(8,128)(2,1)}), bf16[32,16,128]{2,1,0:T(8,128)(2,1)S(1)}, u32[]{:S(2)}, u32[]{:S(2)}) async-start(bf16[32,16,128]{2,1,0:T(8,128)(2,1)} %get-tuple-element.39), calls=%async_computation.1 | async-start | bytes 262144 | tf_op jit(solution)/shard_map/all_to_all | solution.py:521
  32.3 1.8 %collective-permute-start.11 = (bf16[32,1152]{1,0:T(8,128)(2,1)S(1)}, bf16[32,1152]{1,0:T(8,128)(2,1)S(1)}, u32[]{:S(2)}, u32[]{:S(2)}) collective-permute-start(bf16[32,1152]{1,0:T(8,128)(2,1)S(1)} %get-tuple-element.43.after_ref), channel_id=1, source_target_pairs={{0,8},{4,12},{8,0},{12,4},{16,24},{20,28},{24,16},{28,20},{1,9},{5... | collective-permute-start | bytes 221192 | tf_op jit(solution)/shard_map/ppermute | solution.py:427
  34.0 1.5 %collective-permute-start.12 = (bf16[32,1152]{1,0:T(8,128)(2,1)S(1)}, bf16[32,1152]{1,0:T(8,128)(2,1)S(1)}, u32[]{:S(2)}, u32[]{:S(2)}) collective-permute-start(bf16[32,1152]{1,0:T(8,128)(2,1)S(1)} %get-tuple-element.44), channel_id=1, source_target_pairs={{0,16},{4,20},{8,24},{12,28},{16,0},{20,4},{24,8},{28,12},{1,17},{... | collective-permute-start | bytes 221192 | tf_op jit(solution)/shard_map/ppermute | solution.py:427
  35.8 1.0 %collective-permute-done.15.refs_2_ = bf16[192,256]{1,0:T(8,128)(2,1)S(1)} collective-permute-done((bf16[192,256]{1,0:T(8,128)(2,1)S(1)}, bf16[192,256]{1,0:T(8,128)(2,1)S(1)}, u32[]{:S(2)}, u32[]{:S(2)}) %collective-permute-start.15) | collective-permute-done | bytes 98336 | tf_op jit(solution)/shard_map/ppermute | solution.py:418
  36.8 0.7 %shard_map.118 = bf16[192,256]{1,0:T(8,128)(2,1)} custom-call(f32[192,256]{1,0:T(8,128)S(1)} %get-tuple-element.47.refs_0_, bf16[192,256]{1,0:T(8,128)(2,1)S(1)} %collective-permute-done.14.refs_1_, bf16[192,256]{1,0:T(8,128)(2,1)S(1)} %collective-permute-done.15.refs_2_, bf16[192,256]{1,0:T(8,128)(2,1)S(1)} %collective-permute-done.16.refs_3_), custom_call_target="tpu_custom_call" | custom-call | flops 10000000000 | tf_op jit(solution)/shard_map/pallas_call | solution.py:532
  37.9 1.5 %collective-permute-done.12.refs_2_ = bf16[32,1152]{1,0:T(8,128)(2,1)S(1)} collective-permute-done((bf16[32,1152]{1,0:T(8,128)(2,1)S(1)}, bf16[32,1152]{1,0:T(8,128)(2,1)S(1)}, u32[]{:S(2)}, u32[]{:S(2)}) %collective-permute-start.12) | collective-permute-done | bytes 73760 | tf_op jit(solution)/shard_map/ppermute | solution.py:427
  39.4 1.6 %collective-permute-done.13.refs_3_ = bf16[32,1152]{1,0:T(8,128)(2,1)S(1)} collective-permute-done((bf16[32,1152]{1,0:T(8,128)(2,1)S(1)}, bf16[32,1152]{1,0:T(8,128)(2,1)S(1)}, u32[]{:S(2)}, u32[]{:S(2)}) %collective-permute-start.13) | collective-permute-done | bytes 73760 | tf_op jit(solution)/shard_map/ppermute | solution.py:427
  41.1 1.1 %shard_map.116.after_ref = f32[32,864]{1,0:T(8,128)} custom-call(f32[32,1152]{1,0:T(8,128)S(1)} %get-tuple-element.42.refs_0_, bf16[32,1152]{1,0:T(8,128)(2,1)S(1)} %collective-permute-done.11.refs_1_, bf16[32,1152]{1,0:T(8,128)(2,1)S(1)} %collective-permute-done.12.refs_2_, bf16[32,1152]{1,0:T(8,128)(2,1)S(1)} %collective-permute-done.13.refs_3_, ...), custom_call_target="tpu_custom_call" | custom-call | flops 10000000000 | tf_op jit(solution)/shard_map/pallas_call | solution.py:538
  42.2 0.8 %shard_map.117 = (bf16[4,32,128]{2,1,0:T(8,128)(2,1)}, f32[1,128]{1,0:T(1,128)}, f32[1,128]{1,0:T(1,128)}) custom-call(f32[32,1,128]{2,1,0:T(1,128)S(1)} %get-tuple-element.29.holds_ref, bf16[32,16,128]{2,1,0:T(8,128)(2,1)S(1)} %all-to-all-done.1.act_in, f32[32,864]{1,0:T(8,128)} %shard_map.116.after_ref), custom_call_target="tpu_custom_call" | custom-call | tf_op jit(solution)/shard_map/pallas_call | solution.py:545
  (29 shorter events, 2.0 us)
Async XLA Ops:
  0.6 10.0 %collective-permute-start = (bf16[32,864]{1,0:T(8,128)(2,1)}, bf16[32,864]{1,0:T(8,128)(2,1)S(1)}, u32[]{:S(2)}, u32[]{:S(2)}) collective-permute-start(bf16[32,864]{1,0:T(8,128)(2,1)} %refs_0_.1), channel_id=1, source_target_pairs={{0,8},{4,12},{8,0},{12,4},{16,24},{20,28},{24,16},{28,20},{1,9},{5... | collective-permute-start | bytes 165896 | tf_op jit(solution)/shard_map/ppermute | solution.py:471
  3.6 11.9 %collective-permute-start.7 = (bf16[192,256]{1,0:T(8,128)(2,1)}, bf16[192,256]{1,0:T(8,128)(2,1)S(1)}, u32[]{:S(2)}, u32[]{:S(2)}) collective-permute-start(bf16[192,256]{1,0:T(8,128)(2,1)} %bitcast.16), channel_id=1, source_target_pairs={{0,1},{1,2},{2,3},{3,0},{4,5},{5,6},{6,7},{7,4},{8,9},{9,10},{10,1... | collective-permute-start | bytes 294920 | tf_op jit(solution)/shard_map/ppermute | solution.py:418
  5.2 10.7 %collective-permute-start.8 = (bf16[192,256]{1,0:T(8,128)(2,1)}, bf16[192,256]{1,0:T(8,128)(2,1)S(1)}, u32[]{:S(2)}, u32[]{:S(2)}) collective-permute-start(bf16[192,256]{1,0:T(8,128)(2,1)} %bitcast.17), channel_id=1, source_target_pairs={{0,2},{1,3},{2,0},{3,1},{4,6},{5,7},{6,4},{7,5},{8,10},{9,11},{10,... | collective-permute-start | bytes 294920 | tf_op jit(solution)/shard_map/ppermute | solution.py:418
  7.8 8.7 %collective-permute-start.9 = (bf16[192,256]{1,0:T(8,128)(2,1)}, bf16[192,256]{1,0:T(8,128)(2,1)S(1)}, u32[]{:S(2)}, u32[]{:S(2)}) collective-permute-start(bf16[192,256]{1,0:T(8,128)(2,1)} %bitcast.18), channel_id=1, source_target_pairs={{0,3},{1,0},{2,1},{3,2},{4,7},{5,4},{6,5},{7,6},{8,11},{9,8},{10,9... | collective-permute-start | bytes 294920 | tf_op jit(solution)/shard_map/ppermute | solution.py:418
  9.2 6.2 %collective-permute-start.1 = (bf16[32,864]{1,0:T(8,128)(2,1)}, bf16[32,864]{1,0:T(8,128)(2,1)S(1)}, u32[]{:S(2)}, u32[]{:S(2)}) collective-permute-start(bf16[32,864]{1,0:T(8,128)(2,1)} %refs_0_.1), channel_id=1, source_target_pairs={{0,16},{4,20},{8,24},{12,28},{16,0},{20,4},{24,8},{28,12},{1,17},{... | collective-permute-start | bytes 165896 | tf_op jit(solution)/shard_map/ppermute | solution.py:471
  10.7 5.4 %collective-permute-start.2 = (bf16[32,864]{1,0:T(8,128)(2,1)S(1)}, bf16[32,864]{1,0:T(8,128)(2,1)S(1)}, u32[]{:S(2)}, u32[]{:S(2)}) collective-permute-start(bf16[32,864]{1,0:T(8,128)(2,1)S(1)} %collective-permute-done.refs_1_), channel_id=1, source_target_pairs={{0,16},{4,20},{8,24},{12,28},{16,0},{20,4},{24,8},{28,12},{1,17},{... | collective-permute-start | bytes 165896 | tf_op jit(solution)/shard_map/ppermute | solution.py:471
  12.7 10.1 %all-to-all-start = ((bf16[32,8,128]{2,1,0:T(8,128)(2,1)}), bf16[32,8,128]{2,1,0:T(8,128)(2,1)S(1)}, u32[]{:S(2)}, u32[]{:S(2)}) async-start(bf16[32,8,128]{2,1,0:T(8,128)(2,1)} %get-tuple-element.38), calls=%async_computation | async-start | bytes 131072 | tf_op jit(solution)/shard_map/all_to_all | solution.py:467
  15.3 2.1 %copy-start = (bf16[32,864]{1,0:T(8,128)(2,1)S(1)}, bf16[32,864]{1,0:T(8,128)(2,1)}, u32[]{:S(2)}) copy-start(bf16[32,864]{1,0:T(8,128)(2,1)} %refs_0_.1) | copy-start | bytes 165892
  15.3 2.1 %copy-start.1 = (f32[128]{0:T(128)S(1)}, f32[128]{0:T(128)}, u32[]{:S(2)}) copy-start(f32[128]{0:T(128)} %param.11) | copy-start | bytes 1540
  15.3 2.1 %copy-start.2 = (f32[128]{0:T(128)S(1)}, f32[128]{0:T(128)}, u32[]{:S(2)}) copy-start(f32[128]{0:T(128)} %param.12) | copy-start | bytes 1540
  15.4 2.0 %collective-permute-start.3 = (bf16[32,864]{1,0:T(8,128)(2,1)}, bf16[32,864]{1,0:T(8,128)(2,1)S(1)}, u32[]{:S(2)}, u32[]{:S(2)}) collective-permute-start(bf16[32,864]{1,0:T(8,128)(2,1)} %refs_0_.1), channel_id=1, source_target_pairs={{0,4},{4,0},{8,12},{12,8},{16,20},{20,16},{24,28},{28,24},{1,5},{5... | collective-permute-start | bytes 165896 | tf_op jit(solution)/shard_map/ppermute | solution.py:432
  15.6 1.9 %collective-permute-start.4 = (bf16[32,864]{1,0:T(8,128)(2,1)S(1)}, bf16[32,864]{1,0:T(8,128)(2,1)S(1)}, u32[]{:S(2)}, u32[]{:S(2)}) collective-permute-start(bf16[32,864]{1,0:T(8,128)(2,1)S(1)} %collective-permute-done.refs_1_), channel_id=1, source_target_pairs={{0,4},{4,0},{8,12},{12,8},{16,20},{20,16},{24,28},{28,24},{1,5},{5... | collective-permute-start | bytes 165896 | tf_op jit(solution)/shard_map/ppermute | solution.py:432
  16.0 1.5 %collective-permute-start.5 = (bf16[32,864]{1,0:T(8,128)(2,1)S(1)}, bf16[32,864]{1,0:T(8,128)(2,1)S(1)}, u32[]{:S(2)}, u32[]{:S(2)}) collective-permute-start(bf16[32,864]{1,0:T(8,128)(2,1)S(1)} %collective-permute-done.1.refs_2_), channel_id=1, source_target_pairs={{0,4},{4,0},{8,12},{12,8},{16,20},{20,16},{24,28},{28,24},{1,5},{5... | collective-permute-start | bytes 165896 | tf_op jit(solution)/shard_map/ppermute | solution.py:432
  16.1 1.4 %collective-permute-start.6 = (bf16[32,864]{1,0:T(8,128)(2,1)S(1)}, bf16[32,864]{1,0:T(8,128)(2,1)S(1)}, u32[]{:S(2)}, u32[]{:S(2)}) collective-permute-start(bf16[32,864]{1,0:T(8,128)(2,1)S(1)} %collective-permute-done.2.refs_3_), channel_id=1, source_target_pairs={{0,4},{4,0},{8,12},{12,8},{16,20},{20,16},{24,28},{28,24},{1,5},{5... | collective-permute-start | bytes 165896 | tf_op jit(solution)/shard_map/ppermute | solution.py:432
  25.6 6.5 %collective-permute-start.10 = (bf16[4,32,1152]{2,1,0:T(8,128)(2,1)S(1)}, bf16[4,32,1152]{2,1,0:T(8,128)(2,1)S(1)}, u32[]{:S(2)}, u32[]{:S(2)}) collective-permute-start(bf16[4,32,1152]{2,1,0:T(8,128)(2,1)S(1)} %get-tuple-element.41), channel_id=1, source_target_pairs={{0,4},{4,0},{8,12},{12,8},{16,20},{20,16},{24,28},{28,24},{1,5},{5... | collective-permute-start | bytes 884744 | tf_op jit(solution)/shard_map/ppermute | solution.py:432
  25.7 9.8 %collective-permute-start.14 = (bf16[192,256]{1,0:T(8,128)(2,1)S(1)}, bf16[192,256]{1,0:T(8,128)(2,1)S(1)}, u32[]{:S(2)}, u32[]{:S(2)}) collective-permute-start(bf16[192,256]{1,0:T(8,128)(2,1)S(1)} %get-tuple-element.48), channel_id=1, source_target_pairs={{0,1},{1,2},{2,3},{3,0},{4,5},{5,6},{6,7},{7,4},{8,9},{9,10},{10,1... | collective-permute-start | bytes 294920 | tf_op jit(solution)/shard_map/ppermute | solution.py:418
  26.1 10.7 %collective-permute-start.15 = (bf16[192,256]{1,0:T(8,128)(2,1)S(1)}, bf16[192,256]{1,0:T(8,128)(2,1)S(1)}, u32[]{:S(2)}, u32[]{:S(2)}) collective-permute-start(bf16[192,256]{1,0:T(8,128)(2,1)S(1)} %get-tuple-element.49), channel_id=1, source_target_pairs={{0,2},{1,3},{2,0},{3,1},{4,6},{5,7},{6,4},{7,5},{8,10},{9,11},{10,... | collective-permute-start | bytes 294920 | tf_op jit(solution)/shard_map/ppermute | solution.py:418
  27.6 9.2 %collective-permute-start.16 = (bf16[192,256]{1,0:T(8,128)(2,1)S(1)}, bf16[192,256]{1,0:T(8,128)(2,1)S(1)}, u32[]{:S(2)}, u32[]{:S(2)}) collective-permute-start(bf16[192,256]{1,0:T(8,128)(2,1)S(1)} %get-tuple-element.50), channel_id=1, source_target_pairs={{0,3},{1,0},{2,1},{3,2},{4,7},{5,4},{6,5},{7,6},{8,11},{9,8},{10,9... | collective-permute-start | bytes 294920 | tf_op jit(solution)/shard_map/ppermute | solution.py:418
  29.6 12.6 %all-to-all-start.1 = ((bf16[32,16,128]{2,1,0:T(8,128)(2,1)}), bf16[32,16,128]{2,1,0:T(8,128)(2,1)S(1)}, u32[]{:S(2)}, u32[]{:S(2)}) async-start(bf16[32,16,128]{2,1,0:T(8,128)(2,1)} %get-tuple-element.39), calls=%async_computation.1 | async-start | bytes 262144 | tf_op jit(solution)/shard_map/all_to_all | solution.py:521
  32.3 5.6 %collective-permute-start.11 = (bf16[32,1152]{1,0:T(8,128)(2,1)S(1)}, bf16[32,1152]{1,0:T(8,128)(2,1)S(1)}, u32[]{:S(2)}, u32[]{:S(2)}) collective-permute-start(bf16[32,1152]{1,0:T(8,128)(2,1)S(1)} %get-tuple-element.43.after_ref), channel_id=1, source_target_pairs={{0,8},{4,12},{8,0},{12,4},{16,24},{20,28},{24,16},{28,20},{1,9},{5... | collective-permute-start | bytes 221192 | tf_op jit(solution)/shard_map/ppermute | solution.py:427
  34.0 5.4 %collective-permute-start.12 = (bf16[32,1152]{1,0:T(8,128)(2,1)S(1)}, bf16[32,1152]{1,0:T(8,128)(2,1)S(1)}, u32[]{:S(2)}, u32[]{:S(2)}) collective-permute-start(bf16[32,1152]{1,0:T(8,128)(2,1)S(1)} %get-tuple-element.44), channel_id=1, source_target_pairs={{0,16},{4,20},{8,24},{12,28},{16,0},{20,4},{24,8},{28,12},{1,17},{... | collective-permute-start | bytes 221192 | tf_op jit(solution)/shard_map/ppermute | solution.py:427
  35.5 5.6 %collective-permute-start.13 = (bf16[32,1152]{1,0:T(8,128)(2,1)S(1)}, bf16[32,1152]{1,0:T(8,128)(2,1)S(1)}, u32[]{:S(2)}, u32[]{:S(2)}) collective-permute-start(bf16[32,1152]{1,0:T(8,128)(2,1)S(1)} %get-tuple-element.45), channel_id=1, source_target_pairs={{0,24},{4,28},{8,16},{12,20},{16,8},{20,12},{24,0},{28,4},{1,25},{... | collective-permute-start | bytes 221192 | tf_op jit(solution)/shard_map/ppermute | solution.py:427

commit v4 on v3

--- a/solution.py
+++ b/solution.py
@@ -76,13 +76,34 @@
 
 
 def send_kernel(
-    dims, blocks_hbm, order_hbm, cot_hbm, out_ref, holds_ref, blocks_ref, order_ref, cot_ref, sems
+    dims,
+    blocks_hbm,
+    order_hbm,
+    cot_hbm,
+    out_ref,
+    holds_ref,
+    slots_ref,
+    blocks_ref,
+    order_ref,
+    cot_ref,
+    sems,
 ):
     devs, slab, slots, clips, held, och = dims
     pairs = [(blocks_hbm, blocks_ref), (order_hbm, order_ref), (cot_hbm, cot_ref)]
-    for copy in fetch(pairs, sems):
+    copies = fetch(pairs, sems)
+    out_ref[...] = jnp.zeros_like(out_ref)
+    for copy in copies:
         copy.wait()
     me = lax.axis_index("clips")
+    start = first_block_of(blocks_ref, me * held, clips)
+    for k in range(held):
+        count = blocks_ref[me * held + k]
+        for b in range(BMAX):
+            device = jnp.where(b < count, order_ref[jnp.mod(start + b, devs)], devs)
+            for d in range(devs):
+                hit = jnp.where(device == d, 1.0, 0.0)
+                slots_ref[(k * BMAX + b) * devs + d] = jnp.full((1, LANES), hit, F32)
+        start = start + count
     holders = slot_holders(blocks_ref, order_ref, me, slots, clips, held, devs)
     for q in range(slots):
         block = cot_ref[q].astype(F32)
@@ -140,11 +161,11 @@
     weights = shards[...].reshape(c_in, width).astype(BF16)
     weights = jnp.dot(weights, table_ref[...], preferred_element_type=F32).astype(BF16)
 
-    total = None
-    for b in range(3):
-        rows = video_pad[b : b + slab].reshape(many, c_in)
-        term = jnp.dot(rows, weights[:, 384 * b : 384 * (b + 1)], preferred_element_type=F32)
-        total = term if total is None else total + term
+    total = jnp.dot(
+        jnp.concatenate([video_pad[b : b + slab].reshape(many, c_in) for b in range(3)], axis=1),
+        jnp.concatenate([weights[:, 384 * b : 384 * (b + 1)] for b in range(3)], axis=0),
+        preferred_element_type=F32,
+    )
     mixed = (
         from_left(total[:, 0:LANES], columns)
         + total[:, LANES : 2 * LANES]
@@ -157,21 +178,27 @@
     bias = pltpu.roll(jnp.broadcast_to(bias_ref[...], (8, LANES)), shift, 1)[0:1, :och]
     block_rows = FB * columns
     copy.wait()
+    convs, kept, counts, limits = [], [], [], []
     for k in range(held):
         blocks = blocks_ref[me * held + k]
         conv = frame_shifts[0][:, k * per_clip : (k + 1) * per_clip]
         for a in (1, 2):
             part = frame_shifts[a][:, k * per_clip : (k + 1) * per_clip - a * columns]
             conv = conv + jnp.concatenate([jnp.zeros((slab, a * columns, och), F32), part], axis=1)
-        alive = frame_of < blocks * FB
+        convs.append(conv)
+        kept.append(jnp.where(frame_of < blocks * FB, conv, 0.0))
         count = (blocks * (FB * slab * columns * per_group)).astype(F32)
-        kept = jnp.where(alive, conv, 0.0)
-        mean = group_mean_of(kept, count, per_group)
-        var = group_mean_of(kept * conv, count, per_group) - mean * mean
-        inv_std = lax.rsqrt(var + 1e-05)
+        counts.append(jnp.full((1, och), count, F32))
+        limits.append(jnp.full((1, och), (blocks * FB).astype(F32), F32))
+    sums = group_sums(kept + [a * b for a, b in zip(kept, convs)], per_group)
+    for k in range(held):
+        conv = convs[k]
+        mean = sums[k] / counts[k]
+        inv_std = lax.rsqrt(sums[held + k] / counts[k] - mean * mean + 1e-05)
+        inv_ref[k] = jnp.concatenate([inv_std, counts[k], limits[k], jnp.zeros((5, och), F32)], axis=0)
+        mean, inv_std = mean[None], inv_std[None]
         normed = (conv - mean) * inv_std
         normed_ref[:, k * per_clip : (k + 1) * per_clip, :] = normed
-        inv_ref[k] = jnp.broadcast_to(inv_std[0], (8, och))
         affine = normed * gain[None] + bias[None]
         sigmoid = jax.nn.sigmoid(affine)
         act = affine * sigmoid
@@ -195,23 +222,28 @@
     return jnp.where(column < columns - 1, pltpu.roll(values, values.shape[0] - 1, 0), 0.0)
 
 
-def group_mean_of(values, count, per_group):
-    och = values.shape[-1]
-    same = lax.broadcasted_iota(jnp.int32, (och, och), 0) // per_group
-    same = (same == lax.broadcasted_iota(jnp.int32, (och, och), 1) // per_group).astype(F32)
-    sums = jnp.sum(jnp.sum(values, axis=0), axis=0, keepdims=True)
-    sums = jnp.broadcast_to(sums, (8, och))
-    sums = jnp.dot(sums, same, precision=lax.Precision.HIGHEST, preferred_element_type=F32)
-    return (sums[0:1] / count)[None]
-
-
-def backward_kernel(dims, blocks_hbm, order_hbm, gain_ref, weights_ref, *refs):
+def group_sums(arrays, per_group):
+    och = arrays[0].shape[-1]
+    rows = [jnp.sum(jnp.sum(a, axis=0), axis=0, keepdims=True) for a in arrays]
+    rows.append(jnp.zeros((-len(rows) % 8, och), F32))
+    total = jnp.concatenate([r for r in rows if r.shape[0]], axis=0)
+    if och < LANES:
+        total = jnp.concatenate([total, jnp.zeros((total.shape[0], LANES - och), F32)], axis=1)
+    lane = lax.broadcasted_iota(jnp.int32, total.shape, 1)
+    step = 1
+    while step < per_group:
+        down, up = pltpu.roll(total, LANES - step, 1), pltpu.roll(total, step, 1)
+        total = total + jnp.where((lane // step) % 2 == 0, down, up)
+        step *= 2
+    return [total[i : i + 1, :och] for i in range(len(arrays))]
+
+
+def backward_kernel(dims, slots_ref, gain_ref, weights_ref, *refs):
     devs, slab, clips, held, frames, columns, rows_in, cols, och, per_group = dims
     video_t_ref, normed_ref, inv_ref, slope_ref, act_in, cot_ref = refs[:6]
     act_hbm, keep_ref, send_ref = refs[6:9]
     video_grad_refs = refs[9 : 9 + slab]
-    act_ref, grad_ref, rows_ref, blocks_ref, order_ref, sems = refs[9 + slab :]
-    copies = fetch([(blocks_hbm, blocks_ref), (order_hbm, order_ref)], sems)
+    act_ref, grad_ref, rows_ref, sems = refs[9 + slab :]
     me, own = lax.axis_index("clips"), lax.axis_index("slab")
     places = held * frames * columns
     per_clip = frames * columns
@@ -222,38 +254,42 @@
     shift = jnp.mod(LANES - own * och, LANES)
     gain = pltpu.roll(jnp.broadcast_to(gain_ref[...], (8, LANES)), shift, 1)[0:1, :och]
     frame_of = lax.broadcasted_iota(jnp.int32, (slab, per_clip, och), 1) // columns
+    frame_of = frame_of.astype(F32)
     gain_part = jnp.zeros((1, och), F32)
     bias_part = jnp.zeros((1, och), F32)
-    for copy in copies:
-        copy.wait()
-    start = first_block_of(blocks_ref, me * held, clips)
-    conv_grads = []
-    act_blocks = []
+    blocks = [[None] * slab for _ in range(held * BMAX)]
+    for d in range(devs):
+        for s in range(slab):
+            folded = cot_ref[d * slab + s].astype(F32)
+            for j in range(held * BMAX):
+                term = folded * slots_ref[j * devs + d]
+                blocks[j][s] = term if d == 0 else blocks[j][s] + term
+    normeds, grads, alives = [], [], []
     for k in range(held):
-        blocks = blocks_ref[me * held + k]
         cot = []
         for b in range(BMAX):
-            device = order_ref[jnp.mod(start + b, devs)]
             rows = []
-            for s in range(slab):
-                folded = cot_ref[device * slab + s].astype(F32)
+            for folded in blocks[k * BMAX + b]:
                 parts = [folded[:, g * och : (g + 1) * och] for g in range(groups)]
                 rows.append(jnp.concatenate(parts, axis=0)[:block_rows])
             cot.append(jnp.stack(rows, axis=0))
         cot = jnp.concatenate(cot, axis=1)
-        alive = frame_of < blocks * FB
-        count = (blocks * (FB * slab * columns * per_group)).astype(F32)
-        inv_std = inv_ref[k][None, 0:1]
+        alive = frame_of < inv_ref[k][None, 2:3]
         normed = normed_ref[:, k * per_clip : (k + 1) * per_clip, :]
         slope = slope_ref[:, k * per_clip : (k + 1) * per_clip, :]
         grad_affine = jnp.where(alive, cot * slope, 0.0)
         gain_part += jnp.sum(jnp.sum(grad_affine * normed, axis=0), axis=0, keepdims=True)
         bias_part += jnp.sum(jnp.sum(grad_affine, axis=0), axis=0, keepdims=True)
-        grad_normed = grad_affine * gain[None]
-        mean_grad = group_mean_of(grad_normed, count, per_group)
-        mean_cross = group_mean_of(grad_normed * normed, count, per_group)
-        grad_conv = inv_std * (grad_normed - mean_grad - normed * mean_cross)
-        grad_conv = jnp.where(alive, grad_conv, 0.0).astype(BF16).astype(F32)
+        normeds.append(normed)
+        grads.append(grad_affine * gain[None])
+        alives.append(alive)
+    sums = group_sums(grads + [a * b for a, b in zip(grads, normeds)], per_group)
+    conv_grads = []
+    for k in range(held):
+        inv_std, count = inv_ref[k][None, 0:1], inv_ref[k][1:2]
+        mean_grad, mean_cross = (sums[k] / count)[None], (sums[held + k] / count)[None]
+        grad_conv = inv_std * (grads[k] - mean_grad - normeds[k] * mean_cross)
+        grad_conv = jnp.where(alives[k], grad_conv, 0.0).astype(BF16).astype(F32)
         lanes = [grad_conv]
         for a in (1, 2):
             zeros = jnp.zeros((slab, a * columns, och), F32)
@@ -261,25 +297,19 @@
         if LANES > 3 * och:
             lanes.append(jnp.zeros((slab, per_clip, LANES - 3 * och), F32))
         conv_grads.append(jnp.concatenate(lanes, axis=2))
-        for b in range(BMAX):
-            device = order_ref[jnp.mod(start + b, devs)]
-            for h in range(slab):
-                act_blocks.append((b < blocks, device * slab + h, act_in[k * BMAX + b, h]))
-        start = start + blocks
 
     sums = split3(gain_part) + split3(bias_part) + [jnp.zeros((2, och), F32)]
     sums = jnp.concatenate(sums, axis=0)
     sums = jnp.concatenate([sums, jnp.zeros((8, LANES - och), F32)], axis=1)
-    nothing = jnp.concatenate([jnp.zeros_like(act_blocks[0][2]), sums], axis=0).astype(BF16)
-    for d in range(devs * slab):
-        act_ref[d] = nothing
-    for alive, dest, block in act_blocks:
-
-        @pl.when(alive)
-        def _(dest=dest, block=block):
-            act_ref[dest] = jnp.concatenate([block, sums], axis=0).astype(BF16)
-
-    act_copy = pltpu.make_async_copy(act_ref, act_hbm, sems.at[2])
+    for d in range(devs):
+        for h in range(slab):
+            total = None
+            for j in range(held * BMAX):
+                term = act_in[j, h] * slots_ref[j * devs + d]
+                total = term if total is None else total + term
+            act_ref[d * slab + h] = jnp.concatenate([total, sums], axis=0).astype(BF16)
+
+    act_copy = pltpu.make_async_copy(act_ref, act_hbm, sems.at[0])
     act_copy.start()
 
     grads = jnp.concatenate(conv_grads, axis=1).reshape(many, LANES)
@@ -289,23 +319,15 @@
         shifted = shifted.astype(BF16).reshape(slab, places, LANES)
         grad_ref[1 : slab + 1, :, e * LANES : (e + 1) * LANES] = shifted
 
-    total = None
-    for b in range(3):
-        term = jnp.dot(
-            grad_ref[2 - b : 2 - b + slab].reshape(many, 3 * LANES),
-            weights_ref[384 * b : 384 * (b + 1)],
-            preferred_element_type=F32,
-        )
-        total = term if total is None else total + term
+    moved = [grad_ref[2 - b : 2 - b + slab].reshape(many, 3 * LANES) for b in range(3)]
+    moved = jnp.concatenate(moved, axis=1)
+    total = jnp.dot(moved, weights_ref[...], preferred_element_type=F32)
     rows_ref[...] = total.reshape(slab, places, c_in)
     for i, ref in enumerate(video_grad_refs):
         ref[...] = rows_ref[jnp.mod(own + i, slab)].astype(ref.dtype)
 
-    parts = []
-    for b in range(3):
-        moved = grad_ref[2 - b : 2 - b + slab].reshape(many, 3 * LANES)
-        parts.append(jnp.dot(video_t_ref[...], moved, preferred_element_type=F32))
-    terms = jnp.concatenate(parts, axis=1).reshape(devs // 2, 2 * rows_in, 9 * LANES)
+    terms = jnp.dot(video_t_ref[...], moved, preferred_element_type=F32)
+    terms = terms.reshape(devs // 2, 2 * rows_in, 9 * LANES)
     low, high = terms[:, :rows_in], terms[:, rows_in:]
     odd = me % 2 == 1
     keep_ref[...] = jnp.where(odd, high, low)
@@ -324,9 +346,13 @@
 
 def pair_kernel(chips, keep_ref, other_ref, *outs):
     me = lax.axis_index("clips") // 2
+    cols = outs[0].shape[1]
+    used = cols // 9
     for t, ref in enumerate(outs):
         chip = partner(me, t, chips)
-        ref[...] = (keep_ref[chip] + other_ref[chip].astype(F32)).astype(ref.dtype)
+        total = keep_ref[chip] + other_ref[chip].astype(F32)
+        parts = [total[:, g * LANES : g * LANES + used] for g in range(9)]
+        ref[...] = jnp.concatenate(parts, axis=1).astype(ref.dtype)
 
 
 def sum_kernel(*refs):
@@ -338,21 +364,31 @@
 
 def table_kernel(och, after_ref, table_ref):
     rows, cols = table_ref.shape
-    lane = lax.broadcasted_iota(jnp.int32, (LANES, LANES), 0)
-    source = jnp.where(lane < 3 * och, 27 * (lane % och) + 9 * (2 - lane // och), -cols)
-    ahead = source - lax.broadcasted_iota(jnp.int32, (LANES, LANES), 1)
-    for group in range(rows // LANES):
+    place = lax.broadcasted_iota(jnp.int32, (LANES, LANES), 0)
+    column = lax.broadcasted_iota(jnp.int32, (LANES, LANES), 1)
+    for i in range(0, rows, LANES):
+        inner = (place + i) % (3 * och)
+        source = 27 * (inner % och) + 9 * (2 - inner // och) + (place + i) // (3 * och)
+        ahead = jnp.where(place + i < 27 * och, source, -cols) - column
         for j in range(0, cols, LANES):
-            hit = jnp.where(ahead == j - group, 1.0, 0.0).astype(BF16)
-            table_ref[group * LANES : (group + 1) * LANES, j : j + LANES] = hit
-
-
-def weights_kernel(*refs):
-    kernel_refs, table_ref, kernel_grad_ref = refs[:-2], refs[-2], refs[-1]
+            table_ref[i : i + LANES, j : j + LANES] = jnp.where(ahead == j, 1.0, 0.0).astype(BF16)
+
+
+def finish_kernel(dims, holds_ref, act_in, table_ref, *refs):
+    devs, slab, slots, och = dims
+    chips = devs // 2
+    kernel_refs, hbm_refs = refs[:chips], refs[chips : chips + 4]
+    out_refs, sems = refs[chips + 4 : chips + 8], refs[chips + 8]
+    kernel_grad_ref, act_ref, gain_ref, bias_ref = out_refs
+    copies = [pltpu.make_async_copy(a, b, sems.at[i]) for i, (a, b) in enumerate(zip(out_refs, hbm_refs))]
+
     total = kernel_refs[0][...]
     for ref in kernel_refs[1:]:
         total = total + ref[...].astype(F32)
-    rows, cols = kernel_grad_ref.shape
+    rows, cols = total.shape
+    width = table_ref.shape[0]
+    if width > cols:
+        total = jnp.concatenate([total, jnp.zeros((rows, width - cols), F32)], axis=1)
     native = jnp.dot(
         jnp.concatenate(split3(total), axis=0).astype(BF16),
         table_ref[...],
@@ -360,11 +396,8 @@
     )
     native = native[:rows] + (native[rows : 2 * rows] + native[2 * rows :])
     kernel_grad_ref[...] = native[:, :cols]
-
-
-def finish_kernel(dims, holds_ref, act_in, after_ref, *refs):
-    devs, slab, slots, och = dims
-    hbm_refs, (act_ref, gain_ref, bias_ref), sems = refs[:3], refs[3:6], refs[6]
+    copies[0].start()
+
     groups = LANES // och
     rows = act_in.shape[1] - 8
     sums = []
@@ -377,19 +410,18 @@
             for q in range(slots):
                 blocks[q][s] = blocks[q][s] + both[:rows] * holds_ref[q * devs + d]
         sums.append(part[:, :och])
-    sums = jnp.concatenate(sums, axis=1)
-    gain_ref[...] = sums[0:1] + (sums[1:2] + sums[2:3])
-    bias_ref[...] = sums[3:4] + (sums[4:5] + sums[5:6])
-    copies = [pltpu.make_async_copy(a, b, sems.at[i]) for i, (a, b) in enumerate(zip(refs[3:6], hbm_refs))]
-    copies[1].start()
-    copies[2].start()
     for q in range(slots):
         block = []
         for g in range(groups):
             parts = [p[:, g * och : (g + 1) * och] for p in blocks[q]]
             block.append(jnp.concatenate(parts, axis=1))
         act_ref[q] = jnp.concatenate(block, axis=0)[: act_ref.shape[1]].astype(BF16)
-    copies[0].start()
+    copies[1].start()
+    sums = jnp.concatenate(sums, axis=1)
+    gain_ref[...] = sums[0:1] + (sums[1:2] + sums[2:3])
+    bias_ref[...] = sums[3:4] + (sums[4:5] + sums[5:6])
+    copies[2].start()
+    copies[3].start()
     for copy in copies:
         copy.wait()
 
@@ -457,9 +489,10 @@
     )
 
     videos = shifts([video.reshape(places, c_in)] * slab, "slab")
-    cots, holds = call(
+    cots, holds, slot_of = call(
         functools.partial(send_kernel, (devs, slab, slots, clips, held, och)),
-        [shape((devs * slab, fold_rows, LANES), BF16), shape((slots * devs, 1, LANES), F32)],
+        [shape((devs * slab, fold_rows, LANES), BF16), shape((slots * devs, 1, LANES), F32)]
+        + [shape((held * BMAX * devs, 1, LANES), F32)],
         [HBM, HBM, HBM],
         smem + [pltpu.VMEM((slots, block_rows, c_out), BF16), pltpu.SemaphoreType.DMA((3,))],
         cost=pl.CostEstimate(flops=FIRST, bytes_accessed=0, transcendentals=0),
@@ -505,27 +538,26 @@
             shape((chips, rows_in, 9 * LANES), BF16),
         ]
         + [shape((places, c_in), F32 if i == 0 else BF16) for i in range(slab)],
-        [HBM, HBM] + [VMEM] * 8,
+        [VMEM] * 9,
         [
             pltpu.VMEM((devs * slab, fold_rows + 8, LANES), BF16),
             pltpu.VMEM((slab + 2, places, 3 * LANES), BF16),
             pltpu.VMEM((slab, places, c_in), F32),
-        ]
-        + smem
-        + [pltpu.SemaphoreType.DMA((3,))],
+            pltpu.SemaphoreType.DMA((1,)),
+        ],
         large,
         [HBM] + [VMEM] * (2 + slab),
-    )(clip_blocks, deal_order, gain, weights, video_t, normed, inv_std, slope, act, cots)
+    )(slot_of, gain, weights, video_t, normed, inv_std, slope, act, cots)
     video_grads = shifts(video_grads, "slab")
     send = core_swap(send, "clips")
     acts = lax.all_to_all(acts, everyone, split_axis=0, concat_axis=0, tiled=True)
     kernel_grads = call(
         functools.partial(pair_kernel, chips),
-        [shape((rows_in, 9 * LANES), F32 if t == 0 else BF16) for t in range(chips)],
+        [shape((rows_in, cols), F32 if t == 0 else BF16) for t in range(chips)],
         [VMEM, VMEM],
     )(keep, send)
     table = call(
-        functools.partial(table_kernel, och), [shape((9 * LANES, width), BF16)], [ANY]
+        functools.partial(table_kernel, och), [shape((width, width), BF16)], [ANY]
     )(kernel_grads[1])[0]
     kernel_grads = chip_swaps(kernel_grads, "clips")
 
@@ -535,29 +567,20 @@
         [VMEM] * slab,
         cost=pl.CostEstimate(flops=STAGE, bytes_accessed=0, transcendentals=0),
     )(*video_grads)[0]
-    kernel_grad = call(
-        weights_kernel,
-        [shape((rows_in, cols), F32)],
-        [VMEM] * (chips + 1),
-        limit=2 * slab * MIB,
-        cost=pl.CostEstimate(flops=STAGE, bytes_accessed=0, transcendentals=0),
-    )(*kernel_grads, table)[0]
-    act, gain_grad, bias_grad = call(
+    outs = [
+        ((rows_in, cols), F32),
+        ((slots, block_rows, c_out), BF16),
+        ((1, c_out), F32),
+        ((1, c_out), F32),
+    ]
+    kernel_grad, act, gain_grad, bias_grad = call(
         functools.partial(finish_kernel, (devs, slab, slots, och)),
-        [
-            pltpu.HBM((slots, block_rows, c_out), BF16),
-            pltpu.HBM((1, c_out), F32),
-            pltpu.HBM((1, c_out), F32),
-        ],
-        [VMEM, VMEM, HBM],
-        [
-            pltpu.VMEM((slots, block_rows, c_out), BF16),
-            pltpu.VMEM((1, c_out), F32),
-            pltpu.VMEM((1, c_out), F32),
-            pltpu.SemaphoreType.DMA((3,)),
-        ],
-        out_specs=[HBM] * 3,
-    )(holds, acts, pltpu.with_memory_space_constraint(kernel_grad, pltpu.HBM))
+        [pltpu.HBM(*out) for out in outs],
+        [VMEM] * (3 + chips),
+        [pltpu.VMEM(*out) for out in outs] + [pltpu.SemaphoreType.DMA((4,))],
+        2 * slab * MIB,
+        [HBM] * 4,
+    )(holds, acts, table, *kernel_grads)
     return (
         act.reshape(cotangent.shape),
         video_grad.reshape(video.shape),

time: 43.3 us -> 41.6 us (0.961)
  Pallas kernels: 11.1 us -> 10.1 us
  waiting for transfers between devices: 6.68 us -> 6 us
    ppermute x3, waiting for transfers between devices: 3.15 us -> 0.05 us  [chip_swaps(): moved.append(lax.ppermute(arrays[t], axis, pairs))]
    all_to_all x1, waiting for transfers between devices: 0.01 us -> 2.52 us  [body(): lax.all_to_all(acts, everyone, split_axis=0, concat_axis=0, tiled=True)]
    pallas_call x1, Pallas kernels: 2.81 us -> 1.9 us  [body(): call(functools.partial(backward_kernel, dims), [pltpu.HBM((devs * slab, f...]
    pallas_call x3 -> x2, Pallas kernels: 1.58 us -> 1.04 us  [the longest x1 0.88 us: body(): call(functools.partial(table_kernel, och), [shape((width, width), BF16)],...]
  transfers between devices with their start and end apart: 19 -> 19, of which waited for: 4 -> 3; matrix products, arithmetic and copies ran while one was open for 0% -> 0% of each run, Pallas kernels for 18% -> 17%
where the time goes in v4:
time: 41.6 us; the launch traced here: 41.3 us
  starting transfers between devices  24.3 us (58%)
  Pallas kernels  10.1 us (24%)
  waiting for transfers between devices  6 us (14%)
  between operations  0.81 us (2%)
    ppermute x6, starting transfers between devices, shifts(): lax.ppermute(arrays[i], axis, [(j, (j + i) % size) for j in range(size)])  9.39 us
    ppermute x3, starting transfers between devices, body(): shards = shards + [lax.ppermute(shard, 'clips', pairs) for shard in shards]  5.03 us
    ppermute x3, starting transfers between devices, chip_swaps(): moved.append(lax.ppermute(arrays[t], axis, pairs))  3.55 us
    pallas_call x1, Pallas kernels, body(): call(functools.partial(forward_kernel, dims), [shape((9 * LANES, c_in), B...  2.9 us
    all_to_all x1, starting transfers between devices, body(): lax.all_to_all(cots, everyone, split_axis=0, concat_axis=0, tiled=True)  2.59 us
    all_to_all x1, starting transfers between devices, body(): lax.all_to_all(acts, everyone, split_axis=0, concat_axis=0, tiled=True)  2.57 us
    all_to_all x1, waiting for transfers between devices, body(): lax.all_to_all(acts, everyone, split_axis=0, concat_axis=0, tiled=True)  2.52 us
    all_to_all x1, waiting for transfers between devices, body(): lax.all_to_all(cots, everyone, split_axis=0, concat_axis=0, tiled=True)  2.45 us
  transfers between devices with their start and end apart: 19, of which 3 were waited for; matrix products, arithmetic and copies ran while one was open for 0% of the time, Pallas kernels for 17%

profile of v4, /device:TPU:0, one launch (start us, length us, event | category | flops | bytes accessed | tf_op | source)
XLA Modules:
  0.0 41.3 jit_solution(17792340162906966558)
XLA Ops:
  0.6 3.0 %collective-permute-start = (bf16[32,864]{1,0:T(8,128)(2,1)}, bf16[32,864]{1,0:T(8,128)(2,1)S(1)}, u32[]{:S(2)}, u32[]{:S(2)}) collective-permute-start(bf16[32,864]{1,0:T(8,128)(2,1)} %refs_0_.1), channel_id=1, source_target_pairs={{0,8},{4,12},{8,0},{12,4},{16,24},{20,28},{24,16},{28,20},{1,9},{5... | collective-permute-start | bytes 165896 | tf_op jit(solution)/shard_map/ppermute | solution.py:504
  3.6 1.6 %collective-permute-start.7 = (bf16[192,256]{1,0:T(8,128)(2,1)}, bf16[192,256]{1,0:T(8,128)(2,1)S(1)}, u32[]{:S(2)}, u32[]{:S(2)}) collective-permute-start(bf16[192,256]{1,0:T(8,128)(2,1)} %bitcast.16), channel_id=1, source_target_pairs={{0,1},{1,2},{2,3},{3,0},{4,5},{5,6},{6,7},{7,4},{8,9},{9,10},{10,1... | collective-permute-start | bytes 294920 | tf_op jit(solution)/shard_map/ppermute | solution.py:450
  5.2 2.6 %collective-permute-start.8 = (bf16[192,256]{1,0:T(8,128)(2,1)}, bf16[192,256]{1,0:T(8,128)(2,1)S(1)}, u32[]{:S(2)}, u32[]{:S(2)}) collective-permute-start(bf16[192,256]{1,0:T(8,128)(2,1)} %bitcast.17), channel_id=1, source_target_pairs={{0,2},{1,3},{2,0},{3,1},{4,6},{5,7},{6,4},{7,5},{8,10},{9,11},{10,... | collective-permute-start | bytes 294920 | tf_op jit(solution)/shard_map/ppermute | solution.py:450
  7.8 1.3 %collective-permute-start.9 = (bf16[192,256]{1,0:T(8,128)(2,1)}, bf16[192,256]{1,0:T(8,128)(2,1)S(1)}, u32[]{:S(2)}, u32[]{:S(2)}) collective-permute-start(bf16[192,256]{1,0:T(8,128)(2,1)} %bitcast.18), channel_id=1, source_target_pairs={{0,3},{1,0},{2,1},{3,2},{4,7},{5,4},{6,5},{7,6},{8,11},{9,8},{10,9... | collective-permute-start | bytes 294920 | tf_op jit(solution)/shard_map/ppermute | solution.py:450
  9.2 1.5 %collective-permute-start.1 = (bf16[32,864]{1,0:T(8,128)(2,1)}, bf16[32,864]{1,0:T(8,128)(2,1)S(1)}, u32[]{:S(2)}, u32[]{:S(2)}) collective-permute-start(bf16[32,864]{1,0:T(8,128)(2,1)} %refs_0_.1), channel_id=1, source_target_pairs={{0,16},{4,20},{8,24},{12,28},{16,0},{20,4},{24,8},{28,12},{1,17},{... | collective-permute-start | bytes 165896 | tf_op jit(solution)/shard_map/ppermute | solution.py:504
  10.7 0.5 %collective-permute-start.2 = (bf16[32,864]{1,0:T(8,128)(2,1)S(1)}, bf16[32,864]{1,0:T(8,128)(2,1)S(1)}, u32[]{:S(2)}, u32[]{:S(2)}) collective-permute-start(bf16[32,864]{1,0:T(8,128)(2,1)S(1)} %collective-permute-done.refs_1_), channel_id=1, source_target_pairs={{0,16},{4,20},{8,24},{12,28},{16,0},{20,4},{24,8},{28,12},{1,17},{... | collective-permute-start | bytes 165896 | tf_op jit(solution)/shard_map/ppermute | solution.py:504
  11.2 1.6 %shard_map.110 = (bf16[32,8,128]{2,1,0:T(8,128)(2,1)}, f32[32,1,128]{2,1,0:T(1,128)S(1)}, f32[48,1,128]{2,1,0:T(1,128)S(1)}) custom-call(s32[16]{0:T(128)} %blocks_hbm.3, s32[8]{0:T(128)} %order_hbm.1, bf16[4,32,128]{2,1,0:T(8,128)(2,1)} %bitcast.15), custom_call_target="tpu_custom_call" | custom-call | flops 1000000 | tf_op jit(solution)/shard_map/pallas_call | solution.py:492
  12.8 2.6 %all-to-all-start = ((bf16[32,8,128]{2,1,0:T(8,128)(2,1)}), bf16[32,8,128]{2,1,0:T(8,128)(2,1)S(1)}, u32[]{:S(2)}, u32[]{:S(2)}) async-start(bf16[32,8,128]{2,1,0:T(8,128)(2,1)} %get-tuple-element.41), calls=%async_computation | async-start | bytes 131072 | tf_op jit(solution)/shard_map/all_to_all | solution.py:500
  15.6 0.4 collective-permute-start.4
  16.1 0.4 collective-permute-start.6
  16.5 0.9 %shard_map.111 = (bf16[6,192,256]{2,1,0:T(8,128)(2,1)S(1)}, bf16[896,1152]{1,0:T(8,128)(2,1)S(1)}) custom-call(bf16[192,256]{1,0:T(8,128)(2,1)} %bitcast.19, bf16[192,256]{1,0:T(8,128)(2,1)S(1)} %collective-permute-done.7.refs_1_, bf16[192,256]{1,0:T(8,128)(2,1)S(1)} %collective-permute-done.8.refs_2_, bf16[192,256]{1,0:T(8,128)(2,1)S(1)} %collective-permute-done.9.refs_3_), custom_call_target="tpu_custom_call" | custom-call | flops 10000000000 | tf_op jit(solution)/shard_map/pallas_call | solution.py:508
  17.5 2.9 %shard_map.112 = (bf16[1152,256]{1,0:T(8,128)(2,1)S(1)}, bf16[256,768]{1,0:T(8,128)(2,1)S(1)}, f32[4,192,32]{2,1,0:T(8,128)S(1)}, f32[2,8,32]{2,1,0:T(8,128)S(1)...) custom-call(s32[16]{0:T(128)} %blocks_hbm.3, f32[1,128]{1,0:T(1,128)S(1)} %bitcast.12, f32[1,128]{1,0:T(1,128)S(1)} %bitcast.14, ...), custom_call_target="tpu_custom_call" | custom-call | tf_op jit(solution)/shard_map/pallas_call | solution.py:515
  20.4 2.4 %all-to-all-done.refs_5_ = bf16[32,8,128]{2,1,0:T(8,128)(2,1)S(1)} async-done(((bf16[32,8,128]{2,1,0:T(8,128)(2,1)}), bf16[32,8,128]{2,1,0:T(8,128)(2,1)S(1)}, u32[]{:S(2)}, u32[]{:S(2)}) %all-to-all-start) | async-done | bytes 65568 | tf_op jit(solution)/shard_map/all_to_all | solution.py:500
  22.9 1.9 %shard_map.113 = (bf16[32,16,128]{2,1,0:T(8,128)(2,1)}, f32[4,32,1152]{2,1,0:T(8,128)S(1)}, bf16[4,32,1152]{2,1,0:T(8,128)(2,1)S(1)}, f32[192,256]{1,0:T(8,128)S...) custom-call(f32[48,1,128]{2,1,0:T(1,128)S(1)} %get-tuple-element.32.slots_ref, ...), custom_call_target="tpu_custom_call" | custom-call | tf_op jit(solution)/shard_map/pallas_call | solution.py:533
  25.3 1.6 %collective-permute-start.15 = (bf16[192,256]{1,0:T(8,128)(2,1)S(1)}, bf16[192,256]{1,0:T(8,128)(2,1)S(1)}, u32[]{:S(2)}, u32[]{:S(2)}) collective-permute-start(bf16[192,256]{1,0:T(8,128)(2,1)S(1)} %get-tuple-element.52), channel_id=1, source_target_pairs={{0,2},{1,3},{2,0},{3,1},{4,6},{5,7},{6,4},{7,5},{8,10},{9,11},{10,... | collective-permute-start | bytes 294920 | tf_op jit(solution)/shard_map/ppermute | solution.py:450
  26.9 1.9 %collective-permute-start.16 = (bf16[192,256]{1,0:T(8,128)(2,1)S(1)}, bf16[192,256]{1,0:T(8,128)(2,1)S(1)}, u32[]{:S(2)}, u32[]{:S(2)}) collective-permute-start(bf16[192,256]{1,0:T(8,128)(2,1)S(1)} %get-tuple-element.53), channel_id=1, source_target_pairs={{0,3},{1,0},{2,1},{3,2},{4,7},{5,4},{6,5},{7,6},{8,11},{9,8},{10,9... | collective-permute-start | bytes 294920 | tf_op jit(solution)/shard_map/ppermute | solution.py:450
  28.8 2.6 %all-to-all-start.1 = ((bf16[32,16,128]{2,1,0:T(8,128)(2,1)}), bf16[32,16,128]{2,1,0:T(8,128)(2,1)S(1)}, u32[]{:S(2)}, u32[]{:S(2)}) async-start(bf16[32,16,128]{2,1,0:T(8,128)(2,1)} %get-tuple-element.42), calls=%async_computation.1 | async-start | bytes 262144 | tf_op jit(solution)/shard_map/all_to_all | solution.py:553
  31.5 1.8 %collective-permute-start.11 = (bf16[32,864]{1,0:T(8,128)(2,1)S(1)}, bf16[32,864]{1,0:T(8,128)(2,1)S(1)}, u32[]{:S(2)}, u32[]{:S(2)}) collective-permute-start(bf16[32,864]{1,0:T(8,128)(2,1)S(1)} %get-tuple-element.45.after_ref), channel_id=1, source_target_pairs={{0,8},{4,12},{8,0},{12,4},{16,24},{20,28},{24,16},{28,20},{1,9},{5... | collective-permute-start | bytes 165896 | tf_op jit(solution)/shard_map/ppermute | solution.py:459
  33.3 1.5 %collective-permute-start.12 = (bf16[32,864]{1,0:T(8,128)(2,1)S(1)}, bf16[32,864]{1,0:T(8,128)(2,1)S(1)}, u32[]{:S(2)}, u32[]{:S(2)}) collective-permute-start(bf16[32,864]{1,0:T(8,128)(2,1)S(1)} %get-tuple-element.47), channel_id=1, source_target_pairs={{0,16},{4,20},{8,24},{12,28},{16,0},{20,4},{24,8},{28,12},{1,17},{... | collective-permute-start | bytes 165896 | tf_op jit(solution)/shard_map/ppermute | solution.py:459
  35.1 0.9 %collective-permute-done.15.refs_2_ = bf16[192,256]{1,0:T(8,128)(2,1)S(1)} collective-permute-done((bf16[192,256]{1,0:T(8,128)(2,1)S(1)}, bf16[192,256]{1,0:T(8,128)(2,1)S(1)}, u32[]{:S(2)}, u32[]{:S(2)}) %collective-permute-start.15) | collective-permute-done | bytes 98336 | tf_op jit(solution)/shard_map/ppermute | solution.py:450
  36.0 0.7 %shard_map.117 = bf16[192,256]{1,0:T(8,128)(2,1)} custom-call(f32[192,256]{1,0:T(8,128)S(1)} %get-tuple-element.50.refs_0_, bf16[192,256]{1,0:T(8,128)(2,1)S(1)} %collective-permute-done.14.refs_1_, bf16[192,256]{1,0:T(8,128)(2,1)S(1)} %collective-permute-done.15.refs_2_, bf16[192,256]{1,0:T(8,128)(2,1)S(1)} %collective-permute-done.16.refs_3_), custom_call_target="tpu_custom_call" | custom-call | flops 10000000000 | tf_op jit(solution)/shard_map/pallas_call | solution.py:564
  36.7 0.9 %shard_map.115.table_ref = bf16[896,896]{1,0:T(8,128)(2,1)S(1)} custom-call(bf16[32,864]{1,0:T(8,128)(2,1)S(1)} %get-tuple-element.45.after_ref), custom_call_target="tpu_custom_call" | custom-call | tf_op jit(solution)/shard_map/pallas_call | solution.py:559
  37.6 2.5 %all-to-all-done.1.act_in = bf16[32,16,128]{2,1,0:T(8,128)(2,1)S(1)} async-done(((bf16[32,16,128]{2,1,0:T(8,128)(2,1)}), bf16[32,16,128]{2,1,0:T(8,128)(2,1)S(1)}, u32[]{:S(2)}, u32[]{:S(2)}) %all-to-all-start.1) | async-done | bytes 131104 | tf_op jit(solution)/shard_map/all_to_all | solution.py:553
  40.2 1.1 %shard_map.116 = (f32[32,864]{1,0:T(8,128)}, bf16[4,32,128]{2,1,0:T(8,128)(2,1)}, f32[1,128]{1,0:T(1,128)}, f32[1,128]{1,0:T(1,128)}) custom-call(f32[32,1,128]{2,1,0:T(1,128)S(1)} %get-tuple-element.31.holds_ref, bf16[32,16,128]{2,1,0:T(8,128)(2,1)S(1)} %all-to-all-done.1.act_in, bf16[896,896]{1,0:T(8,128)(2,1)S(1)} %shard_map.115.table_ref, ...), custom_call_target="tpu_custom_call" | custom-call | tf_op jit(solution)/shard_map/pallas_call | solution.py:576
  (28 shorter events, 1.3 us)
Async XLA Ops:
  0.6 10.0 %collective-permute-start = (bf16[32,864]{1,0:T(8,128)(2,1)}, bf16[32,864]{1,0:T(8,128)(2,1)S(1)}, u32[]{:S(2)}, u32[]{:S(2)}) collective-permute-start(bf16[32,864]{1,0:T(8,128)(2,1)} %refs_0_.1), channel_id=1, source_target_pairs={{0,8},{4,12},{8,0},{12,4},{16,24},{20,28},{24,16},{28,20},{1,9},{5... | collective-permute-start | bytes 165896 | tf_op jit(solution)/shard_map/ppermute | solution.py:504
  3.6 12.0 %collective-permute-start.7 = (bf16[192,256]{1,0:T(8,128)(2,1)}, bf16[192,256]{1,0:T(8,128)(2,1)S(1)}, u32[]{:S(2)}, u32[]{:S(2)}) collective-permute-start(bf16[192,256]{1,0:T(8,128)(2,1)} %bitcast.16), channel_id=1, source_target_pairs={{0,1},{1,2},{2,3},{3,0},{4,5},{5,6},{6,7},{7,4},{8,9},{9,10},{10,1... | collective-permute-start | bytes 294920 | tf_op jit(solution)/shard_map/ppermute | solution.py:450
  5.2 10.8 %collective-permute-start.8 = (bf16[192,256]{1,0:T(8,128)(2,1)}, bf16[192,256]{1,0:T(8,128)(2,1)S(1)}, u32[]{:S(2)}, u32[]{:S(2)}) collective-permute-start(bf16[192,256]{1,0:T(8,128)(2,1)} %bitcast.17), channel_id=1, source_target_pairs={{0,2},{1,3},{2,0},{3,1},{4,6},{5,7},{6,4},{7,5},{8,10},{9,11},{10,... | collective-permute-start | bytes 294920 | tf_op jit(solution)/shard_map/ppermute | solution.py:450
  7.8 8.7 %collective-permute-start.9 = (bf16[192,256]{1,0:T(8,128)(2,1)}, bf16[192,256]{1,0:T(8,128)(2,1)S(1)}, u32[]{:S(2)}, u32[]{:S(2)}) collective-permute-start(bf16[192,256]{1,0:T(8,128)(2,1)} %bitcast.18), channel_id=1, source_target_pairs={{0,3},{1,0},{2,1},{3,2},{4,7},{5,4},{6,5},{7,6},{8,11},{9,8},{10,9... | collective-permute-start | bytes 294920 | tf_op jit(solution)/shard_map/ppermute | solution.py:450
  9.2 6.3 %collective-permute-start.1 = (bf16[32,864]{1,0:T(8,128)(2,1)}, bf16[32,864]{1,0:T(8,128)(2,1)S(1)}, u32[]{:S(2)}, u32[]{:S(2)}) collective-permute-start(bf16[32,864]{1,0:T(8,128)(2,1)} %refs_0_.1), channel_id=1, source_target_pairs={{0,16},{4,20},{8,24},{12,28},{16,0},{20,4},{24,8},{28,12},{1,17},{... | collective-permute-start | bytes 165896 | tf_op jit(solution)/shard_map/ppermute | solution.py:504
  10.7 5.5 %collective-permute-start.2 = (bf16[32,864]{1,0:T(8,128)(2,1)S(1)}, bf16[32,864]{1,0:T(8,128)(2,1)S(1)}, u32[]{:S(2)}, u32[]{:S(2)}) collective-permute-start(bf16[32,864]{1,0:T(8,128)(2,1)S(1)} %collective-permute-done.refs_1_), channel_id=1, source_target_pairs={{0,16},{4,20},{8,24},{12,28},{16,0},{20,4},{24,8},{28,12},{1,17},{... | collective-permute-start | bytes 165896 | tf_op jit(solution)/shard_map/ppermute | solution.py:504
  12.8 10.1 %all-to-all-start = ((bf16[32,8,128]{2,1,0:T(8,128)(2,1)}), bf16[32,8,128]{2,1,0:T(8,128)(2,1)S(1)}, u32[]{:S(2)}, u32[]{:S(2)}) async-start(bf16[32,8,128]{2,1,0:T(8,128)(2,1)} %get-tuple-element.41), calls=%async_computation | async-start | bytes 131072 | tf_op jit(solution)/shard_map/all_to_all | solution.py:500
  15.4 2.1 %copy-start = (bf16[32,864]{1,0:T(8,128)(2,1)S(1)}, bf16[32,864]{1,0:T(8,128)(2,1)}, u32[]{:S(2)}) copy-start(bf16[32,864]{1,0:T(8,128)(2,1)} %refs_0_.1) | copy-start | bytes 165892
  15.4 2.1 %copy-start.1 = (f32[128]{0:T(128)S(1)}, f32[128]{0:T(128)}, u32[]{:S(2)}) copy-start(f32[128]{0:T(128)} %param.11) | copy-start | bytes 1540
  15.4 2.1 %copy-start.2 = (f32[128]{0:T(128)S(1)}, f32[128]{0:T(128)}, u32[]{:S(2)}) copy-start(f32[128]{0:T(128)} %param.12) | copy-start | bytes 1540
  15.4 2.0 %collective-permute-start.3 = (bf16[32,864]{1,0:T(8,128)(2,1)}, bf16[32,864]{1,0:T(8,128)(2,1)S(1)}, u32[]{:S(2)}, u32[]{:S(2)}) collective-permute-start(bf16[32,864]{1,0:T(8,128)(2,1)} %refs_0_.1), channel_id=1, source_target_pairs={{0,4},{4,0},{8,12},{12,8},{16,20},{20,16},{24,28},{28,24},{1,5},{5... | collective-permute-start | bytes 165896 | tf_op jit(solution)/shard_map/ppermute | solution.py:464
  15.6 1.9 %collective-permute-start.4 = (bf16[32,864]{1,0:T(8,128)(2,1)S(1)}, bf16[32,864]{1,0:T(8,128)(2,1)S(1)}, u32[]{:S(2)}, u32[]{:S(2)}) collective-permute-start(bf16[32,864]{1,0:T(8,128)(2,1)S(1)} %collective-permute-done.refs_1_), channel_id=1, source_target_pairs={{0,4},{4,0},{8,12},{12,8},{16,20},{20,16},{24,28},{28,24},{1,5},{5... | collective-permute-start | bytes 165896 | tf_op jit(solution)/shard_map/ppermute | solution.py:464
  16.0 1.5 %collective-permute-start.5 = (bf16[32,864]{1,0:T(8,128)(2,1)S(1)}, bf16[32,864]{1,0:T(8,128)(2,1)S(1)}, u32[]{:S(2)}, u32[]{:S(2)}) collective-permute-start(bf16[32,864]{1,0:T(8,128)(2,1)S(1)} %collective-permute-done.1.refs_2_), channel_id=1, source_target_pairs={{0,4},{4,0},{8,12},{12,8},{16,20},{20,16},{24,28},{28,24},{1,5},{5... | collective-permute-start | bytes 165896 | tf_op jit(solution)/shard_map/ppermute | solution.py:464
  16.1 1.4 %collective-permute-start.6 = (bf16[32,864]{1,0:T(8,128)(2,1)S(1)}, bf16[32,864]{1,0:T(8,128)(2,1)S(1)}, u32[]{:S(2)}, u32[]{:S(2)}) collective-permute-start(bf16[32,864]{1,0:T(8,128)(2,1)S(1)} %collective-permute-done.2.refs_3_), channel_id=1, source_target_pairs={{0,4},{4,0},{8,12},{12,8},{16,20},{20,16},{24,28},{28,24},{1,5},{5... | collective-permute-start | bytes 165896 | tf_op jit(solution)/shard_map/ppermute | solution.py:464
  24.8 6.5 %collective-permute-start.10 = (bf16[4,32,1152]{2,1,0:T(8,128)(2,1)S(1)}, bf16[4,32,1152]{2,1,0:T(8,128)(2,1)S(1)}, u32[]{:S(2)}, u32[]{:S(2)}) collective-permute-start(bf16[4,32,1152]{2,1,0:T(8,128)(2,1)S(1)} %get-tuple-element.44), channel_id=1, source_target_pairs={{0,4},{4,0},{8,12},{12,8},{16,20},{20,16},{24,28},{28,24},{1,5},{5... | collective-permute-start | bytes 884744 | tf_op jit(solution)/shard_map/ppermute | solution.py:464
  24.9 9.9 %collective-permute-start.14 = (bf16[192,256]{1,0:T(8,128)(2,1)S(1)}, bf16[192,256]{1,0:T(8,128)(2,1)S(1)}, u32[]{:S(2)}, u32[]{:S(2)}) collective-permute-start(bf16[192,256]{1,0:T(8,128)(2,1)S(1)} %get-tuple-element.51), channel_id=1, source_target_pairs={{0,1},{1,2},{2,3},{3,0},{4,5},{5,6},{6,7},{7,4},{8,9},{9,10},{10,1... | collective-permute-start | bytes 294920 | tf_op jit(solution)/shard_map/ppermute | solution.py:450
  25.3 10.8 %collective-permute-start.15 = (bf16[192,256]{1,0:T(8,128)(2,1)S(1)}, bf16[192,256]{1,0:T(8,128)(2,1)S(1)}, u32[]{:S(2)}, u32[]{:S(2)}) collective-permute-start(bf16[192,256]{1,0:T(8,128)(2,1)S(1)} %get-tuple-element.52), channel_id=1, source_target_pairs={{0,2},{1,3},{2,0},{3,1},{4,6},{5,7},{6,4},{7,5},{8,10},{9,11},{10,... | collective-permute-start | bytes 294920 | tf_op jit(solution)/shard_map/ppermute | solution.py:450
  26.9 9.1 %collective-permute-start.16 = (bf16[192,256]{1,0:T(8,128)(2,1)S(1)}, bf16[192,256]{1,0:T(8,128)(2,1)S(1)}, u32[]{:S(2)}, u32[]{:S(2)}) collective-permute-start(bf16[192,256]{1,0:T(8,128)(2,1)S(1)} %get-tuple-element.53), channel_id=1, source_target_pairs={{0,3},{1,0},{2,1},{3,2},{4,7},{5,4},{6,5},{7,6},{8,11},{9,8},{10,9... | collective-permute-start | bytes 294920 | tf_op jit(solution)/shard_map/ppermute | solution.py:450
  28.8 11.3 %all-to-all-start.1 = ((bf16[32,16,128]{2,1,0:T(8,128)(2,1)}), bf16[32,16,128]{2,1,0:T(8,128)(2,1)S(1)}, u32[]{:S(2)}, u32[]{:S(2)}) async-start(bf16[32,16,128]{2,1,0:T(8,128)(2,1)} %get-tuple-element.42), calls=%async_computation.1 | async-start | bytes 262144 | tf_op jit(solution)/shard_map/all_to_all | solution.py:553
  31.5 8.6 %collective-permute-start.11 = (bf16[32,864]{1,0:T(8,128)(2,1)S(1)}, bf16[32,864]{1,0:T(8,128)(2,1)S(1)}, u32[]{:S(2)}, u32[]{:S(2)}) collective-permute-start(bf16[32,864]{1,0:T(8,128)(2,1)S(1)} %get-tuple-element.45.after_ref), channel_id=1, source_target_pairs={{0,8},{4,12},{8,0},{12,4},{16,24},{20,28},{24,16},{28,20},{1,9},{5... | collective-permute-start | bytes 165896 | tf_op jit(solution)/shard_map/ppermute | solution.py:459
  33.3 6.8 %collective-permute-start.12 = (bf16[32,864]{1,0:T(8,128)(2,1)S(1)}, bf16[32,864]{1,0:T(8,128)(2,1)S(1)}, u32[]{:S(2)}, u32[]{:S(2)}) collective-permute-start(bf16[32,864]{1,0:T(8,128)(2,1)S(1)} %get-tuple-element.47), channel_id=1, source_target_pairs={{0,16},{4,20},{8,24},{12,28},{16,0},{20,4},{24,8},{28,12},{1,17},{... | collective-permute-start | bytes 165896 | tf_op jit(solution)/shard_map/ppermute | solution.py:459
  34.7 5.4 %collective-permute-start.13 = (bf16[32,864]{1,0:T(8,128)(2,1)S(1)}, bf16[32,864]{1,0:T(8,128)(2,1)S(1)}, u32[]{:S(2)}, u32[]{:S(2)}) collective-permute-start(bf16[32,864]{1,0:T(8,128)(2,1)S(1)} %get-tuple-element.48), channel_id=1, source_target_pairs={{0,24},{4,28},{8,16},{12,20},{16,8},{20,12},{24,0},{28,4},{1,25},{... | collective-permute-start | bytes 165896 | tf_op jit(solution)/shard_map/ppermute | solution.py:459

commit v5 on v4

--- a/solution.py
+++ b/solution.py
@@ -135,15 +135,16 @@
     video_pad[0] = zeros
     video_pad[slab + 1] = zeros
     for i in range(1, slab):
-        video_pad[jnp.mod(own - i + slab, slab) + 1] = video_refs[i - 1][...]
+        video_pad[jnp.mod(own - i + slab, slab) + 1] = video_refs[-i][...]
     copy.wait()
 
 
-def forward_kernel(dims, blocks_hbm, gain_ref, bias_ref, *refs):
+def forward_kernel(dims, blocks_hbm, slots_ref, gain_ref, bias_ref, *refs):
     devs, slab, clips, held, frames, columns, rows_in, cols, och, per_group = dims
     shard_refs, video_pad, table_ref = refs[:devs], refs[devs], refs[devs + 1]
     weights_ref, video_t_ref, normed_ref, inv_ref, slope_ref, act_ref = refs[devs + 2 : devs + 8]
-    shards, blocks_ref, sems = refs[devs + 8 :]
+    act_hbm, act_ref = act_ref, refs[devs + 8]
+    shards, blocks_ref, sems = refs[devs + 9 :]
     copy = fetch([(blocks_hbm, blocks_ref)], sems)[0]
     me, own = lax.axis_index("clips"), lax.axis_index("slab")
     places = held * frames * columns
@@ -191,6 +192,7 @@
         counts.append(jnp.full((1, och), count, F32))
         limits.append(jnp.full((1, och), (blocks * FB).astype(F32), F32))
     sums = group_sums(kept + [a * b for a, b in zip(kept, convs)], per_group)
+    act_blocks = []
     for k in range(held):
         conv = convs[k]
         mean = sums[k] / counts[k]
@@ -207,9 +209,20 @@
         for b in range(BMAX):
             for h in range(slab):
                 block = act[h, b * block_rows : (b + 1) * block_rows]
-                act_ref[k * BMAX + b, h] = unfolded_to_lanes(block, 8)
+                act_blocks.append(unfolded_to_lanes(block, 8))
+    for d in range(devs):
+        for h in range(slab):
+            total = None
+            for j in range(held * BMAX):
+                term = act_blocks[j * slab + h] * slots_ref[j * devs + d]
+                total = term if total is None else total + term
+            pairs = [total[i : i + 2] for i in range(0, total.shape[0], 2)] + [jnp.zeros((2, LANES), F32)]
+            act_ref[d * slab + h] = jnp.concatenate(pairs, axis=1).astype(BF16)
+    act_copy = pltpu.make_async_copy(act_ref, act_hbm, sems.at[1])
+    act_copy.start()
     weights_ref[...] = jnp.transpose(weights)
     video_t_ref[...] = jnp.transpose(video_pad[1 : slab + 1].reshape(many, c_in))
+    act_copy.wait()
 
 
 def from_left(values, columns):
@@ -243,7 +256,7 @@
     video_t_ref, normed_ref, inv_ref, slope_ref, act_in, cot_ref = refs[:6]
     act_hbm, keep_ref, send_ref = refs[6:9]
     video_grad_refs = refs[9 : 9 + slab]
-    act_ref, grad_ref, rows_ref, sems = refs[9 + slab :]
+    sums_ref, grad_ref, rows_ref, sems = refs[9 + slab :]
     me, own = lax.axis_index("clips"), lax.axis_index("slab")
     places = held * frames * columns
     per_clip = frames * columns
@@ -298,19 +311,15 @@
             lanes.append(jnp.zeros((slab, per_clip, LANES - 3 * och), F32))
         conv_grads.append(jnp.concatenate(lanes, axis=2))
 
-    sums = split3(gain_part) + split3(bias_part) + [jnp.zeros((2, och), F32)]
+    sums = split3(gain_part) + split3(bias_part)
+    sums = [jnp.concatenate(sums[:4], axis=1), jnp.concatenate(sums[4:] + [jnp.zeros((1, 2 * och), F32)], axis=1)]
     sums = jnp.concatenate(sums, axis=0)
-    sums = jnp.concatenate([sums, jnp.zeros((8, LANES - och), F32)], axis=1)
-    for d in range(devs):
-        for h in range(slab):
-            total = None
-            for j in range(held * BMAX):
-                term = act_in[j, h] * slots_ref[j * devs + d]
-                total = term if total is None else total + term
-            act_ref[d * slab + h] = jnp.concatenate([total, sums], axis=0).astype(BF16)
-
-    act_copy = pltpu.make_async_copy(act_ref, act_hbm, sems.at[0])
-    act_copy.start()
+    if LANES > 4 * och:
+        sums = jnp.concatenate([sums, jnp.zeros((2, LANES - 4 * och), F32)], axis=1)
+    sums_ref[...] = jnp.broadcast_to(sums.astype(BF16)[None], sums_ref.shape)
+    last = act_hbm.shape[2] - LANES
+    sums_copy = pltpu.make_async_copy(sums_ref, act_hbm.at[:, :, last : last + LANES], sems.at[0])
+    sums_copy.start()
 
     grads = jnp.concatenate(conv_grads, axis=1).reshape(many, LANES)
     grad_ref[0] = jnp.zeros((places, 3 * LANES), BF16)
@@ -332,7 +341,7 @@
     odd = me % 2 == 1
     keep_ref[...] = jnp.where(odd, high, low)
     send_ref[...] = jnp.where(odd, low, high).astype(BF16)
-    act_copy.wait()
+    sums_copy.wait()
 
 
 def unfolded_to_lanes(values, unit):
@@ -399,17 +408,19 @@
     copies[0].start()
 
     groups = LANES // och
-    rows = act_in.shape[1] - 8
+    pairs = act_in.shape[2] // LANES - 1
     sums = []
-    blocks = [[jnp.zeros((rows, LANES), F32)] * slab for _ in range(slots)]
+    blocks = [[jnp.zeros((2 * pairs, LANES), F32)] * slab for _ in range(slots)]
     for s in range(slab):
-        part = jnp.zeros((8, LANES), F32)
+        part = jnp.zeros((2, LANES), F32)
         for d in range(devs):
             both = act_in[d * slab + s].astype(F32)
-            part = part + both[rows:]
+            part = part + both[:, pairs * LANES :]
+            both = [both[:, i * LANES : (i + 1) * LANES] for i in range(pairs)]
+            both = jnp.concatenate(both, axis=0)
             for q in range(slots):
-                blocks[q][s] = blocks[q][s] + both[:rows] * holds_ref[q * devs + d]
-        sums.append(part[:, :och])
+                blocks[q][s] = blocks[q][s] + both * holds_ref[q * devs + d]
+        sums.append(part)
     for q in range(slots):
         block = []
         for g in range(groups):
@@ -417,16 +428,17 @@
             block.append(jnp.concatenate(parts, axis=1))
         act_ref[q] = jnp.concatenate(block, axis=0)[: act_ref.shape[1]].astype(BF16)
     copies[1].start()
-    sums = jnp.concatenate(sums, axis=1)
-    gain_ref[...] = sums[0:1] + (sums[1:2] + sums[2:3])
-    bias_ref[...] = sums[3:4] + (sums[4:5] + sums[5:6])
+    gains = [p[0:1, :och] + (p[0:1, och : 2 * och] + p[0:1, 2 * och : 3 * och]) for p in sums]
+    gain_ref[...] = jnp.concatenate(gains, axis=1)
+    biases = [p[0:1, 3 * och : 4 * och] + (p[1:2, :och] + p[1:2, och : 2 * och]) for p in sums]
+    bias_ref[...] = jnp.concatenate(biases, axis=1)
     copies[2].start()
     copies[3].start()
     for copy in copies:
         copy.wait()
 
 
-def call(kernel, outs, specs, scratch=(), limit=None, out_specs=None, cost=None):
+def call(kernel, outs, specs, scratch=(), limit=None, out_specs=None, cost=None, alias=None):
     limit = limit or lax.axis_size("slab") * MIB
     return pl.pallas_call(
         kernel,
@@ -434,6 +446,7 @@
         in_specs=specs,
         out_specs=out_specs or [VMEM] * len(outs),
         cost_estimate=cost,
+        input_output_aliases=alias or {},
         scratch_shapes=list(scratch),
         compiler_params=pltpu.CompilerParams(vmem_limit_bytes=limit),
     )
@@ -478,6 +491,7 @@
     fold_rows = round_up(-(-block_rows // (LANES // och)), 8)
     chips = devs // 2
     everyone = ("clips", "slab")
+    act_shape = (devs * slab, 2, fold_rows // 2 * LANES + LANES)
     shape = jax.ShapeDtypeStruct
     smem = [pltpu.SMEM((clips,), jnp.int32), pltpu.SMEM((devs,), jnp.int32)]
     large = (6 + 3 * slab) * MIB
@@ -511,7 +525,7 @@
         [HBM] + [VMEM] * (slab - 1),
         [pltpu.SemaphoreType.DMA((1,))],
         cost=pl.CostEstimate(flops=STAGE, bytes_accessed=0, transcendentals=0),
-    )(pltpu.with_memory_space_constraint(videos[0], pltpu.HBM), *videos[1:])
+    )(pltpu.with_memory_space_constraint(videos[0], pltpu.HBM), *videos[:0:-1])
     weights, video_t, normed, inv_std, slope, act = call(
         functools.partial(forward_kernel, dims),
         [
@@ -520,33 +534,36 @@
             shape((slab, places, och), F32),
             shape((held, 8, och), F32),
             shape((slab, places, och), F32),
-            shape((held * BMAX, slab, fold_rows, LANES), F32),
+            pltpu.HBM(act_shape, BF16),
         ],
-        [HBM] + [VMEM] * (devs + 4),
+        [HBM] + [VMEM] * (devs + 5),
         [
+            pltpu.VMEM(act_shape, BF16),
             pltpu.VMEM((devs, rows_in, width), F32 if rows_in % 16 else BF16),
             smem[0],
-            pltpu.SemaphoreType.DMA((1,)),
+            pltpu.SemaphoreType.DMA((2,)),
         ],
         large,
-    )(clip_blocks, gain, bias, *shards, video_pad, table)
+        [VMEM] * 5 + [HBM],
+    )(clip_blocks, slot_of, gain, bias, *shards, video_pad, table)
     acts, keep, send, *video_grads = call(
         functools.partial(backward_kernel, dims),
         [
-            pltpu.HBM((devs * slab, fold_rows + 8, LANES), BF16),
+            pltpu.HBM(act_shape, BF16),
             shape((chips, rows_in, 9 * LANES), F32),
             shape((chips, rows_in, 9 * LANES), BF16),
         ]
         + [shape((places, c_in), F32 if i == 0 else BF16) for i in range(slab)],
-        [VMEM] * 9,
+        [VMEM] * 7 + [HBM, VMEM],
         [
-            pltpu.VMEM((devs * slab, fold_rows + 8, LANES), BF16),
+            pltpu.VMEM((devs * slab, 2, LANES), BF16),
             pltpu.VMEM((slab + 2, places, 3 * LANES), BF16),
             pltpu.VMEM((slab, places, c_in), F32),
             pltpu.SemaphoreType.DMA((1,)),
         ],
         large,
         [HBM] + [VMEM] * (2 + slab),
+        alias={7: 0},
     )(slot_of, gain, weights, video_t, normed, inv_std, slope, act, cots)
     video_grads = shifts(video_grads, "slab")
     send = core_swap(send, "clips")
@@ -580,7 +597,7 @@
         [pltpu.VMEM(*out) for out in outs] + [pltpu.SemaphoreType.DMA((4,))],
         2 * slab * MIB,
         [HBM] * 4,
-    )(holds, acts, table, *kernel_grads)
+    )(holds, acts, table, kernel_grads[0], *kernel_grads[:0:-1])
     return (
         act.reshape(cotangent.shape),
         video_grad.reshape(video.shape),

time: 41.6 us -> 41.1 us (0.988)
  waiting for transfers between devices: 6 us -> 4.58 us
  Pallas kernels: 10.1 us -> 10.7 us
    pallas_call x1, Pallas kernels: 2.9 us -> 3.44 us  [body(): call(functools.partial(forward_kernel, dims), [shape((9 * LANES, c_in), B...]
    all_to_all x1, waiting for transfers between devices: 2.45 us -> 1.91 us  [body(): lax.all_to_all(cots, everyone, split_axis=0, concat_axis=0, tiled=True)]
    all_to_all x1, waiting for transfers between devices: 2.52 us -> 2.01 us  [body(): lax.all_to_all(acts, everyone, split_axis=0, concat_axis=0, tiled=True)]
  transfers between devices with their start and end apart: 19 -> 19, of which waited for: 3 -> 3; matrix products, arithmetic and copies ran while one was open for 0% -> 0% of each run, Pallas kernels for 17% -> 19%
where the time goes in v5:
time: 41.1 us; the launch traced here: 40.8 us
  starting transfers between devices  24.6 us (60%)
  Pallas kernels  10.7 us (26%)
  waiting for transfers between devices  4.58 us (11%)
  between operations  0.81 us (2%)
    ppermute x6, starting transfers between devices, shifts(): lax.ppermute(arrays[i], axis, [(j, (j + i) % size) for j in range(size)])  9.44 us
    ppermute x3, starting transfers between devices, body(): shards = shards + [lax.ppermute(shard, 'clips', pairs) for shard in shards]  5.03 us
    ppermute x3, starting transfers between devices, chip_swaps(): moved.append(lax.ppermute(arrays[t], axis, pairs))  3.55 us
    pallas_call x1, Pallas kernels, body(): call(functools.partial(forward_kernel, dims), [shape((9 * LANES, c_in), B...  3.44 us
    all_to_all x1, starting transfers between devices, body(): lax.all_to_all(acts, everyone, split_axis=0, concat_axis=0, tiled=True)  2.85 us
    all_to_all x1, starting transfers between devices, body(): lax.all_to_all(cots, everyone, split_axis=0, concat_axis=0, tiled=True)  2.59 us
    all_to_all x1, waiting for transfers between devices, body(): lax.all_to_all(acts, everyone, split_axis=0, concat_axis=0, tiled=True)  2.01 us
    all_to_all x1, waiting for transfers between devices, body(): lax.all_to_all(cots, everyone, split_axis=0, concat_axis=0, tiled=True)  1.91 us
  transfers between devices with their start and end apart: 19, of which 3 were waited for; matrix products, arithmetic and copies ran while one was open for 0% of the time, Pallas kernels for 19%

profile of v5, /device:TPU:0, one launch (start us, length us, event | category | flops | bytes accessed | tf_op | source)
XLA Modules:
  0.0 40.8 jit_solution(1713564608478899375)
XLA Ops:
  0.6 3.0 %collective-permute-start = (bf16[32,864]{1,0:T(8,128)(2,1)}, bf16[32,864]{1,0:T(8,128)(2,1)S(1)}, u32[]{:S(2)}, u32[]{:S(2)}) collective-permute-start(bf16[32,864]{1,0:T(8,128)(2,1)} %refs_0_.1), channel_id=1, source_target_pairs={{0,8},{4,12},{8,0},{12,4},{16,24},{20,28},{24,16},{28,20},{1,9},{5... | collective-permute-start | bytes 165896 | tf_op jit(solution)/shard_map/ppermute | solution.py:518
  3.6 1.6 %collective-permute-start.9 = (bf16[192,256]{1,0:T(8,128)(2,1)}, bf16[192,256]{1,0:T(8,128)(2,1)S(1)}, u32[]{:S(2)}, u32[]{:S(2)}) collective-permute-start(bf16[192,256]{1,0:T(8,128)(2,1)} %bitcast.16), channel_id=1, source_target_pairs={{0,1},{1,2},{2,3},{3,0},{4,5},{5,6},{6,7},{7,4},{8,9},{9,10},{10,1... | collective-permute-start | bytes 294920 | tf_op jit(solution)/shard_map/ppermute | solution.py:463
  5.2 2.6 %collective-permute-start.8 = (bf16[192,256]{1,0:T(8,128)(2,1)}, bf16[192,256]{1,0:T(8,128)(2,1)S(1)}, u32[]{:S(2)}, u32[]{:S(2)}) collective-permute-start(bf16[192,256]{1,0:T(8,128)(2,1)} %bitcast.17), channel_id=1, source_target_pairs={{0,2},{1,3},{2,0},{3,1},{4,6},{5,7},{6,4},{7,5},{8,10},{9,11},{10,... | collective-permute-start | bytes 294920 | tf_op jit(solution)/shard_map/ppermute | solution.py:463
  7.8 1.3 %collective-permute-start.7 = (bf16[192,256]{1,0:T(8,128)(2,1)}, bf16[192,256]{1,0:T(8,128)(2,1)S(1)}, u32[]{:S(2)}, u32[]{:S(2)}) collective-permute-start(bf16[192,256]{1,0:T(8,128)(2,1)} %bitcast.18), channel_id=1, source_target_pairs={{0,3},{1,0},{2,1},{3,2},{4,7},{5,4},{6,5},{7,6},{8,11},{9,8},{10,9... | collective-permute-start | bytes 294920 | tf_op jit(solution)/shard_map/ppermute | solution.py:463
  9.2 1.5 %collective-permute-start.1 = (bf16[32,864]{1,0:T(8,128)(2,1)}, bf16[32,864]{1,0:T(8,128)(2,1)S(1)}, u32[]{:S(2)}, u32[]{:S(2)}) collective-permute-start(bf16[32,864]{1,0:T(8,128)(2,1)} %refs_0_.1), channel_id=1, source_target_pairs={{0,16},{4,20},{8,24},{12,28},{16,0},{20,4},{24,8},{28,12},{1,17},{... | collective-permute-start | bytes 165896 | tf_op jit(solution)/shard_map/ppermute | solution.py:518
  10.7 0.5 %collective-permute-start.2 = (bf16[32,864]{1,0:T(8,128)(2,1)S(1)}, bf16[32,864]{1,0:T(8,128)(2,1)S(1)}, u32[]{:S(2)}, u32[]{:S(2)}) collective-permute-start(bf16[32,864]{1,0:T(8,128)(2,1)S(1)} %collective-permute-done.refs_1_), channel_id=1, source_target_pairs={{0,16},{4,20},{8,24},{12,28},{16,0},{20,4},{24,8},{28,12},{1,17},{... | collective-permute-start | bytes 165896 | tf_op jit(solution)/shard_map/ppermute | solution.py:518
  11.2 1.6 %shard_map.110 = (bf16[32,8,128]{2,1,0:T(8,128)(2,1)}, f32[32,1,128]{2,1,0:T(1,128)S(1)}, f32[48,1,128]{2,1,0:T(1,128)S(1)}) custom-call(s32[16]{0:T(128)} %blocks_hbm.3, s32[8]{0:T(128)} %order_hbm.1, bf16[4,32,128]{2,1,0:T(8,128)(2,1)} %bitcast.15), custom_call_target="tpu_custom_call" | custom-call | flops 1000000 | tf_op jit(solution)/shard_map/pallas_call | solution.py:506
  12.8 2.6 %all-to-all-start = ((bf16[32,8,128]{2,1,0:T(8,128)(2,1)}), bf16[32,8,128]{2,1,0:T(8,128)(2,1)S(1)}, u32[]{:S(2)}, u32[]{:S(2)}) async-start(bf16[32,8,128]{2,1,0:T(8,128)(2,1)} %get-tuple-element.41), calls=%async_computation | async-start | bytes 131072 | tf_op jit(solution)/shard_map/all_to_all | solution.py:514
  15.6 0.4 collective-permute-start.4
  16.1 0.4 collective-permute-start.6
  16.5 0.9 %shard_map.111 = (bf16[6,192,256]{2,1,0:T(8,128)(2,1)S(1)}, bf16[896,1152]{1,0:T(8,128)(2,1)S(1)}) custom-call(bf16[192,256]{1,0:T(8,128)(2,1)} %bitcast.19, bf16[192,256]{1,0:T(8,128)(2,1)S(1)} %collective-permute-done.7.refs_1_, bf16[192,256]{1,0:T(8,128)(2,1)S(1)} %collective-permute-done.8.refs_2_, bf16[192,256]{1,0:T(8,128)(2,1)S(1)} %collective-permute-done.9.refs_3_), custom_call_target="tpu_custom_call" | custom-call | flops 10000000000 | tf_op jit(solution)/shard_map/pallas_call | solution.py:522
  17.5 3.4 %shard_map.112 = (bf16[1152,256]{1,0:T(8,128)(2,1)S(1)}, bf16[256,768]{1,0:T(8,128)(2,1)S(1)}, f32[4,192,32]{2,1,0:T(8,128)S(1)}, f32[2,8,32]{2,1,0:T(8,128)S(1)...) custom-call(s32[16]{0:T(128)} %blocks_hbm.3, f32[48,1,128]{2,1,0:T(1,128)S(1)} %get-tuple-element.32.slots_ref, ...), custom_call_target="tpu_custom_call" | custom-call | tf_op jit(solution)/shard_map/pallas_call | solution.py:529
  21.0 1.9 %all-to-all-done.refs_5_ = bf16[32,8,128]{2,1,0:T(8,128)(2,1)S(1)} async-done(((bf16[32,8,128]{2,1,0:T(8,128)(2,1)}), bf16[32,8,128]{2,1,0:T(8,128)(2,1)S(1)}, u32[]{:S(2)}, u32[]{:S(2)}) %all-to-all-start) | async-done | bytes 65568 | tf_op jit(solution)/shard_map/all_to_all | solution.py:514
  22.9 1.9 %shard_map.113 = (bf16[32,2,640]{2,1,0:T(2,128)(2,1)}, f32[4,32,1152]{2,1,0:T(8,128)S(1)}, bf16[4,32,1152]{2,1,0:T(8,128)(2,1)S(1)}, f32[192,256]{1,0:T(8,128)S(...) custom-call(f32[48,1,128]{2,1,0:T(1,128)S(1)} %get-tuple-element.32., ...), custom_call_target="tpu_custom_call", output_to_operand_aliasing={{0}: (7, {})} | custom-call | tf_op jit(solution)/shard_map/pallas_call | solution.py:549
  25.3 2.2 %collective-permute-start.15 = (bf16[192,256]{1,0:T(8,128)(2,1)S(1)}, bf16[192,256]{1,0:T(8,128)(2,1)S(1)}, u32[]{:S(2)}, u32[]{:S(2)}) collective-permute-start(bf16[192,256]{1,0:T(8,128)(2,1)S(1)} %get-tuple-element.52), channel_id=1, source_target_pairs={{0,2},{1,3},{2,0},{3,1},{4,6},{5,7},{6,4},{7,5},{8,10},{9,11},{10,... | collective-permute-start | bytes 294920 | tf_op jit(solution)/shard_map/ppermute | solution.py:463
  27.4 1.4 %collective-permute-start.16 = (bf16[192,256]{1,0:T(8,128)(2,1)S(1)}, bf16[192,256]{1,0:T(8,128)(2,1)S(1)}, u32[]{:S(2)}, u32[]{:S(2)}) collective-permute-start(bf16[192,256]{1,0:T(8,128)(2,1)S(1)} %get-tuple-element.53), channel_id=1, source_target_pairs={{0,3},{1,0},{2,1},{3,2},{4,7},{5,4},{6,5},{7,6},{8,11},{9,8},{10,9... | collective-permute-start | bytes 294920 | tf_op jit(solution)/shard_map/ppermute | solution.py:463
  28.8 2.9 %all-to-all-start.1 = ((bf16[32,2,640]{2,1,0:T(2,128)(2,1)}), bf16[32,2,640]{2,1,0:T(2,128)(2,1)S(1)}, u32[]{:S(2)}, u32[]{:S(2)}) async-start(bf16[32,2,640]{2,1,0:T(2,128)(2,1)} %get-tuple-element.42), calls=%async_computation.1 | async-start | bytes 163840 | tf_op jit(solution)/shard_map/all_to_all | solution.py:570
  31.9 2.7 %collective-permute-start.11 = (bf16[32,864]{1,0:T(8,128)(2,1)S(1)}, bf16[32,864]{1,0:T(8,128)(2,1)S(1)}, u32[]{:S(2)}, u32[]{:S(2)}) collective-permute-start(bf16[32,864]{1,0:T(8,128)(2,1)S(1)} %get-tuple-element.47), channel_id=1, source_target_pairs={{0,24},{4,28},{8,16},{12,20},{16,8},{20,12},{24,0},{28,4},{1,25},{... | collective-permute-start | bytes 165896 | tf_op jit(solution)/shard_map/ppermute | solution.py:472
  34.6 0.6 %collective-permute-start.12 = (bf16[32,864]{1,0:T(8,128)(2,1)S(1)}, bf16[32,864]{1,0:T(8,128)(2,1)S(1)}, u32[]{:S(2)}, u32[]{:S(2)}) collective-permute-start(bf16[32,864]{1,0:T(8,128)(2,1)S(1)} %get-tuple-element.48), channel_id=1, source_target_pairs={{0,16},{4,20},{8,24},{12,28},{16,0},{20,4},{24,8},{28,12},{1,17},{... | collective-permute-start | bytes 165896 | tf_op jit(solution)/shard_map/ppermute | solution.py:472
  35.4 0.6 %collective-permute-done.15.refs_2_ = bf16[192,256]{1,0:T(8,128)(2,1)S(1)} collective-permute-done((bf16[192,256]{1,0:T(8,128)(2,1)S(1)}, bf16[192,256]{1,0:T(8,128)(2,1)S(1)}, u32[]{:S(2)}, u32[]{:S(2)}) %collective-permute-start.15) | collective-permute-done | bytes 98336 | tf_op jit(solution)/shard_map/ppermute | solution.py:463
  36.0 0.7 %shard_map.117 = bf16[192,256]{1,0:T(8,128)(2,1)} custom-call(f32[192,256]{1,0:T(8,128)S(1)} %get-tuple-element.50.refs_0_, bf16[192,256]{1,0:T(8,128)(2,1)S(1)} %collective-permute-done.14.refs_1_, bf16[192,256]{1,0:T(8,128)(2,1)S(1)} %collective-permute-done.15.refs_2_, bf16[192,256]{1,0:T(8,128)(2,1)S(1)} %collective-permute-done.16.refs_3_), custom_call_target="tpu_custom_call" | custom-call | flops 10000000000 | tf_op jit(solution)/shard_map/pallas_call | solution.py:581
  36.7 0.9 %shard_map.115.table_ref = bf16[896,896]{1,0:T(8,128)(2,1)S(1)} custom-call(bf16[32,864]{1,0:T(8,128)(2,1)S(1)} %get-tuple-element.45.after_ref), custom_call_target="tpu_custom_call" | custom-call | tf_op jit(solution)/shard_map/pallas_call | solution.py:576
  37.6 2.0 %all-to-all-done.1.act_in = bf16[32,2,640]{2,1,0:T(2,128)(2,1)S(1)} async-done(((bf16[32,2,640]{2,1,0:T(2,128)(2,1)}), bf16[32,2,640]{2,1,0:T(2,128)(2,1)S(1)}, u32[]{:S(2)}, u32[]{:S(2)}) %all-to-all-start.1) | async-done | bytes 81952 | tf_op jit(solution)/shard_map/all_to_all | solution.py:570
  39.6 1.1 %shard_map.116 = (f32[32,864]{1,0:T(8,128)}, bf16[4,32,128]{2,1,0:T(8,128)(2,1)}, f32[1,128]{1,0:T(1,128)}, f32[1,128]{1,0:T(1,128)}) custom-call(f32[32,1,128]{2,1,0:T(1,128)S(1)} %get-tuple-element.31.holds_ref, bf16[32,2,640]{2,1,0:T(2,128)(2,1)S(1)} %all-to-all-done.1.act_in, bf16[896,896]{1,0:T(8,128)(2,1)S(1)} %shard_map.115.table_ref, ...), custom_call_target="tpu_custom_call" | custom-call | tf_op jit(solution)/shard_map/pallas_call | solution.py:593
  (28 shorter events, 1.2 us)
Async XLA Ops:
  0.6 10.0 %collective-permute-start = (bf16[32,864]{1,0:T(8,128)(2,1)}, bf16[32,864]{1,0:T(8,128)(2,1)S(1)}, u32[]{:S(2)}, u32[]{:S(2)}) collective-permute-start(bf16[32,864]{1,0:T(8,128)(2,1)} %refs_0_.1), channel_id=1, source_target_pairs={{0,8},{4,12},{8,0},{12,4},{16,24},{20,28},{24,16},{28,20},{1,9},{5... | collective-permute-start | bytes 165896 | tf_op jit(solution)/shard_map/ppermute | solution.py:518
  3.6 12.0 %collective-permute-start.9 = (bf16[192,256]{1,0:T(8,128)(2,1)}, bf16[192,256]{1,0:T(8,128)(2,1)S(1)}, u32[]{:S(2)}, u32[]{:S(2)}) collective-permute-start(bf16[192,256]{1,0:T(8,128)(2,1)} %bitcast.16), channel_id=1, source_target_pairs={{0,1},{1,2},{2,3},{3,0},{4,5},{5,6},{6,7},{7,4},{8,9},{9,10},{10,1... | collective-permute-start | bytes 294920 | tf_op jit(solution)/shard_map/ppermute | solution.py:463
  5.2 10.8 %collective-permute-start.8 = (bf16[192,256]{1,0:T(8,128)(2,1)}, bf16[192,256]{1,0:T(8,128)(2,1)S(1)}, u32[]{:S(2)}, u32[]{:S(2)}) collective-permute-start(bf16[192,256]{1,0:T(8,128)(2,1)} %bitcast.17), channel_id=1, source_target_pairs={{0,2},{1,3},{2,0},{3,1},{4,6},{5,7},{6,4},{7,5},{8,10},{9,11},{10,... | collective-permute-start | bytes 294920 | tf_op jit(solution)/shard_map/ppermute | solution.py:463
  7.8 8.7 %collective-permute-start.7 = (bf16[192,256]{1,0:T(8,128)(2,1)}, bf16[192,256]{1,0:T(8,128)(2,1)S(1)}, u32[]{:S(2)}, u32[]{:S(2)}) collective-permute-start(bf16[192,256]{1,0:T(8,128)(2,1)} %bitcast.18), channel_id=1, source_target_pairs={{0,3},{1,0},{2,1},{3,2},{4,7},{5,4},{6,5},{7,6},{8,11},{9,8},{10,9... | collective-permute-start | bytes 294920 | tf_op jit(solution)/shard_map/ppermute | solution.py:463
  9.2 6.3 %collective-permute-start.1 = (bf16[32,864]{1,0:T(8,128)(2,1)}, bf16[32,864]{1,0:T(8,128)(2,1)S(1)}, u32[]{:S(2)}, u32[]{:S(2)}) collective-permute-start(bf16[32,864]{1,0:T(8,128)(2,1)} %refs_0_.1), channel_id=1, source_target_pairs={{0,16},{4,20},{8,24},{12,28},{16,0},{20,4},{24,8},{28,12},{1,17},{... | collective-permute-start | bytes 165896 | tf_op jit(solution)/shard_map/ppermute | solution.py:518
  10.7 5.5 %collective-permute-start.2 = (bf16[32,864]{1,0:T(8,128)(2,1)S(1)}, bf16[32,864]{1,0:T(8,128)(2,1)S(1)}, u32[]{:S(2)}, u32[]{:S(2)}) collective-permute-start(bf16[32,864]{1,0:T(8,128)(2,1)S(1)} %collective-permute-done.refs_1_), channel_id=1, source_target_pairs={{0,16},{4,20},{8,24},{12,28},{16,0},{20,4},{24,8},{28,12},{1,17},{... | collective-permute-start | bytes 165896 | tf_op jit(solution)/shard_map/ppermute | solution.py:518
  12.8 10.1 %all-to-all-start = ((bf16[32,8,128]{2,1,0:T(8,128)(2,1)}), bf16[32,8,128]{2,1,0:T(8,128)(2,1)S(1)}, u32[]{:S(2)}, u32[]{:S(2)}) async-start(bf16[32,8,128]{2,1,0:T(8,128)(2,1)} %get-tuple-element.41), calls=%async_computation | async-start | bytes 131072 | tf_op jit(solution)/shard_map/all_to_all | solution.py:514
  15.4 2.1 %copy-start = (bf16[32,864]{1,0:T(8,128)(2,1)S(1)}, bf16[32,864]{1,0:T(8,128)(2,1)}, u32[]{:S(2)}) copy-start(bf16[32,864]{1,0:T(8,128)(2,1)} %refs_0_.1) | copy-start | bytes 165892
  15.4 2.1 %copy-start.1 = (f32[128]{0:T(128)S(1)}, f32[128]{0:T(128)}, u32[]{:S(2)}) copy-start(f32[128]{0:T(128)} %param.11) | copy-start | bytes 1540
  15.4 2.1 %copy-start.2 = (f32[128]{0:T(128)S(1)}, f32[128]{0:T(128)}, u32[]{:S(2)}) copy-start(f32[128]{0:T(128)} %param.12) | copy-start | bytes 1540
  15.4 2.0 %collective-permute-start.3 = (bf16[32,864]{1,0:T(8,128)(2,1)}, bf16[32,864]{1,0:T(8,128)(2,1)S(1)}, u32[]{:S(2)}, u32[]{:S(2)}) collective-permute-start(bf16[32,864]{1,0:T(8,128)(2,1)} %refs_0_.1), channel_id=1, source_target_pairs={{0,4},{4,0},{8,12},{12,8},{16,20},{20,16},{24,28},{28,24},{1,5},{5... | collective-permute-start | bytes 165896 | tf_op jit(solution)/shard_map/ppermute | solution.py:477
  15.6 1.9 %collective-permute-start.4 = (bf16[32,864]{1,0:T(8,128)(2,1)S(1)}, bf16[32,864]{1,0:T(8,128)(2,1)S(1)}, u32[]{:S(2)}, u32[]{:S(2)}) collective-permute-start(bf16[32,864]{1,0:T(8,128)(2,1)S(1)} %collective-permute-done.refs_1_), channel_id=1, source_target_pairs={{0,4},{4,0},{8,12},{12,8},{16,20},{20,16},{24,28},{28,24},{1,5},{5... | collective-permute-start | bytes 165896 | tf_op jit(solution)/shard_map/ppermute | solution.py:477
  16.0 1.4 %collective-permute-start.5 = (bf16[32,864]{1,0:T(8,128)(2,1)S(1)}, bf16[32,864]{1,0:T(8,128)(2,1)S(1)}, u32[]{:S(2)}, u32[]{:S(2)}) collective-permute-start(bf16[32,864]{1,0:T(8,128)(2,1)S(1)} %collective-permute-done.1.refs_2_), channel_id=1, source_target_pairs={{0,4},{4,0},{8,12},{12,8},{16,20},{20,16},{24,28},{28,24},{1,5},{5... | collective-permute-start | bytes 165896 | tf_op jit(solution)/shard_map/ppermute | solution.py:477
  16.1 1.4 %collective-permute-start.6 = (bf16[32,864]{1,0:T(8,128)(2,1)S(1)}, bf16[32,864]{1,0:T(8,128)(2,1)S(1)}, u32[]{:S(2)}, u32[]{:S(2)}) collective-permute-start(bf16[32,864]{1,0:T(8,128)(2,1)S(1)} %collective-permute-done.2.refs_3_), channel_id=1, source_target_pairs={{0,4},{4,0},{8,12},{12,8},{16,20},{20,16},{24,28},{28,24},{1,5},{5... | collective-permute-start | bytes 165896 | tf_op jit(solution)/shard_map/ppermute | solution.py:477
  24.8 6.9 %collective-permute-start.10 = (bf16[4,32,1152]{2,1,0:T(8,128)(2,1)S(1)}, bf16[4,32,1152]{2,1,0:T(8,128)(2,1)S(1)}, u32[]{:S(2)}, u32[]{:S(2)}) collective-permute-start(bf16[4,32,1152]{2,1,0:T(8,128)(2,1)S(1)} %get-tuple-element.44), channel_id=1, source_target_pairs={{0,4},{4,0},{8,12},{12,8},{16,20},{20,16},{24,28},{28,24},{1,5},{5... | collective-permute-start | bytes 884744 | tf_op jit(solution)/shard_map/ppermute | solution.py:477
  24.9 10.3 %collective-permute-start.14 = (bf16[192,256]{1,0:T(8,128)(2,1)S(1)}, bf16[192,256]{1,0:T(8,128)(2,1)S(1)}, u32[]{:S(2)}, u32[]{:S(2)}) collective-permute-start(bf16[192,256]{1,0:T(8,128)(2,1)S(1)} %get-tuple-element.51), channel_id=1, source_target_pairs={{0,1},{1,2},{2,3},{3,0},{4,5},{5,6},{6,7},{7,4},{8,9},{9,10},{10,1... | collective-permute-start | bytes 294920 | tf_op jit(solution)/shard_map/ppermute | solution.py:463
  25.3 10.8 %collective-permute-start.15 = (bf16[192,256]{1,0:T(8,128)(2,1)S(1)}, bf16[192,256]{1,0:T(8,128)(2,1)S(1)}, u32[]{:S(2)}, u32[]{:S(2)}) collective-permute-start(bf16[192,256]{1,0:T(8,128)(2,1)S(1)} %get-tuple-element.52), channel_id=1, source_target_pairs={{0,2},{1,3},{2,0},{3,1},{4,6},{5,7},{6,4},{7,5},{8,10},{9,11},{10,... | collective-permute-start | bytes 294920 | tf_op jit(solution)/shard_map/ppermute | solution.py:463
  27.4 8.6 %collective-permute-start.16 = (bf16[192,256]{1,0:T(8,128)(2,1)S(1)}, bf16[192,256]{1,0:T(8,128)(2,1)S(1)}, u32[]{:S(2)}, u32[]{:S(2)}) collective-permute-start(bf16[192,256]{1,0:T(8,128)(2,1)S(1)} %get-tuple-element.53), channel_id=1, source_target_pairs={{0,3},{1,0},{2,1},{3,2},{4,7},{5,4},{6,5},{7,6},{8,11},{9,8},{10,9... | collective-permute-start | bytes 294920 | tf_op jit(solution)/shard_map/ppermute | solution.py:463
  28.8 10.8 %all-to-all-start.1 = ((bf16[32,2,640]{2,1,0:T(2,128)(2,1)}), bf16[32,2,640]{2,1,0:T(2,128)(2,1)S(1)}, u32[]{:S(2)}, u32[]{:S(2)}) async-start(bf16[32,2,640]{2,1,0:T(2,128)(2,1)} %get-tuple-element.42), calls=%async_computation.1 | async-start | bytes 163840 | tf_op jit(solution)/shard_map/all_to_all | solution.py:570
  31.9 7.8 %collective-permute-start.11 = (bf16[32,864]{1,0:T(8,128)(2,1)S(1)}, bf16[32,864]{1,0:T(8,128)(2,1)S(1)}, u32[]{:S(2)}, u32[]{:S(2)}) collective-permute-start(bf16[32,864]{1,0:T(8,128)(2,1)S(1)} %get-tuple-element.47), channel_id=1, source_target_pairs={{0,24},{4,28},{8,16},{12,20},{16,8},{20,12},{24,0},{28,4},{1,25},{... | collective-permute-start | bytes 165896 | tf_op jit(solution)/shard_map/ppermute | solution.py:472
  34.6 5.0 %collective-permute-start.12 = (bf16[32,864]{1,0:T(8,128)(2,1)S(1)}, bf16[32,864]{1,0:T(8,128)(2,1)S(1)}, u32[]{:S(2)}, u32[]{:S(2)}) collective-permute-start(bf16[32,864]{1,0:T(8,128)(2,1)S(1)} %get-tuple-element.48), channel_id=1, source_target_pairs={{0,16},{4,20},{8,24},{12,28},{16,0},{20,4},{24,8},{28,12},{1,17},{... | collective-permute-start | bytes 165896 | tf_op jit(solution)/shard_map/ppermute | solution.py:472
  35.2 4.5 %collective-permute-start.13 = (bf16[32,864]{1,0:T(8,128)(2,1)S(1)}, bf16[32,864]{1,0:T(8,128)(2,1)S(1)}, u32[]{:S(2)}, u32[]{:S(2)}) collective-permute-start(bf16[32,864]{1,0:T(8,128)(2,1)S(1)} %get-tuple-element.45.after_ref), channel_id=1, source_target_pairs={{0,8},{4,12},{8,0},{12,4},{16,24},{20,28},{24,16},{28,20},{1,9},{5... | collective-permute-start | bytes 165896 | tf_op jit(solution)/shard_map/ppermute | solution.py:472

commit v6 on v5

--- a/solution.py
+++ b/solution.py
@@ -80,12 +80,13 @@
     blocks_hbm,
     order_hbm,
     cot_hbm,
-    out_ref,
+    out_hbm,
     holds_ref,
     slots_ref,
     blocks_ref,
     order_ref,
     cot_ref,
+    out_ref,
     sems,
 ):
     devs, slab, slots, clips, held, och = dims
@@ -95,6 +96,16 @@
     for copy in copies:
         copy.wait()
     me = lax.axis_index("clips")
+    holders = slot_holders(blocks_ref, order_ref, me, slots, clips, held, devs)
+    for q in range(slots):
+        block = cot_ref[q].astype(F32)
+        for s in range(slab):
+            out_ref[holders[q] * slab + s] = fold(block, s, och, 8).astype(BF16)
+    out_copy = pltpu.make_async_copy(out_ref, out_hbm, sems.at[3])
+    out_copy.start()
+    for q in range(slots):
+        for d in range(devs):
+            holds_ref[q * devs + d] = jnp.full((1, LANES), jnp.where(holders[q] == d, 1.0, 0.0), F32)
     start = first_block_of(blocks_ref, me * held, clips)
     for k in range(held):
         count = blocks_ref[me * held + k]
@@ -104,13 +115,7 @@
                 hit = jnp.where(device == d, 1.0, 0.0)
                 slots_ref[(k * BMAX + b) * devs + d] = jnp.full((1, LANES), hit, F32)
         start = start + count
-    holders = slot_holders(blocks_ref, order_ref, me, slots, clips, held, devs)
-    for q in range(slots):
-        block = cot_ref[q].astype(F32)
-        for s in range(slab):
-            out_ref[holders[q] * slab + s] = fold(block, s, och, 8).astype(BF16)
-        for d in range(devs):
-            holds_ref[q * devs + d] = jnp.full((1, LANES), jnp.where(holders[q] == d, 1.0, 0.0), F32)
+    out_copy.wait()
 
 
 def make_table(och, out_ref):
@@ -391,22 +396,6 @@
     kernel_grad_ref, act_ref, gain_ref, bias_ref = out_refs
     copies = [pltpu.make_async_copy(a, b, sems.at[i]) for i, (a, b) in enumerate(zip(out_refs, hbm_refs))]
 
-    total = kernel_refs[0][...]
-    for ref in kernel_refs[1:]:
-        total = total + ref[...].astype(F32)
-    rows, cols = total.shape
-    width = table_ref.shape[0]
-    if width > cols:
-        total = jnp.concatenate([total, jnp.zeros((rows, width - cols), F32)], axis=1)
-    native = jnp.dot(
-        jnp.concatenate(split3(total), axis=0).astype(BF16),
-        table_ref[...],
-        preferred_element_type=F32,
-    )
-    native = native[:rows] + (native[rows : 2 * rows] + native[2 * rows :])
-    kernel_grad_ref[...] = native[:, :cols]
-    copies[0].start()
-
     groups = LANES // och
     pairs = act_in.shape[2] // LANES - 1
     sums = []
@@ -434,6 +423,22 @@
     bias_ref[...] = jnp.concatenate(biases, axis=1)
     copies[2].start()
     copies[3].start()
+    total = kernel_refs[0][...]
+    for ref in kernel_refs[1:]:
+        total = total + ref[...].astype(F32)
+    rows, cols = total.shape
+    width = table_ref.shape[0]
+    if width > cols:
+        total = jnp.concatenate([total, jnp.zeros((rows, width - cols), F32)], axis=1)
+    native = jnp.dot(
+        jnp.concatenate(split3(total), axis=0).astype(BF16),
+        table_ref[...],
+        preferred_element_type=F32,
+    )
+    native = native[:rows] + (native[rows : 2 * rows] + native[2 * rows :])
+    kernel_grad_ref[...] = native[:, :cols]
+    copies[0].start()
+
     for copy in copies:
         copy.wait()
 
@@ -505,10 +510,16 @@
     videos = shifts([video.reshape(places, c_in)] * slab, "slab")
     cots, holds, slot_of = call(
         functools.partial(send_kernel, (devs, slab, slots, clips, held, och)),
-        [shape((devs * slab, fold_rows, LANES), BF16), shape((slots * devs, 1, LANES), F32)]
+        [pltpu.HBM((devs * slab, fold_rows, LANES), BF16), shape((slots * devs, 1, LANES), F32)]
         + [shape((held * BMAX * devs, 1, LANES), F32)],
         [HBM, HBM, HBM],
-        smem + [pltpu.VMEM((slots, block_rows, c_out), BF16), pltpu.SemaphoreType.DMA((3,))],
+        smem
+        + [
+            pltpu.VMEM((slots, block_rows, c_out), BF16),
+            pltpu.VMEM((devs * slab, fold_rows, LANES), BF16),
+            pltpu.SemaphoreType.DMA((4,)),
+        ],
+        out_specs=[HBM, VMEM, VMEM],
         cost=pl.CostEstimate(flops=FIRST, bytes_accessed=0, transcendentals=0),
     )(clip_blocks, deal_order, cotangent_blocks)
     cots = lax.all_to_all(cots, everyone, split_axis=0, concat_axis=0, tiled=True)

time: 41.1 us -> 41.1 us (level)
  no operation moved by 1% of the time
where the time goes in v6:
time: 41.1 us; the launch traced here: 40.8 us
  starting transfers between devices  24.6 us (60%)
  Pallas kernels  10.7 us (26%)
  waiting for transfers between devices  4.58 us (11%)
  between operations  0.81 us (2%)
    ppermute x6, starting transfers between devices, shifts(): lax.ppermute(arrays[i], axis, [(j, (j + i) % size) for j in range(size)])  9.44 us
    ppermute x3, starting transfers between devices, body(): shards = shards + [lax.ppermute(shard, 'clips', pairs) for shard in shards]  5.03 us
    ppermute x3, starting transfers between devices, chip_swaps(): moved.append(lax.ppermute(arrays[t], axis, pairs))  3.55 us
    pallas_call x1, Pallas kernels, body(): call(functools.partial(forward_kernel, dims), [shape((9 * LANES, c_in), B...  3.44 us
    all_to_all x1, starting transfers between devices, body(): lax.all_to_all(acts, everyone, split_axis=0, concat_axis=0, tiled=True)  2.85 us
    all_to_all x1, starting transfers between devices, body(): lax.all_to_all(cots, everyone, split_axis=0, concat_axis=0, tiled=True)  2.59 us
    all_to_all x1, waiting for transfers between devices, body(): lax.all_to_all(acts, everyone, split_axis=0, concat_axis=0, tiled=True)  2.01 us
    all_to_all x1, waiting for transfers between devices, body(): lax.all_to_all(cots, everyone, split_axis=0, concat_axis=0, tiled=True)  1.91 us
  transfers between devices with their start and end apart: 19, of which 3 were waited for; matrix products, arithmetic and copies ran while one was open for 0% of the time, Pallas kernels for 19%

profile of v6, /device:TPU:0, one launch (start us, length us, event | category | flops | bytes accessed | tf_op | source)
XLA Modules:
  0.0 40.8 jit_solution(16430316782036490536)
XLA Ops:
  0.6 3.0 %collective-permute-start = (bf16[32,864]{1,0:T(8,128)(2,1)}, bf16[32,864]{1,0:T(8,128)(2,1)S(1)}, u32[]{:S(2)}, u32[]{:S(2)}) collective-permute-start(bf16[32,864]{1,0:T(8,128)(2,1)} %refs_0_.1), channel_id=1, source_target_pairs={{0,8},{4,12},{8,0},{12,4},{16,24},{20,28},{24,16},{28,20},{1,9},{5... | collective-permute-start | bytes 165896 | tf_op jit(solution)/shard_map/ppermute | solution.py:529
  3.6 1.6 %collective-permute-start.9 = (bf16[192,256]{1,0:T(8,128)(2,1)}, bf16[192,256]{1,0:T(8,128)(2,1)S(1)}, u32[]{:S(2)}, u32[]{:S(2)}) collective-permute-start(bf16[192,256]{1,0:T(8,128)(2,1)} %bitcast.16), channel_id=1, source_target_pairs={{0,1},{1,2},{2,3},{3,0},{4,5},{5,6},{6,7},{7,4},{8,9},{9,10},{10,1... | collective-permute-start | bytes 294920 | tf_op jit(solution)/shard_map/ppermute | solution.py:468
  5.2 2.6 %collective-permute-start.8 = (bf16[192,256]{1,0:T(8,128)(2,1)}, bf16[192,256]{1,0:T(8,128)(2,1)S(1)}, u32[]{:S(2)}, u32[]{:S(2)}) collective-permute-start(bf16[192,256]{1,0:T(8,128)(2,1)} %bitcast.17), channel_id=1, source_target_pairs={{0,2},{1,3},{2,0},{3,1},{4,6},{5,7},{6,4},{7,5},{8,10},{9,11},{10,... | collective-permute-start | bytes 294920 | tf_op jit(solution)/shard_map/ppermute | solution.py:468
  7.8 1.3 %collective-permute-start.7 = (bf16[192,256]{1,0:T(8,128)(2,1)}, bf16[192,256]{1,0:T(8,128)(2,1)S(1)}, u32[]{:S(2)}, u32[]{:S(2)}) collective-permute-start(bf16[192,256]{1,0:T(8,128)(2,1)} %bitcast.18), channel_id=1, source_target_pairs={{0,3},{1,0},{2,1},{3,2},{4,7},{5,4},{6,5},{7,6},{8,11},{9,8},{10,9... | collective-permute-start | bytes 294920 | tf_op jit(solution)/shard_map/ppermute | solution.py:468
  9.2 1.5 %collective-permute-start.1 = (bf16[32,864]{1,0:T(8,128)(2,1)}, bf16[32,864]{1,0:T(8,128)(2,1)S(1)}, u32[]{:S(2)}, u32[]{:S(2)}) collective-permute-start(bf16[32,864]{1,0:T(8,128)(2,1)} %refs_0_.1), channel_id=1, source_target_pairs={{0,16},{4,20},{8,24},{12,28},{16,0},{20,4},{24,8},{28,12},{1,17},{... | collective-permute-start | bytes 165896 | tf_op jit(solution)/shard_map/ppermute | solution.py:529
  10.7 0.5 %collective-permute-start.2 = (bf16[32,864]{1,0:T(8,128)(2,1)S(1)}, bf16[32,864]{1,0:T(8,128)(2,1)S(1)}, u32[]{:S(2)}, u32[]{:S(2)}) collective-permute-start(bf16[32,864]{1,0:T(8,128)(2,1)S(1)} %collective-permute-done.refs_1_), channel_id=1, source_target_pairs={{0,16},{4,20},{8,24},{12,28},{16,0},{20,4},{24,8},{28,12},{1,17},{... | collective-permute-start | bytes 165896 | tf_op jit(solution)/shard_map/ppermute | solution.py:529
  11.2 1.6 %shard_map.110 = (bf16[32,8,128]{2,1,0:T(8,128)(2,1)}, f32[32,1,128]{2,1,0:T(1,128)S(1)}, f32[48,1,128]{2,1,0:T(1,128)S(1)}) custom-call(s32[16]{0:T(128)} %blocks_hbm.3, s32[8]{0:T(128)} %order_hbm.1, bf16[4,32,128]{2,1,0:T(8,128)(2,1)} %bitcast.15), custom_call_target="tpu_custom_call" | custom-call | flops 1000000 | tf_op jit(solution)/shard_map/pallas_call | solution.py:511
  12.8 2.6 %all-to-all-start = ((bf16[32,8,128]{2,1,0:T(8,128)(2,1)}), bf16[32,8,128]{2,1,0:T(8,128)(2,1)S(1)}, u32[]{:S(2)}, u32[]{:S(2)}) async-start(bf16[32,8,128]{2,1,0:T(8,128)(2,1)} %get-tuple-element.41), calls=%async_computation | async-start | bytes 131072 | tf_op jit(solution)/shard_map/all_to_all | solution.py:525
  15.6 0.4 collective-permute-start.4
  16.2 0.4 collective-permute-start.6
  16.6 0.9 %shard_map.111 = (bf16[6,192,256]{2,1,0:T(8,128)(2,1)S(1)}, bf16[896,1152]{1,0:T(8,128)(2,1)S(1)}) custom-call(bf16[192,256]{1,0:T(8,128)(2,1)} %bitcast.19, bf16[192,256]{1,0:T(8,128)(2,1)S(1)} %collective-permute-done.7.refs_1_, bf16[192,256]{1,0:T(8,128)(2,1)S(1)} %collective-permute-done.8.refs_2_, bf16[192,256]{1,0:T(8,128)(2,1)S(1)} %collective-permute-done.9.refs_3_), custom_call_target="tpu_custom_call" | custom-call | flops 10000000000 | tf_op jit(solution)/shard_map/pallas_call | solution.py:533
  17.5 3.4 %shard_map.112 = (bf16[1152,256]{1,0:T(8,128)(2,1)S(1)}, bf16[256,768]{1,0:T(8,128)(2,1)S(1)}, f32[4,192,32]{2,1,0:T(8,128)S(1)}, f32[2,8,32]{2,1,0:T(8,128)S(1)...) custom-call(s32[16]{0:T(128)} %blocks_hbm.3, f32[48,1,128]{2,1,0:T(1,128)S(1)} %get-tuple-element.32.slots_ref, ...), custom_call_target="tpu_custom_call" | custom-call | tf_op jit(solution)/shard_map/pallas_call | solution.py:540
  21.0 1.9 %all-to-all-done.refs_5_ = bf16[32,8,128]{2,1,0:T(8,128)(2,1)S(1)} async-done(((bf16[32,8,128]{2,1,0:T(8,128)(2,1)}), bf16[32,8,128]{2,1,0:T(8,128)(2,1)S(1)}, u32[]{:S(2)}, u32[]{:S(2)}) %all-to-all-start) | async-done | bytes 65568 | tf_op jit(solution)/shard_map/all_to_all | solution.py:525
  22.9 1.9 %shard_map.113 = (bf16[32,2,640]{2,1,0:T(2,128)(2,1)}, f32[4,32,1152]{2,1,0:T(8,128)S(1)}, bf16[4,32,1152]{2,1,0:T(8,128)(2,1)S(1)}, f32[192,256]{1,0:T(8,128)S(...) custom-call(f32[48,1,128]{2,1,0:T(1,128)S(1)} %get-tuple-element.32., ...), custom_call_target="tpu_custom_call", output_to_operand_aliasing={{0}: (7, {})} | custom-call | tf_op jit(solution)/shard_map/pallas_call | solution.py:560
  25.3 2.2 %collective-permute-start.15 = (bf16[192,256]{1,0:T(8,128)(2,1)S(1)}, bf16[192,256]{1,0:T(8,128)(2,1)S(1)}, u32[]{:S(2)}, u32[]{:S(2)}) collective-permute-start(bf16[192,256]{1,0:T(8,128)(2,1)S(1)} %get-tuple-element.52), channel_id=1, source_target_pairs={{0,2},{1,3},{2,0},{3,1},{4,6},{5,7},{6,4},{7,5},{8,10},{9,11},{10,... | collective-permute-start | bytes 294920 | tf_op jit(solution)/shard_map/ppermute | solution.py:468
  27.4 1.4 %collective-permute-start.16 = (bf16[192,256]{1,0:T(8,128)(2,1)S(1)}, bf16[192,256]{1,0:T(8,128)(2,1)S(1)}, u32[]{:S(2)}, u32[]{:S(2)}) collective-permute-start(bf16[192,256]{1,0:T(8,128)(2,1)S(1)} %get-tuple-element.53), channel_id=1, source_target_pairs={{0,3},{1,0},{2,1},{3,2},{4,7},{5,4},{6,5},{7,6},{8,11},{9,8},{10,9... | collective-permute-start | bytes 294920 | tf_op jit(solution)/shard_map/ppermute | solution.py:468
  28.8 2.9 %all-to-all-start.1 = ((bf16[32,2,640]{2,1,0:T(2,128)(2,1)}), bf16[32,2,640]{2,1,0:T(2,128)(2,1)S(1)}, u32[]{:S(2)}, u32[]{:S(2)}) async-start(bf16[32,2,640]{2,1,0:T(2,128)(2,1)} %get-tuple-element.42), calls=%async_computation.1 | async-start | bytes 163840 | tf_op jit(solution)/shard_map/all_to_all | solution.py:581
  31.9 2.7 %collective-permute-start.11 = (bf16[32,864]{1,0:T(8,128)(2,1)S(1)}, bf16[32,864]{1,0:T(8,128)(2,1)S(1)}, u32[]{:S(2)}, u32[]{:S(2)}) collective-permute-start(bf16[32,864]{1,0:T(8,128)(2,1)S(1)} %get-tuple-element.47), channel_id=1, source_target_pairs={{0,24},{4,28},{8,16},{12,20},{16,8},{20,12},{24,0},{28,4},{1,25},{... | collective-permute-start | bytes 165896 | tf_op jit(solution)/shard_map/ppermute | solution.py:477
  34.6 0.6 %collective-permute-start.12 = (bf16[32,864]{1,0:T(8,128)(2,1)S(1)}, bf16[32,864]{1,0:T(8,128)(2,1)S(1)}, u32[]{:S(2)}, u32[]{:S(2)}) collective-permute-start(bf16[32,864]{1,0:T(8,128)(2,1)S(1)} %get-tuple-element.48), channel_id=1, source_target_pairs={{0,16},{4,20},{8,24},{12,28},{16,0},{20,4},{24,8},{28,12},{1,17},{... | collective-permute-start | bytes 165896 | tf_op jit(solution)/shard_map/ppermute | solution.py:477
  35.4 0.6 %collective-permute-done.15.refs_2_ = bf16[192,256]{1,0:T(8,128)(2,1)S(1)} collective-permute-done((bf16[192,256]{1,0:T(8,128)(2,1)S(1)}, bf16[192,256]{1,0:T(8,128)(2,1)S(1)}, u32[]{:S(2)}, u32[]{:S(2)}) %collective-permute-start.15) | collective-permute-done | bytes 98336 | tf_op jit(solution)/shard_map/ppermute | solution.py:468
  36.0 0.7 %shard_map.117 = bf16[192,256]{1,0:T(8,128)(2,1)} custom-call(f32[192,256]{1,0:T(8,128)S(1)} %get-tuple-element.50.refs_0_, bf16[192,256]{1,0:T(8,128)(2,1)S(1)} %collective-permute-done.14.refs_1_, bf16[192,256]{1,0:T(8,128)(2,1)S(1)} %collective-permute-done.15.refs_2_, bf16[192,256]{1,0:T(8,128)(2,1)S(1)} %collective-permute-done.16.refs_3_), custom_call_target="tpu_custom_call" | custom-call | flops 10000000000 | tf_op jit(solution)/shard_map/pallas_call | solution.py:592
  36.7 0.9 %shard_map.115.table_ref = bf16[896,896]{1,0:T(8,128)(2,1)S(1)} custom-call(bf16[32,864]{1,0:T(8,128)(2,1)S(1)} %get-tuple-element.45.after_ref), custom_call_target="tpu_custom_call" | custom-call | tf_op jit(solution)/shard_map/pallas_call | solution.py:587
  37.6 2.0 %all-to-all-done.1.act_in = bf16[32,2,640]{2,1,0:T(2,128)(2,1)S(1)} async-done(((bf16[32,2,640]{2,1,0:T(2,128)(2,1)}), bf16[32,2,640]{2,1,0:T(2,128)(2,1)S(1)}, u32[]{:S(2)}, u32[]{:S(2)}) %all-to-all-start.1) | async-done | bytes 81952 | tf_op jit(solution)/shard_map/all_to_all | solution.py:581
  39.6 1.1 %shard_map.116 = (f32[32,864]{1,0:T(8,128)}, bf16[4,32,128]{2,1,0:T(8,128)(2,1)}, f32[1,128]{1,0:T(1,128)}, f32[1,128]{1,0:T(1,128)}) custom-call(f32[32,1,128]{2,1,0:T(1,128)S(1)} %get-tuple-element.31.holds_ref, bf16[32,2,640]{2,1,0:T(2,128)(2,1)S(1)} %all-to-all-done.1.act_in, bf16[896,896]{1,0:T(8,128)(2,1)S(1)} %shard_map.115.table_ref, ...), custom_call_target="tpu_custom_call" | custom-call | tf_op jit(solution)/shard_map/pallas_call | solution.py:604
  (28 shorter events, 1.2 us)
Async XLA Ops:
  0.6 10.0 %collective-permute-start = (bf16[32,864]{1,0:T(8,128)(2,1)}, bf16[32,864]{1,0:T(8,128)(2,1)S(1)}, u32[]{:S(2)}, u32[]{:S(2)}) collective-permute-start(bf16[32,864]{1,0:T(8,128)(2,1)} %refs_0_.1), channel_id=1, source_target_pairs={{0,8},{4,12},{8,0},{12,4},{16,24},{20,28},{24,16},{28,20},{1,9},{5... | collective-permute-start | bytes 165896 | tf_op jit(solution)/shard_map/ppermute | solution.py:529
  3.6 12.0 %collective-permute-start.9 = (bf16[192,256]{1,0:T(8,128)(2,1)}, bf16[192,256]{1,0:T(8,128)(2,1)S(1)}, u32[]{:S(2)}, u32[]{:S(2)}) collective-permute-start(bf16[192,256]{1,0:T(8,128)(2,1)} %bitcast.16), channel_id=1, source_target_pairs={{0,1},{1,2},{2,3},{3,0},{4,5},{5,6},{6,7},{7,4},{8,9},{9,10},{10,1... | collective-permute-start | bytes 294920 | tf_op jit(solution)/shard_map/ppermute | solution.py:468
  5.2 10.8 %collective-permute-start.8 = (bf16[192,256]{1,0:T(8,128)(2,1)}, bf16[192,256]{1,0:T(8,128)(2,1)S(1)}, u32[]{:S(2)}, u32[]{:S(2)}) collective-permute-start(bf16[192,256]{1,0:T(8,128)(2,1)} %bitcast.17), channel_id=1, source_target_pairs={{0,2},{1,3},{2,0},{3,1},{4,6},{5,7},{6,4},{7,5},{8,10},{9,11},{10,... | collective-permute-start | bytes 294920 | tf_op jit(solution)/shard_map/ppermute | solution.py:468
  7.8 8.8 %collective-permute-start.7 = (bf16[192,256]{1,0:T(8,128)(2,1)}, bf16[192,256]{1,0:T(8,128)(2,1)S(1)}, u32[]{:S(2)}, u32[]{:S(2)}) collective-permute-start(bf16[192,256]{1,0:T(8,128)(2,1)} %bitcast.18), channel_id=1, source_target_pairs={{0,3},{1,0},{2,1},{3,2},{4,7},{5,4},{6,5},{7,6},{8,11},{9,8},{10,9... | collective-permute-start | bytes 294920 | tf_op jit(solution)/shard_map/ppermute | solution.py:468
  9.2 6.3 %collective-permute-start.1 = (bf16[32,864]{1,0:T(8,128)(2,1)}, bf16[32,864]{1,0:T(8,128)(2,1)S(1)}, u32[]{:S(2)}, u32[]{:S(2)}) collective-permute-start(bf16[32,864]{1,0:T(8,128)(2,1)} %refs_0_.1), channel_id=1, source_target_pairs={{0,16},{4,20},{8,24},{12,28},{16,0},{20,4},{24,8},{28,12},{1,17},{... | collective-permute-start | bytes 165896 | tf_op jit(solution)/shard_map/ppermute | solution.py:529
  10.7 5.5 %collective-permute-start.2 = (bf16[32,864]{1,0:T(8,128)(2,1)S(1)}, bf16[32,864]{1,0:T(8,128)(2,1)S(1)}, u32[]{:S(2)}, u32[]{:S(2)}) collective-permute-start(bf16[32,864]{1,0:T(8,128)(2,1)S(1)} %collective-permute-done.refs_1_), channel_id=1, source_target_pairs={{0,16},{4,20},{8,24},{12,28},{16,0},{20,4},{24,8},{28,12},{1,17},{... | collective-permute-start | bytes 165896 | tf_op jit(solution)/shard_map/ppermute | solution.py:529
  12.8 10.1 %all-to-all-start = ((bf16[32,8,128]{2,1,0:T(8,128)(2,1)}), bf16[32,8,128]{2,1,0:T(8,128)(2,1)S(1)}, u32[]{:S(2)}, u32[]{:S(2)}) async-start(bf16[32,8,128]{2,1,0:T(8,128)(2,1)} %get-tuple-element.41), calls=%async_computation | async-start | bytes 131072 | tf_op jit(solution)/shard_map/all_to_all | solution.py:525
  15.4 2.1 %copy-start = (bf16[32,864]{1,0:T(8,128)(2,1)S(1)}, bf16[32,864]{1,0:T(8,128)(2,1)}, u32[]{:S(2)}) copy-start(bf16[32,864]{1,0:T(8,128)(2,1)} %refs_0_.1) | copy-start | bytes 165892
  15.4 2.1 %copy-start.1 = (f32[128]{0:T(128)S(1)}, f32[128]{0:T(128)}, u32[]{:S(2)}) copy-start(f32[128]{0:T(128)} %param.11) | copy-start | bytes 1540
  15.4 2.1 %copy-start.2 = (f32[128]{0:T(128)S(1)}, f32[128]{0:T(128)}, u32[]{:S(2)}) copy-start(f32[128]{0:T(128)} %param.12) | copy-start | bytes 1540
  15.5 2.0 %collective-permute-start.3 = (bf16[32,864]{1,0:T(8,128)(2,1)}, bf16[32,864]{1,0:T(8,128)(2,1)S(1)}, u32[]{:S(2)}, u32[]{:S(2)}) collective-permute-start(bf16[32,864]{1,0:T(8,128)(2,1)} %refs_0_.1), channel_id=1, source_target_pairs={{0,4},{4,0},{8,12},{12,8},{16,20},{20,16},{24,28},{28,24},{1,5},{5... | collective-permute-start | bytes 165896 | tf_op jit(solution)/shard_map/ppermute | solution.py:482
  15.6 1.9 %collective-permute-start.4 = (bf16[32,864]{1,0:T(8,128)(2,1)S(1)}, bf16[32,864]{1,0:T(8,128)(2,1)S(1)}, u32[]{:S(2)}, u32[]{:S(2)}) collective-permute-start(bf16[32,864]{1,0:T(8,128)(2,1)S(1)} %collective-permute-done.refs_1_), channel_id=1, source_target_pairs={{0,4},{4,0},{8,12},{12,8},{16,20},{20,16},{24,28},{28,24},{1,5},{5... | collective-permute-start | bytes 165896 | tf_op jit(solution)/shard_map/ppermute | solution.py:482
  16.0 1.4 %collective-permute-start.5 = (bf16[32,864]{1,0:T(8,128)(2,1)S(1)}, bf16[32,864]{1,0:T(8,128)(2,1)S(1)}, u32[]{:S(2)}, u32[]{:S(2)}) collective-permute-start(bf16[32,864]{1,0:T(8,128)(2,1)S(1)} %collective-permute-done.1.refs_2_), channel_id=1, source_target_pairs={{0,4},{4,0},{8,12},{12,8},{16,20},{20,16},{24,28},{28,24},{1,5},{5... | collective-permute-start | bytes 165896 | tf_op jit(solution)/shard_map/ppermute | solution.py:482
  16.2 1.4 %collective-permute-start.6 = (bf16[32,864]{1,0:T(8,128)(2,1)S(1)}, bf16[32,864]{1,0:T(8,128)(2,1)S(1)}, u32[]{:S(2)}, u32[]{:S(2)}) collective-permute-start(bf16[32,864]{1,0:T(8,128)(2,1)S(1)} %collective-permute-done.2.refs_3_), channel_id=1, source_target_pairs={{0,4},{4,0},{8,12},{12,8},{16,20},{20,16},{24,28},{28,24},{1,5},{5... | collective-permute-start | bytes 165896 | tf_op jit(solution)/shard_map/ppermute | solution.py:482
  24.8 6.9 %collective-permute-start.10 = (bf16[4,32,1152]{2,1,0:T(8,128)(2,1)S(1)}, bf16[4,32,1152]{2,1,0:T(8,128)(2,1)S(1)}, u32[]{:S(2)}, u32[]{:S(2)}) collective-permute-start(bf16[4,32,1152]{2,1,0:T(8,128)(2,1)S(1)} %get-tuple-element.44), channel_id=1, source_target_pairs={{0,4},{4,0},{8,12},{12,8},{16,20},{20,16},{24,28},{28,24},{1,5},{5... | collective-permute-start | bytes 884744 | tf_op jit(solution)/shard_map/ppermute | solution.py:482
  24.9 10.3 %collective-permute-start.14 = (bf16[192,256]{1,0:T(8,128)(2,1)S(1)}, bf16[192,256]{1,0:T(8,128)(2,1)S(1)}, u32[]{:S(2)}, u32[]{:S(2)}) collective-permute-start(bf16[192,256]{1,0:T(8,128)(2,1)S(1)} %get-tuple-element.51), channel_id=1, source_target_pairs={{0,1},{1,2},{2,3},{3,0},{4,5},{5,6},{6,7},{7,4},{8,9},{9,10},{10,1... | collective-permute-start | bytes 294920 | tf_op jit(solution)/shard_map/ppermute | solution.py:468
  25.3 10.8 %collective-permute-start.15 = (bf16[192,256]{1,0:T(8,128)(2,1)S(1)}, bf16[192,256]{1,0:T(8,128)(2,1)S(1)}, u32[]{:S(2)}, u32[]{:S(2)}) collective-permute-start(bf16[192,256]{1,0:T(8,128)(2,1)S(1)} %get-tuple-element.52), channel_id=1, source_target_pairs={{0,2},{1,3},{2,0},{3,1},{4,6},{5,7},{6,4},{7,5},{8,10},{9,11},{10,... | collective-permute-start | bytes 294920 | tf_op jit(solution)/shard_map/ppermute | solution.py:468
  27.4 8.6 %collective-permute-start.16 = (bf16[192,256]{1,0:T(8,128)(2,1)S(1)}, bf16[192,256]{1,0:T(8,128)(2,1)S(1)}, u32[]{:S(2)}, u32[]{:S(2)}) collective-permute-start(bf16[192,256]{1,0:T(8,128)(2,1)S(1)} %get-tuple-element.53), channel_id=1, source_target_pairs={{0,3},{1,0},{2,1},{3,2},{4,7},{5,4},{6,5},{7,6},{8,11},{9,8},{10,9... | collective-permute-start | bytes 294920 | tf_op jit(solution)/shard_map/ppermute | solution.py:468
  28.8 10.8 %all-to-all-start.1 = ((bf16[32,2,640]{2,1,0:T(2,128)(2,1)}), bf16[32,2,640]{2,1,0:T(2,128)(2,1)S(1)}, u32[]{:S(2)}, u32[]{:S(2)}) async-start(bf16[32,2,640]{2,1,0:T(2,128)(2,1)} %get-tuple-element.42), calls=%async_computation.1 | async-start | bytes 163840 | tf_op jit(solution)/shard_map/all_to_all | solution.py:581
  31.9 7.8 %collective-permute-start.11 = (bf16[32,864]{1,0:T(8,128)(2,1)S(1)}, bf16[32,864]{1,0:T(8,128)(2,1)S(1)}, u32[]{:S(2)}, u32[]{:S(2)}) collective-permute-start(bf16[32,864]{1,0:T(8,128)(2,1)S(1)} %get-tuple-element.47), channel_id=1, source_target_pairs={{0,24},{4,28},{8,16},{12,20},{16,8},{20,12},{24,0},{28,4},{1,25},{... | collective-permute-start | bytes 165896 | tf_op jit(solution)/shard_map/ppermute | solution.py:477
  34.6 5.0 %collective-permute-start.12 = (bf16[32,864]{1,0:T(8,128)(2,1)S(1)}, bf16[32,864]{1,0:T(8,128)(2,1)S(1)}, u32[]{:S(2)}, u32[]{:S(2)}) collective-permute-start(bf16[32,864]{1,0:T(8,128)(2,1)S(1)} %get-tuple-element.48), channel_id=1, source_target_pairs={{0,16},{4,20},{8,24},{12,28},{16,0},{20,4},{24,8},{28,12},{1,17},{... | collective-permute-start | bytes 165896 | tf_op jit(solution)/shard_map/ppermute | solution.py:477
  35.2 4.5 %collective-permute-start.13 = (bf16[32,864]{1,0:T(8,128)(2,1)S(1)}, bf16[32,864]{1,0:T(8,128)(2,1)S(1)}, u32[]{:S(2)}, u32[]{:S(2)}) collective-permute-start(bf16[32,864]{1,0:T(8,128)(2,1)S(1)} %get-tuple-element.45.after_ref), channel_id=1, source_target_pairs={{0,8},{4,12},{8,0},{12,4},{16,24},{20,28},{24,16},{28,20},{1,9},{5... | collective-permute-start | bytes 165896 | tf_op jit(solution)/shard_map/ppermute | solution.py:477

commit v7 on v5

--- a/solution.py
+++ b/solution.py
@@ -597,7 +597,7 @@
         [pltpu.VMEM(*out) for out in outs] + [pltpu.SemaphoreType.DMA((4,))],
         2 * slab * MIB,
         [HBM] * 4,
-    )(holds, acts, table, kernel_grads[0], *kernel_grads[:0:-1])
+    )(holds, acts, table, kernel_grads[0], *kernel_grads[2:], kernel_grads[1])
     return (
         act.reshape(cotangent.shape),
         video_grad.reshape(video.shape),

time: 41.1 us -> 41.1 us (level)
  no operation moved by 1% of the time
where the time goes in v7:
time: 41.1 us; the launch traced here: 40.8 us
  starting transfers between devices  24.6 us (60%)
  Pallas kernels  10.7 us (26%)
  waiting for transfers between devices  4.61 us (11%)
  between operations  0.81 us (2%)
    ppermute x6, starting transfers between devices, shifts(): lax.ppermute(arrays[i], axis, [(j, (j + i) % size) for j in range(size)])  9.44 us
    ppermute x3, starting transfers between devices, body(): shards = shards + [lax.ppermute(shard, 'clips', pairs) for shard in shards]  5.03 us
    ppermute x3, starting transfers between devices, chip_swaps(): moved.append(lax.ppermute(arrays[t], axis, pairs))  3.55 us
    pallas_call x1, Pallas kernels, body(): call(functools.partial(forward_kernel, dims), [shape((9 * LANES, c_in), B...  3.44 us
    all_to_all x1, starting transfers between devices, body(): lax.all_to_all(acts, everyone, split_axis=0, concat_axis=0, tiled=True)  2.85 us
    all_to_all x1, starting transfers between devices, body(): lax.all_to_all(cots, everyone, split_axis=0, concat_axis=0, tiled=True)  2.59 us
    all_to_all x1, waiting for transfers between devices, body(): lax.all_to_all(acts, everyone, split_axis=0, concat_axis=0, tiled=True)  2.02 us
    all_to_all x1, waiting for transfers between devices, body(): lax.all_to_all(cots, everyone, split_axis=0, concat_axis=0, tiled=True)  1.91 us
  transfers between devices with their start and end apart: 19, of which 3 were waited for; matrix products, arithmetic and copies ran while one was open for 0% of the time, Pallas kernels for 19%

profile of v7, /device:TPU:0, one launch (start us, length us, event | category | flops | bytes accessed | tf_op | source)
XLA Modules:
  0.0 40.8 jit_solution(1654044623948297394)
XLA Ops:
  0.6 3.0 %collective-permute-start = (bf16[32,864]{1,0:T(8,128)(2,1)}, bf16[32,864]{1,0:T(8,128)(2,1)S(1)}, u32[]{:S(2)}, u32[]{:S(2)}) collective-permute-start(bf16[32,864]{1,0:T(8,128)(2,1)} %refs_0_.1), channel_id=1, source_target_pairs={{0,8},{4,12},{8,0},{12,4},{16,24},{20,28},{24,16},{28,20},{1,9},{5... | collective-permute-start | bytes 165896 | tf_op jit(solution)/shard_map/ppermute | solution.py:518
  3.6 1.6 %collective-permute-start.9 = (bf16[192,256]{1,0:T(8,128)(2,1)}, bf16[192,256]{1,0:T(8,128)(2,1)S(1)}, u32[]{:S(2)}, u32[]{:S(2)}) collective-permute-start(bf16[192,256]{1,0:T(8,128)(2,1)} %bitcast.16), channel_id=1, source_target_pairs={{0,1},{1,2},{2,3},{3,0},{4,5},{5,6},{6,7},{7,4},{8,9},{9,10},{10,1... | collective-permute-start | bytes 294920 | tf_op jit(solution)/shard_map/ppermute | solution.py:463
  5.2 2.6 %collective-permute-start.8 = (bf16[192,256]{1,0:T(8,128)(2,1)}, bf16[192,256]{1,0:T(8,128)(2,1)S(1)}, u32[]{:S(2)}, u32[]{:S(2)}) collective-permute-start(bf16[192,256]{1,0:T(8,128)(2,1)} %bitcast.17), channel_id=1, source_target_pairs={{0,2},{1,3},{2,0},{3,1},{4,6},{5,7},{6,4},{7,5},{8,10},{9,11},{10,... | collective-permute-start | bytes 294920 | tf_op jit(solution)/shard_map/ppermute | solution.py:463
  7.8 1.3 %collective-permute-start.7 = (bf16[192,256]{1,0:T(8,128)(2,1)}, bf16[192,256]{1,0:T(8,128)(2,1)S(1)}, u32[]{:S(2)}, u32[]{:S(2)}) collective-permute-start(bf16[192,256]{1,0:T(8,128)(2,1)} %bitcast.18), channel_id=1, source_target_pairs={{0,3},{1,0},{2,1},{3,2},{4,7},{5,4},{6,5},{7,6},{8,11},{9,8},{10,9... | collective-permute-start | bytes 294920 | tf_op jit(solution)/shard_map/ppermute | solution.py:463
  9.2 1.5 %collective-permute-start.1 = (bf16[32,864]{1,0:T(8,128)(2,1)}, bf16[32,864]{1,0:T(8,128)(2,1)S(1)}, u32[]{:S(2)}, u32[]{:S(2)}) collective-permute-start(bf16[32,864]{1,0:T(8,128)(2,1)} %refs_0_.1), channel_id=1, source_target_pairs={{0,16},{4,20},{8,24},{12,28},{16,0},{20,4},{24,8},{28,12},{1,17},{... | collective-permute-start | bytes 165896 | tf_op jit(solution)/shard_map/ppermute | solution.py:518
  10.7 0.5 %collective-permute-start.2 = (bf16[32,864]{1,0:T(8,128)(2,1)S(1)}, bf16[32,864]{1,0:T(8,128)(2,1)S(1)}, u32[]{:S(2)}, u32[]{:S(2)}) collective-permute-start(bf16[32,864]{1,0:T(8,128)(2,1)S(1)} %collective-permute-done.refs_1_), channel_id=1, source_target_pairs={{0,16},{4,20},{8,24},{12,28},{16,0},{20,4},{24,8},{28,12},{1,17},{... | collective-permute-start | bytes 165896 | tf_op jit(solution)/shard_map/ppermute | solution.py:518
  11.2 1.6 %shard_map.110 = (bf16[32,8,128]{2,1,0:T(8,128)(2,1)}, f32[32,1,128]{2,1,0:T(1,128)S(1)}, f32[48,1,128]{2,1,0:T(1,128)S(1)}) custom-call(s32[16]{0:T(128)} %blocks_hbm.3, s32[8]{0:T(128)} %order_hbm.1, bf16[4,32,128]{2,1,0:T(8,128)(2,1)} %bitcast.15), custom_call_target="tpu_custom_call" | custom-call | flops 1000000 | tf_op jit(solution)/shard_map/pallas_call | solution.py:506
  12.8 2.6 %all-to-all-start = ((bf16[32,8,128]{2,1,0:T(8,128)(2,1)}), bf16[32,8,128]{2,1,0:T(8,128)(2,1)S(1)}, u32[]{:S(2)}, u32[]{:S(2)}) async-start(bf16[32,8,128]{2,1,0:T(8,128)(2,1)} %get-tuple-element.41), calls=%async_computation | async-start | bytes 131072 | tf_op jit(solution)/shard_map/all_to_all | solution.py:514
  15.6 0.4 collective-permute-start.4
  16.1 0.4 collective-permute-start.6
  16.5 0.9 %shard_map.111 = (bf16[6,192,256]{2,1,0:T(8,128)(2,1)S(1)}, bf16[896,1152]{1,0:T(8,128)(2,1)S(1)}) custom-call(bf16[192,256]{1,0:T(8,128)(2,1)} %bitcast.19, bf16[192,256]{1,0:T(8,128)(2,1)S(1)} %collective-permute-done.7.refs_1_, bf16[192,256]{1,0:T(8,128)(2,1)S(1)} %collective-permute-done.8.refs_2_, bf16[192,256]{1,0:T(8,128)(2,1)S(1)} %collective-permute-done.9.refs_3_), custom_call_target="tpu_custom_call" | custom-call | flops 10000000000 | tf_op jit(solution)/shard_map/pallas_call | solution.py:522
  17.5 3.4 %shard_map.112 = (bf16[1152,256]{1,0:T(8,128)(2,1)S(1)}, bf16[256,768]{1,0:T(8,128)(2,1)S(1)}, f32[4,192,32]{2,1,0:T(8,128)S(1)}, f32[2,8,32]{2,1,0:T(8,128)S(1)...) custom-call(s32[16]{0:T(128)} %blocks_hbm.3, f32[48,1,128]{2,1,0:T(1,128)S(1)} %get-tuple-element.32.slots_ref, ...), custom_call_target="tpu_custom_call" | custom-call | tf_op jit(solution)/shard_map/pallas_call | solution.py:529
  21.0 1.9 %all-to-all-done.refs_5_ = bf16[32,8,128]{2,1,0:T(8,128)(2,1)S(1)} async-done(((bf16[32,8,128]{2,1,0:T(8,128)(2,1)}), bf16[32,8,128]{2,1,0:T(8,128)(2,1)S(1)}, u32[]{:S(2)}, u32[]{:S(2)}) %all-to-all-start) | async-done | bytes 65568 | tf_op jit(solution)/shard_map/all_to_all | solution.py:514
  22.9 1.9 %shard_map.113 = (bf16[32,2,640]{2,1,0:T(2,128)(2,1)}, f32[4,32,1152]{2,1,0:T(8,128)S(1)}, bf16[4,32,1152]{2,1,0:T(8,128)(2,1)S(1)}, f32[192,256]{1,0:T(8,128)S(...) custom-call(f32[48,1,128]{2,1,0:T(1,128)S(1)} %get-tuple-element.32., ...), custom_call_target="tpu_custom_call", output_to_operand_aliasing={{0}: (7, {})} | custom-call | tf_op jit(solution)/shard_map/pallas_call | solution.py:549
  25.3 2.2 %collective-permute-start.15 = (bf16[192,256]{1,0:T(8,128)(2,1)S(1)}, bf16[192,256]{1,0:T(8,128)(2,1)S(1)}, u32[]{:S(2)}, u32[]{:S(2)}) collective-permute-start(bf16[192,256]{1,0:T(8,128)(2,1)S(1)} %get-tuple-element.52), channel_id=1, source_target_pairs={{0,2},{1,3},{2,0},{3,1},{4,6},{5,7},{6,4},{7,5},{8,10},{9,11},{10,... | collective-permute-start | bytes 294920 | tf_op jit(solution)/shard_map/ppermute | solution.py:463
  27.4 1.4 %collective-permute-start.16 = (bf16[192,256]{1,0:T(8,128)(2,1)S(1)}, bf16[192,256]{1,0:T(8,128)(2,1)S(1)}, u32[]{:S(2)}, u32[]{:S(2)}) collective-permute-start(bf16[192,256]{1,0:T(8,128)(2,1)S(1)} %get-tuple-element.53), channel_id=1, source_target_pairs={{0,3},{1,0},{2,1},{3,2},{4,7},{5,4},{6,5},{7,6},{8,11},{9,8},{10,9... | collective-permute-start | bytes 294920 | tf_op jit(solution)/shard_map/ppermute | solution.py:463
  28.8 2.9 %all-to-all-start.1 = ((bf16[32,2,640]{2,1,0:T(2,128)(2,1)}), bf16[32,2,640]{2,1,0:T(2,128)(2,1)S(1)}, u32[]{:S(2)}, u32[]{:S(2)}) async-start(bf16[32,2,640]{2,1,0:T(2,128)(2,1)} %get-tuple-element.42), calls=%async_computation.1 | async-start | bytes 163840 | tf_op jit(solution)/shard_map/all_to_all | solution.py:570
  31.9 1.8 %collective-permute-start.11 = (bf16[32,864]{1,0:T(8,128)(2,1)S(1)}, bf16[32,864]{1,0:T(8,128)(2,1)S(1)}, u32[]{:S(2)}, u32[]{:S(2)}) collective-permute-start(bf16[32,864]{1,0:T(8,128)(2,1)S(1)} %get-tuple-element.47), channel_id=1, source_target_pairs={{0,16},{4,20},{8,24},{12,28},{16,0},{20,4},{24,8},{28,12},{1,17},{... | collective-permute-start | bytes 165896 | tf_op jit(solution)/shard_map/ppermute | solution.py:472
  33.7 1.5 %collective-permute-start.12 = (bf16[32,864]{1,0:T(8,128)(2,1)S(1)}, bf16[32,864]{1,0:T(8,128)(2,1)S(1)}, u32[]{:S(2)}, u32[]{:S(2)}) collective-permute-start(bf16[32,864]{1,0:T(8,128)(2,1)S(1)} %get-tuple-element.48), channel_id=1, source_target_pairs={{0,24},{4,28},{8,16},{12,20},{16,8},{20,12},{24,0},{28,4},{1,25},{... | collective-permute-start | bytes 165896 | tf_op jit(solution)/shard_map/ppermute | solution.py:472
  35.4 0.6 %collective-permute-done.15.refs_2_ = bf16[192,256]{1,0:T(8,128)(2,1)S(1)} collective-permute-done((bf16[192,256]{1,0:T(8,128)(2,1)S(1)}, bf16[192,256]{1,0:T(8,128)(2,1)S(1)}, u32[]{:S(2)}, u32[]{:S(2)}) %collective-permute-start.15) | collective-permute-done | bytes 98336 | tf_op jit(solution)/shard_map/ppermute | solution.py:463
  36.0 0.7 %shard_map.117 = bf16[192,256]{1,0:T(8,128)(2,1)} custom-call(f32[192,256]{1,0:T(8,128)S(1)} %get-tuple-element.50.refs_0_, bf16[192,256]{1,0:T(8,128)(2,1)S(1)} %collective-permute-done.14.refs_1_, bf16[192,256]{1,0:T(8,128)(2,1)S(1)} %collective-permute-done.15.refs_2_, bf16[192,256]{1,0:T(8,128)(2,1)S(1)} %collective-permute-done.16.refs_3_), custom_call_target="tpu_custom_call" | custom-call | flops 10000000000 | tf_op jit(solution)/shard_map/pallas_call | solution.py:581
  36.7 0.9 %shard_map.115.table_ref = bf16[896,896]{1,0:T(8,128)(2,1)S(1)} custom-call(bf16[32,864]{1,0:T(8,128)(2,1)S(1)} %get-tuple-element.45.after_ref), custom_call_target="tpu_custom_call" | custom-call | tf_op jit(solution)/shard_map/pallas_call | solution.py:576
  37.6 2.0 %all-to-all-done.1.act_in = bf16[32,2,640]{2,1,0:T(2,128)(2,1)S(1)} async-done(((bf16[32,2,640]{2,1,0:T(2,128)(2,1)}), bf16[32,2,640]{2,1,0:T(2,128)(2,1)S(1)}, u32[]{:S(2)}, u32[]{:S(2)}) %all-to-all-start.1) | async-done | bytes 81952 | tf_op jit(solution)/shard_map/all_to_all | solution.py:570
  39.7 1.1 %shard_map.116 = (f32[32,864]{1,0:T(8,128)}, bf16[4,32,128]{2,1,0:T(8,128)(2,1)}, f32[1,128]{1,0:T(1,128)}, f32[1,128]{1,0:T(1,128)}) custom-call(f32[32,1,128]{2,1,0:T(1,128)S(1)} %get-tuple-element.31.holds_ref, bf16[32,2,640]{2,1,0:T(2,128)(2,1)S(1)} %all-to-all-done.1.act_in, bf16[896,896]{1,0:T(8,128)(2,1)S(1)} %shard_map.115.table_ref, ...), custom_call_target="tpu_custom_call" | custom-call | tf_op jit(solution)/shard_map/pallas_call | solution.py:593
  (28 shorter events, 1.2 us)
Async XLA Ops:
  0.6 10.0 %collective-permute-start = (bf16[32,864]{1,0:T(8,128)(2,1)}, bf16[32,864]{1,0:T(8,128)(2,1)S(1)}, u32[]{:S(2)}, u32[]{:S(2)}) collective-permute-start(bf16[32,864]{1,0:T(8,128)(2,1)} %refs_0_.1), channel_id=1, source_target_pairs={{0,8},{4,12},{8,0},{12,4},{16,24},{20,28},{24,16},{28,20},{1,9},{5... | collective-permute-start | bytes 165896 | tf_op jit(solution)/shard_map/ppermute | solution.py:518
  3.6 12.0 %collective-permute-start.9 = (bf16[192,256]{1,0:T(8,128)(2,1)}, bf16[192,256]{1,0:T(8,128)(2,1)S(1)}, u32[]{:S(2)}, u32[]{:S(2)}) collective-permute-start(bf16[192,256]{1,0:T(8,128)(2,1)} %bitcast.16), channel_id=1, source_target_pairs={{0,1},{1,2},{2,3},{3,0},{4,5},{5,6},{6,7},{7,4},{8,9},{9,10},{10,1... | collective-permute-start | bytes 294920 | tf_op jit(solution)/shard_map/ppermute | solution.py:463
  5.2 10.8 %collective-permute-start.8 = (bf16[192,256]{1,0:T(8,128)(2,1)}, bf16[192,256]{1,0:T(8,128)(2,1)S(1)}, u32[]{:S(2)}, u32[]{:S(2)}) collective-permute-start(bf16[192,256]{1,0:T(8,128)(2,1)} %bitcast.17), channel_id=1, source_target_pairs={{0,2},{1,3},{2,0},{3,1},{4,6},{5,7},{6,4},{7,5},{8,10},{9,11},{10,... | collective-permute-start | bytes 294920 | tf_op jit(solution)/shard_map/ppermute | solution.py:463
  7.8 8.7 %collective-permute-start.7 = (bf16[192,256]{1,0:T(8,128)(2,1)}, bf16[192,256]{1,0:T(8,128)(2,1)S(1)}, u32[]{:S(2)}, u32[]{:S(2)}) collective-permute-start(bf16[192,256]{1,0:T(8,128)(2,1)} %bitcast.18), channel_id=1, source_target_pairs={{0,3},{1,0},{2,1},{3,2},{4,7},{5,4},{6,5},{7,6},{8,11},{9,8},{10,9... | collective-permute-start | bytes 294920 | tf_op jit(solution)/shard_map/ppermute | solution.py:463
  9.2 6.3 %collective-permute-start.1 = (bf16[32,864]{1,0:T(8,128)(2,1)}, bf16[32,864]{1,0:T(8,128)(2,1)S(1)}, u32[]{:S(2)}, u32[]{:S(2)}) collective-permute-start(bf16[32,864]{1,0:T(8,128)(2,1)} %refs_0_.1), channel_id=1, source_target_pairs={{0,16},{4,20},{8,24},{12,28},{16,0},{20,4},{24,8},{28,12},{1,17},{... | collective-permute-start | bytes 165896 | tf_op jit(solution)/shard_map/ppermute | solution.py:518
  10.7 5.5 %collective-permute-start.2 = (bf16[32,864]{1,0:T(8,128)(2,1)S(1)}, bf16[32,864]{1,0:T(8,128)(2,1)S(1)}, u32[]{:S(2)}, u32[]{:S(2)}) collective-permute-start(bf16[32,864]{1,0:T(8,128)(2,1)S(1)} %collective-permute-done.refs_1_), channel_id=1, source_target_pairs={{0,16},{4,20},{8,24},{12,28},{16,0},{20,4},{24,8},{28,12},{1,17},{... | collective-permute-start | bytes 165896 | tf_op jit(solution)/shard_map/ppermute | solution.py:518
  12.8 10.1 %all-to-all-start = ((bf16[32,8,128]{2,1,0:T(8,128)(2,1)}), bf16[32,8,128]{2,1,0:T(8,128)(2,1)S(1)}, u32[]{:S(2)}, u32[]{:S(2)}) async-start(bf16[32,8,128]{2,1,0:T(8,128)(2,1)} %get-tuple-element.41), calls=%async_computation | async-start | bytes 131072 | tf_op jit(solution)/shard_map/all_to_all | solution.py:514
  15.4 2.1 %copy-start = (bf16[32,864]{1,0:T(8,128)(2,1)S(1)}, bf16[32,864]{1,0:T(8,128)(2,1)}, u32[]{:S(2)}) copy-start(bf16[32,864]{1,0:T(8,128)(2,1)} %refs_0_.1) | copy-start | bytes 165892
  15.4 2.1 %copy-start.1 = (f32[128]{0:T(128)S(1)}, f32[128]{0:T(128)}, u32[]{:S(2)}) copy-start(f32[128]{0:T(128)} %param.11) | copy-start | bytes 1540
  15.4 2.1 %copy-start.2 = (f32[128]{0:T(128)S(1)}, f32[128]{0:T(128)}, u32[]{:S(2)}) copy-start(f32[128]{0:T(128)} %param.12) | copy-start | bytes 1540
  15.4 2.0 %collective-permute-start.3 = (bf16[32,864]{1,0:T(8,128)(2,1)}, bf16[32,864]{1,0:T(8,128)(2,1)S(1)}, u32[]{:S(2)}, u32[]{:S(2)}) collective-permute-start(bf16[32,864]{1,0:T(8,128)(2,1)} %refs_0_.1), channel_id=1, source_target_pairs={{0,4},{4,0},{8,12},{12,8},{16,20},{20,16},{24,28},{28,24},{1,5},{5... | collective-permute-start | bytes 165896 | tf_op jit(solution)/shard_map/ppermute | solution.py:477
  15.6 1.9 %collective-permute-start.4 = (bf16[32,864]{1,0:T(8,128)(2,1)S(1)}, bf16[32,864]{1,0:T(8,128)(2,1)S(1)}, u32[]{:S(2)}, u32[]{:S(2)}) collective-permute-start(bf16[32,864]{1,0:T(8,128)(2,1)S(1)} %collective-permute-done.refs_1_), channel_id=1, source_target_pairs={{0,4},{4,0},{8,12},{12,8},{16,20},{20,16},{24,28},{28,24},{1,5},{5... | collective-permute-start | bytes 165896 | tf_op jit(solution)/shard_map/ppermute | solution.py:477
  16.0 1.4 %collective-permute-start.5 = (bf16[32,864]{1,0:T(8,128)(2,1)S(1)}, bf16[32,864]{1,0:T(8,128)(2,1)S(1)}, u32[]{:S(2)}, u32[]{:S(2)}) collective-permute-start(bf16[32,864]{1,0:T(8,128)(2,1)S(1)} %collective-permute-done.1.refs_2_), channel_id=1, source_target_pairs={{0,4},{4,0},{8,12},{12,8},{16,20},{20,16},{24,28},{28,24},{1,5},{5... | collective-permute-start | bytes 165896 | tf_op jit(solution)/shard_map/ppermute | solution.py:477
  16.1 1.4 %collective-permute-start.6 = (bf16[32,864]{1,0:T(8,128)(2,1)S(1)}, bf16[32,864]{1,0:T(8,128)(2,1)S(1)}, u32[]{:S(2)}, u32[]{:S(2)}) collective-permute-start(bf16[32,864]{1,0:T(8,128)(2,1)S(1)} %collective-permute-done.2.refs_3_), channel_id=1, source_target_pairs={{0,4},{4,0},{8,12},{12,8},{16,20},{20,16},{24,28},{28,24},{1,5},{5... | collective-permute-start | bytes 165896 | tf_op jit(solution)/shard_map/ppermute | solution.py:477
  24.8 6.9 %collective-permute-start.10 = (bf16[4,32,1152]{2,1,0:T(8,128)(2,1)S(1)}, bf16[4,32,1152]{2,1,0:T(8,128)(2,1)S(1)}, u32[]{:S(2)}, u32[]{:S(2)}) collective-permute-start(bf16[4,32,1152]{2,1,0:T(8,128)(2,1)S(1)} %get-tuple-element.44), channel_id=1, source_target_pairs={{0,4},{4,0},{8,12},{12,8},{16,20},{20,16},{24,28},{28,24},{1,5},{5... | collective-permute-start | bytes 884744 | tf_op jit(solution)/shard_map/ppermute | solution.py:477
  24.9 10.3 %collective-permute-start.14 = (bf16[192,256]{1,0:T(8,128)(2,1)S(1)}, bf16[192,256]{1,0:T(8,128)(2,1)S(1)}, u32[]{:S(2)}, u32[]{:S(2)}) collective-permute-start(bf16[192,256]{1,0:T(8,128)(2,1)S(1)} %get-tuple-element.51), channel_id=1, source_target_pairs={{0,1},{1,2},{2,3},{3,0},{4,5},{5,6},{6,7},{7,4},{8,9},{9,10},{10,1... | collective-permute-start | bytes 294920 | tf_op jit(solution)/shard_map/ppermute | solution.py:463
  25.3 10.8 %collective-permute-start.15 = (bf16[192,256]{1,0:T(8,128)(2,1)S(1)}, bf16[192,256]{1,0:T(8,128)(2,1)S(1)}, u32[]{:S(2)}, u32[]{:S(2)}) collective-permute-start(bf16[192,256]{1,0:T(8,128)(2,1)S(1)} %get-tuple-element.52), channel_id=1, source_target_pairs={{0,2},{1,3},{2,0},{3,1},{4,6},{5,7},{6,4},{7,5},{8,10},{9,11},{10,... | collective-permute-start | bytes 294920 | tf_op jit(solution)/shard_map/ppermute | solution.py:463
  27.4 8.6 %collective-permute-start.16 = (bf16[192,256]{1,0:T(8,128)(2,1)S(1)}, bf16[192,256]{1,0:T(8,128)(2,1)S(1)}, u32[]{:S(2)}, u32[]{:S(2)}) collective-permute-start(bf16[192,256]{1,0:T(8,128)(2,1)S(1)} %get-tuple-element.53), channel_id=1, source_target_pairs={{0,3},{1,0},{2,1},{3,2},{4,7},{5,4},{6,5},{7,6},{8,11},{9,8},{10,9... | collective-permute-start | bytes 294920 | tf_op jit(solution)/shard_map/ppermute | solution.py:463
  28.8 10.8 %all-to-all-start.1 = ((bf16[32,2,640]{2,1,0:T(2,128)(2,1)}), bf16[32,2,640]{2,1,0:T(2,128)(2,1)S(1)}, u32[]{:S(2)}, u32[]{:S(2)}) async-start(bf16[32,2,640]{2,1,0:T(2,128)(2,1)} %get-tuple-element.42), calls=%async_computation.1 | async-start | bytes 163840 | tf_op jit(solution)/shard_map/all_to_all | solution.py:570
  31.9 7.8 %collective-permute-start.11 = (bf16[32,864]{1,0:T(8,128)(2,1)S(1)}, bf16[32,864]{1,0:T(8,128)(2,1)S(1)}, u32[]{:S(2)}, u32[]{:S(2)}) collective-permute-start(bf16[32,864]{1,0:T(8,128)(2,1)S(1)} %get-tuple-element.47), channel_id=1, source_target_pairs={{0,16},{4,20},{8,24},{12,28},{16,0},{20,4},{24,8},{28,12},{1,17},{... | collective-permute-start | bytes 165896 | tf_op jit(solution)/shard_map/ppermute | solution.py:472
  33.7 6.0 %collective-permute-start.12 = (bf16[32,864]{1,0:T(8,128)(2,1)S(1)}, bf16[32,864]{1,0:T(8,128)(2,1)S(1)}, u32[]{:S(2)}, u32[]{:S(2)}) collective-permute-start(bf16[32,864]{1,0:T(8,128)(2,1)S(1)} %get-tuple-element.48), channel_id=1, source_target_pairs={{0,24},{4,28},{8,16},{12,20},{16,8},{20,12},{24,0},{28,4},{1,25},{... | collective-permute-start | bytes 165896 | tf_op jit(solution)/shard_map/ppermute | solution.py:472
  35.2 4.5 %collective-permute-start.13 = (bf16[32,864]{1,0:T(8,128)(2,1)S(1)}, bf16[32,864]{1,0:T(8,128)(2,1)S(1)}, u32[]{:S(2)}, u32[]{:S(2)}) collective-permute-start(bf16[32,864]{1,0:T(8,128)(2,1)S(1)} %get-tuple-element.45.after_ref), channel_id=1, source_target_pairs={{0,8},{4,12},{8,0},{12,4},{16,24},{20,28},{24,16},{28,20},{1,9},{5... | collective-permute-start | bytes 165896 | tf_op jit(solution)/shard_map/ppermute | solution.py:472

commit v8 on v5

--- a/solution.py
+++ b/solution.py
@@ -92,8 +92,8 @@
     pairs = [(blocks_hbm, blocks_ref), (order_hbm, order_ref), (cot_hbm, cot_ref)]
     copies = fetch(pairs, sems)
     out_ref[...] = jnp.zeros_like(out_ref)
-    for copy in copies:
-        copy.wait()
+    copies[0].wait()
+    copies[1].wait()
     me = lax.axis_index("clips")
     start = first_block_of(blocks_ref, me * held, clips)
     for k in range(held):
@@ -105,6 +105,7 @@
                 slots_ref[(k * BMAX + b) * devs + d] = jnp.full((1, LANES), hit, F32)
         start = start + count
     holders = slot_holders(blocks_ref, order_ref, me, slots, clips, held, devs)
+    copies[2].wait()
     for q in range(slots):
         block = cot_ref[q].astype(F32)
         for s in range(slab):

time: 41.1 us -> 41.1 us (level)
  no operation moved by 1% of the time
where the time goes in v8:
time: 41.1 us; the launch traced here: 40.8 us
  starting transfers between devices  24.6 us (60%)
  Pallas kernels  10.7 us (26%)
  waiting for transfers between devices  4.58 us (11%)
  between operations  0.81 us (2%)
    ppermute x6, starting transfers between devices, shifts(): lax.ppermute(arrays[i], axis, [(j, (j + i) % size) for j in range(size)])  9.44 us
    ppermute x3, starting transfers between devices, body(): shards = shards + [lax.ppermute(shard, 'clips', pairs) for shard in shards]  5.03 us
    ppermute x3, starting transfers between devices, chip_swaps(): moved.append(lax.ppermute(arrays[t], axis, pairs))  3.55 us
    pallas_call x1, Pallas kernels, body(): call(functools.partial(forward_kernel, dims), [shape((9 * LANES, c_in), B...  3.44 us
    all_to_all x1, starting transfers between devices, body(): lax.all_to_all(acts, everyone, split_axis=0, concat_axis=0, tiled=True)  2.85 us
    all_to_all x1, starting transfers between devices, body(): lax.all_to_all(cots, everyone, split_axis=0, concat_axis=0, tiled=True)  2.59 us
    all_to_all x1, waiting for transfers between devices, body(): lax.all_to_all(acts, everyone, split_axis=0, concat_axis=0, tiled=True)  2.05 us
    all_to_all x1, waiting for transfers between devices, body(): lax.all_to_all(cots, everyone, split_axis=0, concat_axis=0, tiled=True)  1.91 us
  transfers between devices with their start and end apart: 19, of which 3 were waited for; matrix products, arithmetic and copies ran while one was open for 0% of the time, Pallas kernels for 19%

profile of v8, /device:TPU:0, one launch (start us, length us, event | category | flops | bytes accessed | tf_op | source)
XLA Modules:
  0.0 40.8 jit_solution(477695019462354867)
XLA Ops:
  0.6 3.0 %collective-permute-start = (bf16[32,864]{1,0:T(8,128)(2,1)}, bf16[32,864]{1,0:T(8,128)(2,1)S(1)}, u32[]{:S(2)}, u32[]{:S(2)}) collective-permute-start(bf16[32,864]{1,0:T(8,128)(2,1)} %refs_0_.1), channel_id=1, source_target_pairs={{0,8},{4,12},{8,0},{12,4},{16,24},{20,28},{24,16},{28,20},{1,9},{5... | collective-permute-start | bytes 165896 | tf_op jit(solution)/shard_map/ppermute | solution.py:519
  3.6 1.6 %collective-permute-start.9 = (bf16[192,256]{1,0:T(8,128)(2,1)}, bf16[192,256]{1,0:T(8,128)(2,1)S(1)}, u32[]{:S(2)}, u32[]{:S(2)}) collective-permute-start(bf16[192,256]{1,0:T(8,128)(2,1)} %bitcast.16), channel_id=1, source_target_pairs={{0,1},{1,2},{2,3},{3,0},{4,5},{5,6},{6,7},{7,4},{8,9},{9,10},{10,1... | collective-permute-start | bytes 294920 | tf_op jit(solution)/shard_map/ppermute | solution.py:464
  5.2 2.6 %collective-permute-start.8 = (bf16[192,256]{1,0:T(8,128)(2,1)}, bf16[192,256]{1,0:T(8,128)(2,1)S(1)}, u32[]{:S(2)}, u32[]{:S(2)}) collective-permute-start(bf16[192,256]{1,0:T(8,128)(2,1)} %bitcast.17), channel_id=1, source_target_pairs={{0,2},{1,3},{2,0},{3,1},{4,6},{5,7},{6,4},{7,5},{8,10},{9,11},{10,... | collective-permute-start | bytes 294920 | tf_op jit(solution)/shard_map/ppermute | solution.py:464
  7.8 1.3 %collective-permute-start.7 = (bf16[192,256]{1,0:T(8,128)(2,1)}, bf16[192,256]{1,0:T(8,128)(2,1)S(1)}, u32[]{:S(2)}, u32[]{:S(2)}) collective-permute-start(bf16[192,256]{1,0:T(8,128)(2,1)} %bitcast.18), channel_id=1, source_target_pairs={{0,3},{1,0},{2,1},{3,2},{4,7},{5,4},{6,5},{7,6},{8,11},{9,8},{10,9... | collective-permute-start | bytes 294920 | tf_op jit(solution)/shard_map/ppermute | solution.py:464
  9.2 1.5 %collective-permute-start.1 = (bf16[32,864]{1,0:T(8,128)(2,1)}, bf16[32,864]{1,0:T(8,128)(2,1)S(1)}, u32[]{:S(2)}, u32[]{:S(2)}) collective-permute-start(bf16[32,864]{1,0:T(8,128)(2,1)} %refs_0_.1), channel_id=1, source_target_pairs={{0,16},{4,20},{8,24},{12,28},{16,0},{20,4},{24,8},{28,12},{1,17},{... | collective-permute-start | bytes 165896 | tf_op jit(solution)/shard_map/ppermute | solution.py:519
  10.7 0.5 %collective-permute-start.2 = (bf16[32,864]{1,0:T(8,128)(2,1)S(1)}, bf16[32,864]{1,0:T(8,128)(2,1)S(1)}, u32[]{:S(2)}, u32[]{:S(2)}) collective-permute-start(bf16[32,864]{1,0:T(8,128)(2,1)S(1)} %collective-permute-done.refs_1_), channel_id=1, source_target_pairs={{0,16},{4,20},{8,24},{12,28},{16,0},{20,4},{24,8},{28,12},{1,17},{... | collective-permute-start | bytes 165896 | tf_op jit(solution)/shard_map/ppermute | solution.py:519
  11.2 1.6 %shard_map.110 = (bf16[32,8,128]{2,1,0:T(8,128)(2,1)}, f32[32,1,128]{2,1,0:T(1,128)S(1)}, f32[48,1,128]{2,1,0:T(1,128)S(1)}) custom-call(s32[16]{0:T(128)} %blocks_hbm.3, s32[8]{0:T(128)} %order_hbm.1, bf16[4,32,128]{2,1,0:T(8,128)(2,1)} %bitcast.15), custom_call_target="tpu_custom_call" | custom-call | flops 1000000 | tf_op jit(solution)/shard_map/pallas_call | solution.py:507
  12.8 2.6 %all-to-all-start = ((bf16[32,8,128]{2,1,0:T(8,128)(2,1)}), bf16[32,8,128]{2,1,0:T(8,128)(2,1)S(1)}, u32[]{:S(2)}, u32[]{:S(2)}) async-start(bf16[32,8,128]{2,1,0:T(8,128)(2,1)} %get-tuple-element.41), calls=%async_computation | async-start | bytes 131072 | tf_op jit(solution)/shard_map/all_to_all | solution.py:515
  15.6 0.4 collective-permute-start.4
  16.2 0.4 collective-permute-start.6
  16.6 0.9 %shard_map.111 = (bf16[6,192,256]{2,1,0:T(8,128)(2,1)S(1)}, bf16[896,1152]{1,0:T(8,128)(2,1)S(1)}) custom-call(bf16[192,256]{1,0:T(8,128)(2,1)} %bitcast.19, bf16[192,256]{1,0:T(8,128)(2,1)S(1)} %collective-permute-done.7.refs_1_, bf16[192,256]{1,0:T(8,128)(2,1)S(1)} %collective-permute-done.8.refs_2_, bf16[192,256]{1,0:T(8,128)(2,1)S(1)} %collective-permute-done.9.refs_3_), custom_call_target="tpu_custom_call" | custom-call | flops 10000000000 | tf_op jit(solution)/shard_map/pallas_call | solution.py:523
  17.6 3.4 %shard_map.112 = (bf16[1152,256]{1,0:T(8,128)(2,1)S(1)}, bf16[256,768]{1,0:T(8,128)(2,1)S(1)}, f32[4,192,32]{2,1,0:T(8,128)S(1)}, f32[2,8,32]{2,1,0:T(8,128)S(1)...) custom-call(s32[16]{0:T(128)} %blocks_hbm.3, f32[48,1,128]{2,1,0:T(1,128)S(1)} %get-tuple-element.32.slots_ref, ...), custom_call_target="tpu_custom_call" | custom-call | tf_op jit(solution)/shard_map/pallas_call | solution.py:530
  21.0 1.9 %all-to-all-done.refs_5_ = bf16[32,8,128]{2,1,0:T(8,128)(2,1)S(1)} async-done(((bf16[32,8,128]{2,1,0:T(8,128)(2,1)}), bf16[32,8,128]{2,1,0:T(8,128)(2,1)S(1)}, u32[]{:S(2)}, u32[]{:S(2)}) %all-to-all-start) | async-done | bytes 65568 | tf_op jit(solution)/shard_map/all_to_all | solution.py:515
  22.9 1.9 %shard_map.113 = (bf16[32,2,640]{2,1,0:T(2,128)(2,1)}, f32[4,32,1152]{2,1,0:T(8,128)S(1)}, bf16[4,32,1152]{2,1,0:T(8,128)(2,1)S(1)}, f32[192,256]{1,0:T(8,128)S(...) custom-call(f32[48,1,128]{2,1,0:T(1,128)S(1)} %get-tuple-element.32., ...), custom_call_target="tpu_custom_call", output_to_operand_aliasing={{0}: (7, {})} | custom-call | tf_op jit(solution)/shard_map/pallas_call | solution.py:550
  25.2 2.2 %collective-permute-start.15 = (bf16[192,256]{1,0:T(8,128)(2,1)S(1)}, bf16[192,256]{1,0:T(8,128)(2,1)S(1)}, u32[]{:S(2)}, u32[]{:S(2)}) collective-permute-start(bf16[192,256]{1,0:T(8,128)(2,1)S(1)} %get-tuple-element.52), channel_id=1, source_target_pairs={{0,2},{1,3},{2,0},{3,1},{4,6},{5,7},{6,4},{7,5},{8,10},{9,11},{10,... | collective-permute-start | bytes 294920 | tf_op jit(solution)/shard_map/ppermute | solution.py:464
  27.4 1.4 %collective-permute-start.16 = (bf16[192,256]{1,0:T(8,128)(2,1)S(1)}, bf16[192,256]{1,0:T(8,128)(2,1)S(1)}, u32[]{:S(2)}, u32[]{:S(2)}) collective-permute-start(bf16[192,256]{1,0:T(8,128)(2,1)S(1)} %get-tuple-element.53), channel_id=1, source_target_pairs={{0,3},{1,0},{2,1},{3,2},{4,7},{5,4},{6,5},{7,6},{8,11},{9,8},{10,9... | collective-permute-start | bytes 294920 | tf_op jit(solution)/shard_map/ppermute | solution.py:464
  28.8 2.9 %all-to-all-start.1 = ((bf16[32,2,640]{2,1,0:T(2,128)(2,1)}), bf16[32,2,640]{2,1,0:T(2,128)(2,1)S(1)}, u32[]{:S(2)}, u32[]{:S(2)}) async-start(bf16[32,2,640]{2,1,0:T(2,128)(2,1)} %get-tuple-element.42), calls=%async_computation.1 | async-start | bytes 163840 | tf_op jit(solution)/shard_map/all_to_all | solution.py:571
  31.9 2.7 %collective-permute-start.11 = (bf16[32,864]{1,0:T(8,128)(2,1)S(1)}, bf16[32,864]{1,0:T(8,128)(2,1)S(1)}, u32[]{:S(2)}, u32[]{:S(2)}) collective-permute-start(bf16[32,864]{1,0:T(8,128)(2,1)S(1)} %get-tuple-element.47), channel_id=1, source_target_pairs={{0,24},{4,28},{8,16},{12,20},{16,8},{20,12},{24,0},{28,4},{1,25},{... | collective-permute-start | bytes 165896 | tf_op jit(solution)/shard_map/ppermute | solution.py:473
  34.6 0.6 %collective-permute-start.12 = (bf16[32,864]{1,0:T(8,128)(2,1)S(1)}, bf16[32,864]{1,0:T(8,128)(2,1)S(1)}, u32[]{:S(2)}, u32[]{:S(2)}) collective-permute-start(bf16[32,864]{1,0:T(8,128)(2,1)S(1)} %get-tuple-element.48), channel_id=1, source_target_pairs={{0,16},{4,20},{8,24},{12,28},{16,0},{20,4},{24,8},{28,12},{1,17},{... | collective-permute-start | bytes 165896 | tf_op jit(solution)/shard_map/ppermute | solution.py:473
  35.4 0.6 %collective-permute-done.15.refs_2_ = bf16[192,256]{1,0:T(8,128)(2,1)S(1)} collective-permute-done((bf16[192,256]{1,0:T(8,128)(2,1)S(1)}, bf16[192,256]{1,0:T(8,128)(2,1)S(1)}, u32[]{:S(2)}, u32[]{:S(2)}) %collective-permute-start.15) | collective-permute-done | bytes 98336 | tf_op jit(solution)/shard_map/ppermute | solution.py:464
  36.0 0.7 %shard_map.117 = bf16[192,256]{1,0:T(8,128)(2,1)} custom-call(f32[192,256]{1,0:T(8,128)S(1)} %get-tuple-element.50.refs_0_, bf16[192,256]{1,0:T(8,128)(2,1)S(1)} %collective-permute-done.14.refs_1_, bf16[192,256]{1,0:T(8,128)(2,1)S(1)} %collective-permute-done.15.refs_2_, bf16[192,256]{1,0:T(8,128)(2,1)S(1)} %collective-permute-done.16.refs_3_), custom_call_target="tpu_custom_call" | custom-call | flops 10000000000 | tf_op jit(solution)/shard_map/pallas_call | solution.py:582
  36.7 0.9 %shard_map.115.table_ref = bf16[896,896]{1,0:T(8,128)(2,1)S(1)} custom-call(bf16[32,864]{1,0:T(8,128)(2,1)S(1)} %get-tuple-element.45.after_ref), custom_call_target="tpu_custom_call" | custom-call | tf_op jit(solution)/shard_map/pallas_call | solution.py:577
  37.6 2.1 %all-to-all-done.1.act_in = bf16[32,2,640]{2,1,0:T(2,128)(2,1)S(1)} async-done(((bf16[32,2,640]{2,1,0:T(2,128)(2,1)}), bf16[32,2,640]{2,1,0:T(2,128)(2,1)S(1)}, u32[]{:S(2)}, u32[]{:S(2)}) %all-to-all-start.1) | async-done | bytes 81952 | tf_op jit(solution)/shard_map/all_to_all | solution.py:571
  39.6 1.1 %shard_map.116 = (f32[32,864]{1,0:T(8,128)}, bf16[4,32,128]{2,1,0:T(8,128)(2,1)}, f32[1,128]{1,0:T(1,128)}, f32[1,128]{1,0:T(1,128)}) custom-call(f32[32,1,128]{2,1,0:T(1,128)S(1)} %get-tuple-element.31.holds_ref, bf16[32,2,640]{2,1,0:T(2,128)(2,1)S(1)} %all-to-all-done.1.act_in, bf16[896,896]{1,0:T(8,128)(2,1)S(1)} %shard_map.115.table_ref, ...), custom_call_target="tpu_custom_call" | custom-call | tf_op jit(solution)/shard_map/pallas_call | solution.py:594
  (28 shorter events, 1.2 us)
Async XLA Ops:
  0.6 10.0 %collective-permute-start = (bf16[32,864]{1,0:T(8,128)(2,1)}, bf16[32,864]{1,0:T(8,128)(2,1)S(1)}, u32[]{:S(2)}, u32[]{:S(2)}) collective-permute-start(bf16[32,864]{1,0:T(8,128)(2,1)} %refs_0_.1), channel_id=1, source_target_pairs={{0,8},{4,12},{8,0},{12,4},{16,24},{20,28},{24,16},{28,20},{1,9},{5... | collective-permute-start | bytes 165896 | tf_op jit(solution)/shard_map/ppermute | solution.py:519
  3.6 12.0 %collective-permute-start.9 = (bf16[192,256]{1,0:T(8,128)(2,1)}, bf16[192,256]{1,0:T(8,128)(2,1)S(1)}, u32[]{:S(2)}, u32[]{:S(2)}) collective-permute-start(bf16[192,256]{1,0:T(8,128)(2,1)} %bitcast.16), channel_id=1, source_target_pairs={{0,1},{1,2},{2,3},{3,0},{4,5},{5,6},{6,7},{7,4},{8,9},{9,10},{10,1... | collective-permute-start | bytes 294920 | tf_op jit(solution)/shard_map/ppermute | solution.py:464
  5.2 10.8 %collective-permute-start.8 = (bf16[192,256]{1,0:T(8,128)(2,1)}, bf16[192,256]{1,0:T(8,128)(2,1)S(1)}, u32[]{:S(2)}, u32[]{:S(2)}) collective-permute-start(bf16[192,256]{1,0:T(8,128)(2,1)} %bitcast.17), channel_id=1, source_target_pairs={{0,2},{1,3},{2,0},{3,1},{4,6},{5,7},{6,4},{7,5},{8,10},{9,11},{10,... | collective-permute-start | bytes 294920 | tf_op jit(solution)/shard_map/ppermute | solution.py:464
  7.8 8.8 %collective-permute-start.7 = (bf16[192,256]{1,0:T(8,128)(2,1)}, bf16[192,256]{1,0:T(8,128)(2,1)S(1)}, u32[]{:S(2)}, u32[]{:S(2)}) collective-permute-start(bf16[192,256]{1,0:T(8,128)(2,1)} %bitcast.18), channel_id=1, source_target_pairs={{0,3},{1,0},{2,1},{3,2},{4,7},{5,4},{6,5},{7,6},{8,11},{9,8},{10,9... | collective-permute-start | bytes 294920 | tf_op jit(solution)/shard_map/ppermute | solution.py:464
  9.2 6.3 %collective-permute-start.1 = (bf16[32,864]{1,0:T(8,128)(2,1)}, bf16[32,864]{1,0:T(8,128)(2,1)S(1)}, u32[]{:S(2)}, u32[]{:S(2)}) collective-permute-start(bf16[32,864]{1,0:T(8,128)(2,1)} %refs_0_.1), channel_id=1, source_target_pairs={{0,16},{4,20},{8,24},{12,28},{16,0},{20,4},{24,8},{28,12},{1,17},{... | collective-permute-start | bytes 165896 | tf_op jit(solution)/shard_map/ppermute | solution.py:519
  10.7 5.5 %collective-permute-start.2 = (bf16[32,864]{1,0:T(8,128)(2,1)S(1)}, bf16[32,864]{1,0:T(8,128)(2,1)S(1)}, u32[]{:S(2)}, u32[]{:S(2)}) collective-permute-start(bf16[32,864]{1,0:T(8,128)(2,1)S(1)} %collective-permute-done.refs_1_), channel_id=1, source_target_pairs={{0,16},{4,20},{8,24},{12,28},{16,0},{20,4},{24,8},{28,12},{1,17},{... | collective-permute-start | bytes 165896 | tf_op jit(solution)/shard_map/ppermute | solution.py:519
  12.8 10.1 %all-to-all-start = ((bf16[32,8,128]{2,1,0:T(8,128)(2,1)}), bf16[32,8,128]{2,1,0:T(8,128)(2,1)S(1)}, u32[]{:S(2)}, u32[]{:S(2)}) async-start(bf16[32,8,128]{2,1,0:T(8,128)(2,1)} %get-tuple-element.41), calls=%async_computation | async-start | bytes 131072 | tf_op jit(solution)/shard_map/all_to_all | solution.py:515
  15.4 2.1 %copy-start = (bf16[32,864]{1,0:T(8,128)(2,1)S(1)}, bf16[32,864]{1,0:T(8,128)(2,1)}, u32[]{:S(2)}) copy-start(bf16[32,864]{1,0:T(8,128)(2,1)} %refs_0_.1) | copy-start | bytes 165892
  15.4 2.1 %copy-start.1 = (f32[128]{0:T(128)S(1)}, f32[128]{0:T(128)}, u32[]{:S(2)}) copy-start(f32[128]{0:T(128)} %param.11) | copy-start | bytes 1540
  15.4 2.1 %copy-start.2 = (f32[128]{0:T(128)S(1)}, f32[128]{0:T(128)}, u32[]{:S(2)}) copy-start(f32[128]{0:T(128)} %param.12) | copy-start | bytes 1540
  15.5 2.0 %collective-permute-start.3 = (bf16[32,864]{1,0:T(8,128)(2,1)}, bf16[32,864]{1,0:T(8,128)(2,1)S(1)}, u32[]{:S(2)}, u32[]{:S(2)}) collective-permute-start(bf16[32,864]{1,0:T(8,128)(2,1)} %refs_0_.1), channel_id=1, source_target_pairs={{0,4},{4,0},{8,12},{12,8},{16,20},{20,16},{24,28},{28,24},{1,5},{5... | collective-permute-start | bytes 165896 | tf_op jit(solution)/shard_map/ppermute | solution.py:478
  15.6 1.9 %collective-permute-start.4 = (bf16[32,864]{1,0:T(8,128)(2,1)S(1)}, bf16[32,864]{1,0:T(8,128)(2,1)S(1)}, u32[]{:S(2)}, u32[]{:S(2)}) collective-permute-start(bf16[32,864]{1,0:T(8,128)(2,1)S(1)} %collective-permute-done.refs_1_), channel_id=1, source_target_pairs={{0,4},{4,0},{8,12},{12,8},{16,20},{20,16},{24,28},{28,24},{1,5},{5... | collective-permute-start | bytes 165896 | tf_op jit(solution)/shard_map/ppermute | solution.py:478
  16.0 1.4 %collective-permute-start.5 = (bf16[32,864]{1,0:T(8,128)(2,1)S(1)}, bf16[32,864]{1,0:T(8,128)(2,1)S(1)}, u32[]{:S(2)}, u32[]{:S(2)}) collective-permute-start(bf16[32,864]{1,0:T(8,128)(2,1)S(1)} %collective-permute-done.1.refs_2_), channel_id=1, source_target_pairs={{0,4},{4,0},{8,12},{12,8},{16,20},{20,16},{24,28},{28,24},{1,5},{5... | collective-permute-start | bytes 165896 | tf_op jit(solution)/shard_map/ppermute | solution.py:478
  16.2 1.4 %collective-permute-start.6 = (bf16[32,864]{1,0:T(8,128)(2,1)S(1)}, bf16[32,864]{1,0:T(8,128)(2,1)S(1)}, u32[]{:S(2)}, u32[]{:S(2)}) collective-permute-start(bf16[32,864]{1,0:T(8,128)(2,1)S(1)} %collective-permute-done.2.refs_3_), channel_id=1, source_target_pairs={{0,4},{4,0},{8,12},{12,8},{16,20},{20,16},{24,28},{28,24},{1,5},{5... | collective-permute-start | bytes 165896 | tf_op jit(solution)/shard_map/ppermute | solution.py:478
  24.8 6.9 %collective-permute-start.10 = (bf16[4,32,1152]{2,1,0:T(8,128)(2,1)S(1)}, bf16[4,32,1152]{2,1,0:T(8,128)(2,1)S(1)}, u32[]{:S(2)}, u32[]{:S(2)}) collective-permute-start(bf16[4,32,1152]{2,1,0:T(8,128)(2,1)S(1)} %get-tuple-element.44), channel_id=1, source_target_pairs={{0,4},{4,0},{8,12},{12,8},{16,20},{20,16},{24,28},{28,24},{1,5},{5... | collective-permute-start | bytes 884744 | tf_op jit(solution)/shard_map/ppermute | solution.py:478
  24.9 10.3 %collective-permute-start.14 = (bf16[192,256]{1,0:T(8,128)(2,1)S(1)}, bf16[192,256]{1,0:T(8,128)(2,1)S(1)}, u32[]{:S(2)}, u32[]{:S(2)}) collective-permute-start(bf16[192,256]{1,0:T(8,128)(2,1)S(1)} %get-tuple-element.51), channel_id=1, source_target_pairs={{0,1},{1,2},{2,3},{3,0},{4,5},{5,6},{6,7},{7,4},{8,9},{9,10},{10,1... | collective-permute-start | bytes 294920 | tf_op jit(solution)/shard_map/ppermute | solution.py:464
  25.2 10.8 %collective-permute-start.15 = (bf16[192,256]{1,0:T(8,128)(2,1)S(1)}, bf16[192,256]{1,0:T(8,128)(2,1)S(1)}, u32[]{:S(2)}, u32[]{:S(2)}) collective-permute-start(bf16[192,256]{1,0:T(8,128)(2,1)S(1)} %get-tuple-element.52), channel_id=1, source_target_pairs={{0,2},{1,3},{2,0},{3,1},{4,6},{5,7},{6,4},{7,5},{8,10},{9,11},{10,... | collective-permute-start | bytes 294920 | tf_op jit(solution)/shard_map/ppermute | solution.py:464
  27.4 8.6 %collective-permute-start.16 = (bf16[192,256]{1,0:T(8,128)(2,1)S(1)}, bf16[192,256]{1,0:T(8,128)(2,1)S(1)}, u32[]{:S(2)}, u32[]{:S(2)}) collective-permute-start(bf16[192,256]{1,0:T(8,128)(2,1)S(1)} %get-tuple-element.53), channel_id=1, source_target_pairs={{0,3},{1,0},{2,1},{3,2},{4,7},{5,4},{6,5},{7,6},{8,11},{9,8},{10,9... | collective-permute-start | bytes 294920 | tf_op jit(solution)/shard_map/ppermute | solution.py:464
  28.8 10.8 %all-to-all-start.1 = ((bf16[32,2,640]{2,1,0:T(2,128)(2,1)}), bf16[32,2,640]{2,1,0:T(2,128)(2,1)S(1)}, u32[]{:S(2)}, u32[]{:S(2)}) async-start(bf16[32,2,640]{2,1,0:T(2,128)(2,1)} %get-tuple-element.42), calls=%async_computation.1 | async-start | bytes 163840 | tf_op jit(solution)/shard_map/all_to_all | solution.py:571
  31.9 7.8 %collective-permute-start.11 = (bf16[32,864]{1,0:T(8,128)(2,1)S(1)}, bf16[32,864]{1,0:T(8,128)(2,1)S(1)}, u32[]{:S(2)}, u32[]{:S(2)}) collective-permute-start(bf16[32,864]{1,0:T(8,128)(2,1)S(1)} %get-tuple-element.47), channel_id=1, source_target_pairs={{0,24},{4,28},{8,16},{12,20},{16,8},{20,12},{24,0},{28,4},{1,25},{... | collective-permute-start | bytes 165896 | tf_op jit(solution)/shard_map/ppermute | solution.py:473
  34.6 5.0 %collective-permute-start.12 = (bf16[32,864]{1,0:T(8,128)(2,1)S(1)}, bf16[32,864]{1,0:T(8,128)(2,1)S(1)}, u32[]{:S(2)}, u32[]{:S(2)}) collective-permute-start(bf16[32,864]{1,0:T(8,128)(2,1)S(1)} %get-tuple-element.48), channel_id=1, source_target_pairs={{0,16},{4,20},{8,24},{12,28},{16,0},{20,4},{24,8},{28,12},{1,17},{... | collective-permute-start | bytes 165896 | tf_op jit(solution)/shard_map/ppermute | solution.py:473
  35.2 4.5 %collective-permute-start.13 = (bf16[32,864]{1,0:T(8,128)(2,1)S(1)}, bf16[32,864]{1,0:T(8,128)(2,1)S(1)}, u32[]{:S(2)}, u32[]{:S(2)}) collective-permute-start(bf16[32,864]{1,0:T(8,128)(2,1)S(1)} %get-tuple-element.45.after_ref), channel_id=1, source_target_pairs={{0,8},{4,12},{8,0},{12,4},{16,24},{20,28},{24,16},{28,20},{1,9},{5... | collective-permute-start | bytes 165896 | tf_op jit(solution)/shard_map/ppermute | solution.py:473
